TPU v7x, 128 devices: a whole 4x4x4 slice. The times are simulated.
128 devices in a mesh: row: 8 (over x_lo, y), col: 16 (over z, x_hi, core).
Axes of the slice: x: 4 (x_hi: 2, x_lo: 2; x = x_hi * 2 + x_lo), y: 4, z: 4, core: 2. Of those that a mesh axis runs over, the one named last changes fastest.
Arguments:
- tracer_adj_next: float32 [8, 1024, 8192], P(None, 'row', 'col'), may hold values from -6 to 6
- tracer: float32 [8, 1024, 8192], P(None, 'row', 'col'), may hold values from -6 to 6
- u_east: float32 [1024, 8192], P('row', 'col'), may hold values from -6 to 6
- v_north: float32 [1024, 8192], P('row', 'col'), may hold values from -6 to 6
- surf_adj_next: float32 [1024, 8192], P('row', 'col'), may hold values from -6 to 6
- diag: float32 [1024, 8192], P('row', 'col'), may hold values from 0.1 to 1
- land: int32 [1024, 8192], P('row', 'col'), may hold values 0 or 1
- bottom: int32 [1024, 8192], P('row', 'col'), may hold values from 1 to 8
Outputs:
- tracer_adj: float32 [8, 1024, 8192], P(None, 'row', 'col')
- surf_adj: float32 [1024, 8192], P('row', 'col')
All inputs are finite; a program needn't handle non-finite values. No bound on the sum of `land` on one device may be relied on, other than what follows from the above.
Results may differ from a plain program's by a relative error of at most 0.0001.
Values sent between devices are 32-bit elements; how exact they have to be, the bound alone decides.
No kernel may reach another device: no remote copies, remote signals or barrier semaphores. Data moves between devices by JAX's collectives and lax.ppermute only.
A program may use at most 64 MiB of HBM per device.

v0:
```python
import jax
import jax.numpy as jnp
from jax import lax
from jax.sharding import PartitionSpec as P

ITERS = 3


def padded_2(block, sides, width):
    for axis, dim in sides:
        count = lax.axis_size(axis)
        forward = [(i, i + 1) for i in range(count - 1)]
        backward = [(target, source) for source, target in forward]
        low = lax.ppermute(
            lax.slice_in_dim(block, block.shape[dim] - width, None, axis=dim), axis, forward
        )
        high = lax.ppermute(lax.slice_in_dim(block, 0, width, axis=dim), axis, backward)
        block = jnp.concatenate([low, block, high], axis=dim)
    return block


def from_behind(shard, axis, by):
    size = lax.axis_size(axis)
    pairs = [(i, i + by) for i in range(size) if 0 <= i + by < size]
    return lax.ppermute(shard, axis, pairs)


def operate(field, cu, cv, diag):
    padded = padded_2(field, (("row", 0), ("col", 1)), 1)
    center = diag + cu[:, 1:] + cu[:, :-1] + cv[1:, :] + cv[:-1, :]
    return (
        center * field
        - cu[:, 1:] * padded[1:-1, 2:]
        - cu[:, :-1] * padded[1:-1, :-2]
        - cv[1:, :] * padded[2:, 1:-1]
        - cv[:-1, :] * padded[:-2, 1:-1]
    )


def squares(residual):
    return lax.psum(jnp.sum(residual * residual), ("row", "col"))


def wet_of(code, levels):
    level_frac = (lax.broadcasted_iota(jnp.float32, (levels, 1, 1), 0) + 0.5) / levels
    return jnp.where(level_frac < code[None], 1.0, 0.0).astype(jnp.float32)


def shards(tracer_adj_next, tracer, u_east, v_north, surf_adj_next, diag, land, bottom):
    levels = tracer.shape[0]
    code = jnp.where(land == 1, bottom.astype(jnp.float32), 0.0) / levels
    east_g, east_c, east_code = from_behind(
        (tracer_adj_next[:, :, 0], tracer[:, :, 0], code[:, 0]), "col", -1
    )
    north_g, north_c, north_code = from_behind(
        (tracer_adj_next[:, 0, :], tracer[:, 0, :], code[0, :]), "row", -1
    )
    g_east = jnp.concatenate([tracer_adj_next, east_g[:, :, None]], axis=2)
    c_east = jnp.concatenate([tracer, east_c[:, :, None]], axis=2)
    g_north = jnp.concatenate([tracer_adj_next, north_g[:, None, :]], axis=1)
    c_north = jnp.concatenate([tracer, north_c[:, None, :]], axis=1)
    code_east = jnp.concatenate([code, east_code[:, None]], axis=1)
    code_north = jnp.concatenate([code, north_code[None, :]], axis=0)
    wet_east = wet_of(code_east, levels)
    wet_north = wet_of(code_north, levels)
    face_u = wet_east[:, :, :-1] * wet_east[:, :, 1:]
    face_v = wet_north[:, :-1, :] * wet_north[:, 1:, :]
    cu_own = jnp.minimum(code_east[:, :-1], code_east[:, 1:])
    cv_own = jnp.minimum(code_north[:-1, :], code_north[1:, :])
    flux_u = 0.25 * (g_east[:, :, 1:] - g_east[:, :, :-1])
    flux_v = 0.25 * (g_north[:, 1:, :] - g_north[:, :-1, :])
    push_u = face_u * u_east[None] * flux_u * 0.5
    push_v = face_v * v_north[None] * flux_v * 0.5
    ubar = jnp.sum(face_u * flux_u * (c_east[:, :, :-1] + c_east[:, :, 1:]) * 0.5, axis=0)
    vbar = jnp.sum(face_v * flux_v * (c_north[:, :-1, :] + c_north[:, 1:, :]) * 0.5, axis=0)
    push_w, ubar_w, cu_w = from_behind((push_u[:, :, -1], ubar[:, -1], cu_own[:, -1]), "col", 1)
    push_s, vbar_s, cv_s = from_behind((push_v[:, -1, :], vbar[-1, :], cv_own[-1, :]), "row", 1)
    cu = jnp.concatenate([cu_w[:, None], cu_own], axis=1)
    cv = jnp.concatenate([cv_s[None, :], cv_own], axis=0)
    push_u_prev = jnp.concatenate([push_w[:, :, None], push_u[:, :, :-1]], axis=2)
    push_v_prev = jnp.concatenate([push_s[:, None, :], push_v[:, :-1, :]], axis=1)
    tracer_adj = tracer_adj_next + push_u + push_u_prev + push_v + push_v_prev
    ubar_prev = jnp.concatenate([ubar_w[:, None], ubar[:, :-1]], axis=1)
    vbar_prev = jnp.concatenate([vbar_s[None, :], vbar[:-1, :]], axis=0)
    rhs = surf_adj_next + 0.5 * (ubar - ubar_prev + (vbar - vbar_prev))
    solution = jnp.zeros_like(rhs)
    residual = rhs
    direction = rhs
    rr_now = squares(residual)
    for step in range(ITERS):
        image = operate(direction, cu, cv, diag)
        alpha = rr_now / lax.psum(jnp.sum(direction * image), ("row", "col"))
        solution = solution + alpha * direction
        residual = residual - alpha * image
        rr_next = squares(residual)
        direction = residual + rr_next / rr_now * direction
        rr_now = rr_next
    return (tracer_adj, solution)


def solution(mesh):
    placed = (
        P(None, "row", "col"),
        P(None, "row", "col"),
        P("row", "col"),
        P("row", "col"),
        P("row", "col"),
        P("row", "col"),
        P("row", "col"),
        P("row", "col"),
    )
    return jax.shard_map(
        shards,
        mesh=mesh,
        in_specs=placed,
        out_specs=(P(None, "row", "col"), P("row", "col")),
        check_vma=False,
    )
```

profile of v0, /device:TPU:1, one launch (start us, length us, event | category | flops | bytes accessed | tf_op | source)
XLA Modules:
  0.0 497.1 jit_solution(10889022448298883851)
XLA Ops:
  2.8 3.3 collective-permute-start
  11.9 2.9 copy.111
  30.6 12.6 %fusion.3 = (f32[128,512]{0,1:T(8,128)S(1)}, f32[128,512]{0,1:T(8,128)S(1)}, f32[8,128,512]{1,0,2:T(8,128)}) fusion(f32[8,128,512]{1,0,2:T(8,128)} %copy.111, f32[8,1,512]{1,0,2:T(8,128)} %copy.114, f32[8,129,512]{1,0,2:T(8,128)} %compare_select_fusion, f32[8,128,512]{1,0,2:T(8,128)} %copy-done, f32[8,1,512]{1,0,2:T(8,128)} %copy.105, ...), kind=kLoop, calls=%fused_computation.6 | loop fusion | flops 11927552 | bytes 15507456 | tf_op jit(solution)/shard_map/reduce_sum | solution.py:75
  43.5 5.2 %collective-permute-start.9 = (f32[512]{0:T(512)S(1)}, f32[512]{0:T(512)S(1)}, u32[]{:S(2)}, u32[]{:S(2)}) collective-permute-start(f32[512]{0:T(512)S(1)} %slice_reduce_fusion.1), channel_id=1, source_target_pairs={{0,16},{16,32},{32,48},{48,64},{64,80},{80,96},{96,112},{1,17},{17... | collective-permute-start | bytes 6152 | tf_op jit(solution)/shard_map/ppermute | solution.py:25
  48.7 5.4 %collective-permute-start.7 = (f32[128]{0:T(128)S(1)}, f32[128]{0:T(128)S(1)}, u32[]{:S(2)}, u32[]{:S(2)}) collective-permute-start(f32[128]{0:T(128)S(1)} %slice_bitcast_fusion.4), channel_id=1, source_target_pairs={{0,1},{1,2},{2,3},{3,4},{4,5},{5,6},{6,7},{7,8},{8,9},{9,10},{10,1... | collective-permute-start | bytes 1544 | tf_op jit(solution)/shard_map/ppermute | solution.py:25
  54.4 3.6 collective-permute-start.11
  60.2 4.0 collective-permute-start.12
  68.1 4.9 collective-permute-done.13
  75.0 5.1 %collective-permute-start.15 = (f32[130,1]{0,1:T(1,128)S(1)}, f32[130,1]{0,1:T(1,128)S(1)}, u32[]{:S(2)}, u32[]{:S(2)}) collective-permute-start(f32[130,1]{0,1:T(1,128)S(1)} %get-tuple-element.27), channel_id=1, source_target_pairs={{0,1},{1,2},{2,3},{3,4},{4,5},{5,6},{6,7},{7,8},{8,9},{9,10},{10,1... | collective-permute-start | bytes 1568 | tf_op jit(solution)/shard_map/ppermute | solution.py:14
  81.5 3.3 multiply_reduce_fusion.3
  84.8 75.4 %all-reduce = (f32[]{:T(128)}, f32[]{:T(128)}) all-reduce(f32[]{:T(128)} %get-tuple-element.13, f32[]{:T(128)} %get-tuple-element.12), channel_id=1, replica_groups=mesh['row'=8,'col'=16] {'row','col'}, use_global_device_ids=true, to_apply=%region_3.4 | all-reduce | flops 2 | bytes 16 | tf_op jit(solution)/shard_map/psum | solution.py:41
  163.2 62.5 %psum.44 = f32[]{:T(128)} all-reduce(f32[]{:T(128)} %get-tuple-element.18), channel_id=1, replica_groups=mesh['row'=8,'col'=16] {'row','col'}, use_global_device_ids=true, to_apply=%region_7.8 | all-reduce | flops 1 | bytes 8 | tf_op jit(solution)/shard_map/psum | solution.py:41
  231.4 3.4 collective-permute-done.16
  234.8 3.8 collective-permute-done.17
  238.7 4.0 collective-permute-start.18
  242.7 3.4 collective-permute-start.19
  247.9 68.7 %psum.45 = f32[]{:T(128)} all-reduce(f32[]{:T(128)} %get-tuple-element.16), channel_id=1, replica_groups=mesh['row'=8,'col'=16] {'row','col'}, use_global_device_ids=true, to_apply=%region_9.10 | all-reduce | flops 1 | bytes 8 | tf_op jit(solution)/shard_map/psum | solution.py:92
  320.5 62.5 %psum.46 = f32[]{:T(128)} all-reduce(f32[]{:T(128)} %multiply_reduce_fusion), channel_id=1, replica_groups=mesh['row'=8,'col'=16] {'row','col'}, use_global_device_ids=true, to_apply=%region_11.12 | all-reduce | flops 1 | bytes 8 | tf_op jit(solution)/shard_map/psum | solution.py:41
  393.0 3.8 collective-permute-done.21
  397.0 4.0 collective-permute-start.22
  401.0 3.4 collective-permute-start.23
  416.2 66.8 %psum.47 = f32[]{:T(128)} all-reduce(f32[]{:T(128)} %fusion.21), channel_id=1, replica_groups=mesh['row'=8,'col'=16] {'row','col'}, use_global_device_ids=true, to_apply=%region_13.14 | all-reduce | flops 1 | bytes 8 | tf_op jit(solution)/shard_map/psum | solution.py:92
  488.2 6.0 %fusion.13 = f32[8,128,512]{1,0,2:T(8,128)} fusion(f32[8,128,512]{1,0,2:T(8,128)} %get-tuple-element.21, f32[8,128,511]{1,0,2:T(8,128)} %slice.235, f32[8,128,1]{1,0,2:T(8,128)S(1)} %bitcast.49, f32[8,127,512]{1,0,2:T(8,128)} %bitcast.34, f32[8,1,512]{1,0,2:T(8,128)} %copy.108, f32[8,128,512]{1,0,2:T(8,128)S(1)} %copy-done.2, f32[8,128,512]{1,0,2:T(8,128)} %copy-done.4), kind=kLoop, calls=%fused_computation.22 | loop fusion | flops 3145728 | bytes 12582912 | tf_op jit(solution)/shard_map/add | solution.py:82
  494.2 2.9 copy.120
  (134 shorter events, 67.8 us)
Async XLA Ops:
  2.8 19.4 %collective-permute-start = (f32[128]{0:T(128)S(1)}, f32[128]{0:T(128)S(1)}, u32[]{:S(2)}, u32[]{:S(2)}) collective-permute-start(f32[128]{0:T(128)S(1)} %slice_bitcast_fusion.5), channel_id=1, source_target_pairs={{1,0},{2,1},{3,2},{4,3},{5,4},{6,5},{7,6},{8,7},{9,8},{10,9},{11,1... | collective-permute-start | bytes 1544 | tf_op jit(solution)/shard_map/ppermute | solution.py:25
  6.3 17.5 %collective-permute-start.3 = (f32[512]{0:T(512)S(1)}, f32[512]{0:T(512)S(1)}, u32[]{:S(2)}, u32[]{:S(2)}) collective-permute-start(f32[512]{0:T(512)S(1)} %slice_reduce_fusion.2), channel_id=1, source_target_pairs={{16,0},{32,16},{48,32},{64,48},{80,64},{96,80},{112,96},{17,1},{33... | collective-permute-start | bytes 6152 | tf_op jit(solution)/shard_map/ppermute | solution.py:25
  9.8 20.8 %collective-permute-start.1 = (f32[8,128]{1,0:T(8,128)S(1)}, f32[8,128]{1,0:T(8,128)S(1)}, u32[]{:S(2)}, u32[]{:S(2)}) collective-permute-start(f32[8,128]{1,0:T(8,128)S(1)} %slice_bitcast_fusion.2), channel_id=1, source_target_pairs={{1,0},{2,1},{3,2},{4,3},{5,4},{6,5},{7,6},{8,7},{9,8},{10,9},{11,1... | collective-permute-start | bytes 12296 | tf_op jit(solution)/shard_map/ppermute | solution.py:25
  15.4 15.2 %collective-permute-start.6 = (f32[8,128]{1,0:T(8,128)S(1)}, f32[8,128]{1,0:T(8,128)S(1)}, u32[]{:S(2)}, u32[]{:S(2)}) collective-permute-start(f32[8,128]{1,0:T(8,128)S(1)} %slice_bitcast_fusion), channel_id=1, source_target_pairs={{1,0},{2,1},{3,2},{4,3},{5,4},{6,5},{7,6},{8,7},{9,8},{10,9},{11,1... | collective-permute-start | bytes 12296 | tf_op jit(solution)/shard_map/ppermute | solution.py:25
  18.3 8.3 %collective-permute-start.4 = (f32[8,512]{1,0:T(8,128)S(1)}, f32[8,512]{1,0:T(8,128)S(1)}, u32[]{:S(2)}, u32[]{:S(2)}) collective-permute-start(f32[8,512]{1,0:T(8,128)S(1)} %bitcast.43), channel_id=1, source_target_pairs={{16,0},{32,16},{48,32},{64,48},{80,64},{96,80},{112,96},{17,1},{33... | collective-permute-start | bytes 49160 | tf_op jit(solution)/shard_map/ppermute | solution.py:25
  22.2 6.4 %collective-permute-start.8 = (f32[8,512]{1,0:T(8,128)S(1)}, f32[8,512]{1,0:T(8,128)S(1)}, u32[]{:S(2)}, u32[]{:S(2)}) collective-permute-start(f32[8,512]{1,0:T(8,128)S(1)} %bitcast.44), channel_id=1, source_target_pairs={{16,0},{32,16},{48,32},{64,48},{80,64},{96,80},{112,96},{17,1},{33... | collective-permute-start | bytes 49160 | tf_op jit(solution)/shard_map/ppermute | solution.py:25
  43.5 14.6 %collective-permute-start.9 = (f32[512]{0:T(512)S(1)}, f32[512]{0:T(512)S(1)}, u32[]{:S(2)}, u32[]{:S(2)}) collective-permute-start(f32[512]{0:T(512)S(1)} %slice_reduce_fusion.1), channel_id=1, source_target_pairs={{0,16},{16,32},{32,48},{48,64},{64,80},{80,96},{96,112},{1,17},{17... | collective-permute-start | bytes 6152 | tf_op jit(solution)/shard_map/ppermute | solution.py:25
  48.7 10.2 %collective-permute-start.7 = (f32[128]{0:T(128)S(1)}, f32[128]{0:T(128)S(1)}, u32[]{:S(2)}, u32[]{:S(2)}) collective-permute-start(f32[128]{0:T(128)S(1)} %slice_bitcast_fusion.4), channel_id=1, source_target_pairs={{0,1},{1,2},{2,3},{3,4},{4,5},{5,6},{6,7},{7,8},{8,9},{9,10},{10,1... | collective-permute-start | bytes 1544 | tf_op jit(solution)/shard_map/ppermute | solution.py:25
  54.4 26.9 %collective-permute-start.11 = (f32[512]{0:T(512)S(1)}, f32[512]{0:T(512)S(1)}, u32[]{:S(2)}, u32[]{:S(2)}) collective-permute-start(f32[512]{0:T(512)S(1)} %slice_reduce_fusion), channel_id=1, source_target_pairs={{0,16},{16,32},{32,48},{48,64},{64,80},{80,96},{96,112},{1,17},{17... | collective-permute-start | bytes 6152 | tf_op jit(solution)/shard_map/ppermute | solution.py:25
  60.2 7.8 %collective-permute-start.12 = (f32[1,512]{0,1:T(8,128)S(1)}, f32[1,512]{0,1:T(8,128)S(1)}, u32[]{:S(2)}, u32[]{:S(2)}) collective-permute-start(f32[1,512]{0,1:T(8,128)S(1)} %get-tuple-element.35), channel_id=1, source_target_pairs={{0,16},{16,32},{32,48},{48,64},{64,80},{80,96},{96,112},{1,17},{17... | collective-permute-start | bytes 6152 | tf_op jit(solution)/shard_map/ppermute | solution.py:14
  64.3 8.8 %collective-permute-start.13 = (f32[1,512]{0,1:T(8,128)S(1)}, f32[1,512]{0,1:T(8,128)S(1)}, u32[]{:S(2)}, u32[]{:S(2)}) collective-permute-start(f32[1,512]{0,1:T(8,128)S(1)} %get-tuple-element.34), channel_id=1, source_target_pairs={{16,0},{32,16},{48,32},{64,48},{80,64},{96,80},{112,96},{17,1},{33... | collective-permute-start | bytes 6152 | tf_op jit(solution)/shard_map/ppermute | solution.py:17
  65.6 15.9 %collective-permute-start.10 = (f32[128]{0:T(128)S(1)}, f32[128]{0:T(128)S(1)}, u32[]{:S(2)}, u32[]{:S(2)}) collective-permute-start(f32[128]{0:T(128)S(1)} %slice_bitcast_fusion.3), channel_id=1, source_target_pairs={{0,1},{1,2},{2,3},{3,4},{4,5},{5,6},{6,7},{7,8},{8,9},{9,10},{10,1... | collective-permute-start | bytes 1544 | tf_op jit(solution)/shard_map/ppermute | solution.py:25
  73.1 8.4 %collective-permute-start.14 = (f32[130,1]{0,1:T(1,128)S(1)}, f32[130,1]{0,1:T(1,128)S(1)}, u32[]{:S(2)}, u32[]{:S(2)}) collective-permute-start(f32[130,1]{0,1:T(1,128)S(1)} %get-tuple-element.26), channel_id=1, source_target_pairs={{1,0},{2,1},{3,2},{4,3},{5,4},{6,5},{7,6},{8,7},{9,8},{10,9},{11,1... | collective-permute-start | bytes 1568 | tf_op jit(solution)/shard_map/ppermute | solution.py:17
  75.0 6.5 %collective-permute-start.15 = (f32[130,1]{0,1:T(1,128)S(1)}, f32[130,1]{0,1:T(1,128)S(1)}, u32[]{:S(2)}, u32[]{:S(2)}) collective-permute-start(f32[130,1]{0,1:T(1,128)S(1)} %get-tuple-element.27), channel_id=1, source_target_pairs={{0,1},{1,2},{2,3},{3,4},{4,5},{5,6},{6,7},{7,8},{8,9},{9,10},{10,1... | collective-permute-start | bytes 1568 | tf_op jit(solution)/shard_map/ppermute | solution.py:14
  227.3 7.5 %collective-permute-start.16 = (f32[1,512]{0,1:T(8,128)S(1)}, f32[1,512]{0,1:T(8,128)S(1)}, u32[]{:S(2)}, u32[]{:S(2)}) collective-permute-start(f32[1,512]{0,1:T(8,128)S(1)} %get-tuple-element.31), channel_id=1, source_target_pairs={{0,16},{16,32},{32,48},{48,64},{64,80},{80,96},{96,112},{1,17},{17... | collective-permute-start | bytes 6152 | tf_op jit(solution)/shard_map/ppermute | solution.py:14
  230.1 8.5 %collective-permute-start.17 = (f32[1,512]{0,1:T(8,128)S(1)}, f32[1,512]{0,1:T(8,128)S(1)}, u32[]{:S(2)}, u32[]{:S(2)}) collective-permute-start(f32[1,512]{0,1:T(8,128)S(1)} %get-tuple-element.30), channel_id=1, source_target_pairs={{16,0},{32,16},{48,32},{64,48},{80,64},{96,80},{112,96},{17,1},{33... | collective-permute-start | bytes 6152 | tf_op jit(solution)/shard_map/ppermute | solution.py:17
  238.7 7.4 %collective-permute-start.18 = (f32[130,1]{0,1:T(1,128)S(1)}, f32[130,1]{0,1:T(1,128)S(1)}, u32[]{:S(2)}, u32[]{:S(2)}) collective-permute-start(f32[130,1]{0,1:T(1,128)S(1)} %get-tuple-element.24), channel_id=1, source_target_pairs={{1,0},{2,1},{3,2},{4,3},{5,4},{6,5},{7,6},{8,7},{9,8},{10,9},{11,1... | collective-permute-start | bytes 1568 | tf_op jit(solution)/shard_map/ppermute | solution.py:17
  242.7 4.1 collective-permute-start.19
  385.7 7.4 %collective-permute-start.20 = (f32[1,512]{0,1:T(8,128)S(1)}, f32[1,512]{0,1:T(8,128)S(1)}, u32[]{:S(2)}, u32[]{:S(2)}) collective-permute-start(f32[1,512]{0,1:T(8,128)S(1)} %get-tuple-element.29), channel_id=1, source_target_pairs={{0,16},{16,32},{32,48},{48,64},{64,80},{80,96},{96,112},{1,17},{17... | collective-permute-start | bytes 6152 | tf_op jit(solution)/shard_map/ppermute | solution.py:14
  388.4 8.5 %collective-permute-start.21 = (f32[1,512]{0,1:T(8,128)S(1)}, f32[1,512]{0,1:T(8,128)S(1)}, u32[]{:S(2)}, u32[]{:S(2)}) collective-permute-start(f32[1,512]{0,1:T(8,128)S(1)} %get-tuple-element.28), channel_id=1, source_target_pairs={{16,0},{32,16},{48,32},{64,48},{80,64},{96,80},{112,96},{17,1},{33... | collective-permute-start | bytes 6152 | tf_op jit(solution)/shard_map/ppermute | solution.py:17
  397.0 15.7 %collective-permute-start.22 = (f32[130,1]{0,1:T(1,128)S(1)}, f32[130,1]{0,1:T(1,128)S(1)}, u32[]{:S(2)}, u32[]{:S(2)}) collective-permute-start(f32[130,1]{0,1:T(1,128)S(1)} %get-tuple-element.22), channel_id=1, source_target_pairs={{1,0},{2,1},{3,2},{4,3},{5,4},{6,5},{7,6},{8,7},{9,8},{10,9},{11,1... | collective-permute-start | bytes 1568 | tf_op jit(solution)/shard_map/ppermute | solution.py:17
  401.0 11.7 %collective-permute-start.23 = (f32[130,1]{0,1:T(1,128)S(1)}, f32[130,1]{0,1:T(1,128)S(1)}, u32[]{:S(2)}, u32[]{:S(2)}) collective-permute-start(f32[130,1]{0,1:T(1,128)S(1)} %get-tuple-element.23), channel_id=1, source_target_pairs={{0,1},{1,2},{2,3},{3,4},{4,5},{5,6},{6,7},{7,8},{8,9},{9,10},{10,1... | collective-permute-start | bytes 1568 | tf_op jit(solution)/shard_map/ppermute | solution.py:14
  406.0 82.2 %collective-permute-start.2 = (f32[8,128]{1,0:T(8,128)S(1)}, f32[8,128]{1,0:T(8,128)S(1)}, u32[]{:S(2)}, u32[]{:S(2)}) collective-permute-start(f32[8,128]{1,0:T(8,128)S(1)} %slice_bitcast_fusion.1), channel_id=1, source_target_pairs={{0,1},{1,2},{2,3},{3,4},{4,5},{5,6},{6,7},{7,8},{8,9},{9,10},{10,1... | collective-permute-start | bytes 12296 | tf_op jit(solution)/shard_map/ppermute | solution.py:25
  413.8 72.4 %collective-permute-start.5 = (f32[8,512]{1,0:T(8,128)S(1)}, f32[8,512]{1,0:T(8,128)S(1)}, u32[]{:S(2)}, u32[]{:S(2)}) collective-permute-start(f32[8,512]{1,0:T(8,128)S(1)} %bitcast.37), channel_id=1, source_target_pairs={{0,16},{16,32},{32,48},{48,64},{64,80},{80,96},{96,112},{1,17},{17... | collective-permute-start | bytes 49160 | tf_op jit(solution)/shard_map/ppermute | solution.py:25
  (24 other events, 657.5 us)
where the time goes:
time: 499 us; the launch traced here: 497 us
  blocking collectives  336 us (67%)
  starting transfers between devices  68.1 us (14%)
  other arithmetic  34.3 us (7%)
  local copies, waits for them, and re-layouts  31.9 us (6%)
  waiting for transfers between devices  18.7 us (4%)
  between operations  8.01 us (2%)
    psum x3, blocking collectives, squares(): return lax.psum(jnp.sum(residual * residual), ('row', 'col'))  200 us
    psum x2, blocking collectives, shards(): alpha = rr_now / lax.psum(jnp.sum(direction * image), ('row', 'col'))  136 us
    ppermute x12, starting transfers between devices, from_behind(): return lax.ppermute(shard, axis, pairs)  32.7 us
    ppermute x6, starting transfers between devices, padded_2(): lax.ppermute(lax.slice_in_dim(block, block.shape[dim] - width, None, axis...  21.6 us
    unnamed x60, local copies, waits for them, and re-layouts  15.5 us
    ppermute x6, starting transfers between devices, padded_2(): lax.ppermute(lax.slice_in_dim(block, 0, width, axis=dim), axis, backward)  13.8 us
    ppermute x6, waiting for transfers between devices, padded_2(): lax.ppermute(lax.slice_in_dim(block, 0, width, axis=dim), axis, backward)  12.6 us
    reduce_sum x1, other arithmetic, shards(): jnp.sum(face_v * flux_v * (c_north[:, :-1, :] + c_north[:, 1:, :]) * 0.5,...  12.6 us
  transfers between devices with their start and end apart: 24, of which 6 were waited for; matrix products, arithmetic and copies ran while one was open for 6% of the time, Pallas kernels for 0%

commit v1 on v0

v1 whole, which is shorter than its diff:
```python
import jax
import jax.numpy as jnp
from jax import lax
from jax.experimental import pallas as pl
from jax.experimental.pallas import tpu as pltpu
from jax.sharding import PartitionSpec as P

LEV = 8
DEEP = 4
SHIFT = 1.0
F32 = jnp.float32
VMEM = pl.BlockSpec(memory_space=pltpu.VMEM)
PARAMS = pltpu.CompilerParams(vmem_limit_bytes=48 * 1024 * 1024)


def code_of(land, bottom):
    return jnp.where(land == 1, bottom, 0).astype(F32)


def swap_pairs(axis, first):
    count = lax.axis_size(axis)
    pairs = []
    for low in range(first, count - 1, 2):
        pairs += [(low, low + 1), (low + 1, low)]
    return pairs


def swap(buffers, axis):
    return [lax.ppermute(b, axis, swap_pairs(axis, first)) for first, b in enumerate(buffers)]


def is_even(axis):
    return lax.rem(lax.axis_index(axis), 2) == 0


def iota(shape, dim):
    return lax.broadcasted_iota(jnp.int32, shape, dim)


def planes_of(g, c, land, bottom, surf, diag, speed):
    return (
        [g[k] for k in range(LEV)]
        + [c[k] for k in range(LEV)]
        + [code_of(land[...], bottom[...]), surf[...], diag[...], speed[...]]
    )


def pack_rows(g0, g1, c0, c1, l0, l1, b0, b1, s0, s1, d0, d1, v0, v1, a_ref, b_ref):
    first = planes_of(g0, c0, l0, b0, s0, d0, v0)
    last = planes_of(g1, c1, l1, b1, s1, d1, v1)
    upper = iota(first[0].shape, 0) < 4
    even = is_even("row")
    for t in range(len(first) // 2):
        high = jnp.where(upper, pltpu.roll(last[2 * t], 4, 0), last[2 * t + 1])
        low = jnp.where(upper, first[2 * t], pltpu.roll(first[2 * t + 1], 4, 0))
        a_ref[8 * t : 8 * t + 8, :] = jnp.where(even, high, low)
        b_ref[8 * t : 8 * t + 8, :] = jnp.where(even, low, high)


def row_halo(near, far, lanes):
    even = is_even("row")

    def plane(p):
        t = p // 2
        one, two = near[8 * t : 8 * t + 8, lanes], far[8 * t : 8 * t + 8, lanes]
        north, south = jnp.where(even, one, two), jnp.where(even, two, one)
        upper = iota(north.shape, 0) < 4
        if p % 2 == 0:
            return jnp.where(upper, north, pltpu.roll(south, 4, 0))
        return jnp.where(upper, pltpu.roll(north, 4, 0), south)

    return plane


def lane_pack(planes, of_last):
    lane = iota(planes[0].shape, 1)
    out = jnp.zeros_like(planes[0])
    for p, x in enumerate(planes):
        turn = (DEEP * p + (DEEP if of_last else 0)) % 128
        moved = pltpu.roll(x, turn, 1) if turn else x
        out = jnp.where(lane // DEEP == p, moved, out)
    return out


def pack_cols(g0, g1, c0, c1, l0, l1, b0, b1, s0, s1, d0, d1, u0, u1, a_ref, b_ref):
    low = lane_pack(planes_of(g0, c0, l0, b0, s0, d0, u0), False)
    high = lane_pack(planes_of(g1, c1, l1, b1, s1, d1, u1), True)
    even = is_even("col")
    a_ref[...] = jnp.where(even, high, low)
    b_ref[...] = jnp.where(even, low, high)


def join_cols(a_in, b_in, near, far, a_ref, b_ref):
    rows, width = a_in.shape[0], near.shape[1]
    first = row_halo(near, far, slice(0, 128))
    last = row_halo(near, far, slice(width - 128, width))
    low = lane_pack([first(p) for p in range(2 * LEV + 3)], False)
    high = lane_pack([last(p) for p in range(2 * LEV + 3)], True)
    even = is_even("col")
    a_ref[:rows, :] = a_in[...]
    b_ref[:rows, :] = b_in[...]
    a_ref[rows:, :] = jnp.where(even, high, low)
    b_ref[rows:, :] = jnp.where(even, low, high)


def col_halo(near, far):
    even = is_even("col")
    one, two = near[...], far[...]
    east, west = jnp.where(even, one, two), jnp.where(even, two, one)
    left = iota(east.shape, 1) < 64

    def plane(p):
        e = pltpu.roll(east, (128 - DEEP * p) % 128, 1) if p else east
        w = pltpu.roll(west, 128 - DEEP - DEEP * p, 1)
        return jnp.where(left, e, w)

    return plane


def next_col(a):
    return pltpu.roll(a, a.shape[1] - 1, 1)


def prev_col(a):
    return pltpu.roll(a, 1, 1)


def next_row(a):
    return pltpu.roll(a, a.shape[0] - 1, 0)


def prev_row(a):
    return pltpu.roll(a, 1, 0)


def extended(own, rows, cols):
    return jnp.concatenate([jnp.concatenate([own, rows], axis=0), cols], axis=1)


def faces(code):
    return jnp.minimum(code, next_col(code)), jnp.minimum(code, next_row(code))


def krylov(g, c, land, bottom, surf, diag, rn, rf, cn, cf, r_ref, p1_ref, p2_ref, mom_ref):
    rows, cols = surf.shape
    rh, ch = row_halo(rn, rf, slice(0, cols)), col_halo(cn, cf)

    def wide(own, p):
        return extended(own, rh(p), ch(p))

    cu, cv = faces(wide(code_of(land[...], bottom[...]), 2 * LEV))
    ub = jnp.zeros_like(cu)
    vb = jnp.zeros_like(cv)
    for k in range(LEV):
        gk, ck = wide(g[k], k), wide(c[k], LEV + k)
        ub = ub + jnp.where(cu > k + 0.5, next_col(gk) - gk, 0.0) * (next_col(ck) + ck)
        vb = vb + jnp.where(cv > k + 0.5, next_row(gk) - gk, 0.0) * (next_row(ck) + ck)
    r = wide(surf[...], 2 * LEV + 1) + 0.0625 * ((ub - prev_col(ub)) + (vb - prev_row(vb)))
    cu, cv = cu * 0.125, cv * 0.125
    dg = wide(diag[...], 2 * LEV + 2)

    def shifted(v):
        fu, fv = cu * (v - next_col(v)), cv * (v - next_row(v))
        return (dg - SHIFT) * v + ((fu - prev_col(fu)) + (fv - prev_row(fv)))

    p1 = shifted(r)
    p2 = shifted(p1)
    eu, ev = p2 - next_col(p2), p2 - next_row(p2)
    energy = dg * p2 * p2 + (cu * eu * eu + cv * ev * ev)
    r, p1, p2, energy = [a[:rows, :cols] for a in (r, p1, p2, energy)]
    r_ref[...] = r
    p1_ref[...] = p1
    p2_ref[...] = p2
    lane = iota((8, 128), 1)
    packed = jnp.zeros((8, 128), F32)
    for m, prod in enumerate((r * r, r * p1, p1 * p1, p1 * p2, p2 * p2, energy)):
        tiles = [
            prod[8 * i : 8 * i + 8, 128 * j : 128 * j + 128]
            for i in range(rows // 8)
            for j in range(cols // 128)
        ]
        while len(tiles) > 1:
            tiles = [sum(tiles[i : i + 2][1:], tiles[i]) for i in range(0, len(tiles), 2)]
        part = tiles[0]
        for by in (4, 2, 1):
            part = part + pltpu.roll(part, by, 0)
        for by in (64, 32, 16):
            part = part + pltpu.roll(part, by, 1)
        packed = jnp.where(lane // 16 == m, part, packed)
    for i in range(mom_ref.shape[0] // 8):
        mom_ref[8 * i : 8 * i + 8, :] = packed


def tracer_kernel(g, land, bottom, u, v, rn, rf, cn, cf, out_ref):
    rows, cols = u.shape
    rh, ch = row_halo(rn, rf, slice(0, cols)), col_halo(cn, cf)

    def wide(own, p):
        return extended(own, rh(p), ch(p))

    cu, cv = faces(wide(code_of(land[...], bottom[...]), 2 * LEV))
    uw = 0.125 * wide(u[...], 2 * LEV + 3)
    vw = 0.125 * wide(v[...], 2 * LEV + 3)
    for k in range(LEV):
        gk = wide(g[k], k)
        pu = jnp.where(cu > k + 0.5, next_col(gk) - gk, 0.0) * uw
        pv = jnp.where(cv > k + 0.5, next_row(gk) - gk, 0.0) * vw
        total = gk + pu + prev_col(pu) + pv + prev_row(pv)
        out_ref[k] = total[:rows, :cols]


def two_sum(a, b):
    s = a + b
    t = s - a
    return s, (a - (s - t)) + (b - t)


def quick(a, b):
    s = a + b
    return s, b - (s - a)


def split(a):
    t = a * 4097.0
    high = t - (t - a)
    return high, a - high


def add(x, y):
    s, e = two_sum(x[0], y[0])
    return quick(s, e + (x[1] + y[1]))


def neg(x):
    return -x[0], -x[1]


def mul(x, y):
    p = x[0] * y[0]
    (ah, al), (bh, bl) = split(x[0]), split(y[0])
    e = ((ah * bh - p) + ah * bl + al * bh) + al * bl
    return quick(p, e + (x[0] * y[1] + x[1] * y[0]))


def div(x, y):
    q = x[0] / y[0]
    rest = add(x, neg(mul((q, jnp.zeros_like(q)), y)))
    return quick(q, rest[0] / y[0])


def combine(mom, r, p1, p2, x_ref):
    zero = jnp.zeros((8, 128), F32)
    tiles = [(mom[8 * i : 8 * i + 8, :], zero) for i in range(mom.shape[0] // 8)]
    while len(tiles) > 1:
        tiles = [add(tiles[i], tiles[i + 1]) for i in range(0, len(tiles), 2)]
    total = tiles[0]
    for by in (4, 2, 1):
        total = add(total, tuple(pltpu.roll(a, by, 0) for a in total))
    lane = iota((8, 128), 1)
    sums = []
    for m in range(6):
        mine = tuple(jnp.where(lane // 16 == m, a, 0.0) for a in total)
        for by in (64, 32, 16, 8, 4, 2, 1):
            mine = add(mine, tuple(pltpu.roll(a, by, 1) for a in mine))
        sums.append(mine)
    m00, m01, m11, m12, m22, e22 = sums
    a00, a01, a02 = add(m01, m00), add(m11, m01), add(m12, m11)
    a11, a12, a22 = a02, add(m22, m12), e22
    l10 = div(a01, a00)
    l20 = div(a02, a00)
    w11 = add(a11, neg(mul(l10, a01)))
    w12 = add(a12, neg(mul(l10, a02)))
    ok1 = w11[0] > 1e-9 * a11[0]
    l21 = tuple(jnp.where(ok1, a, 0.0) for a in div(w12, w11))
    w22 = add(add(a22, neg(mul(l20, a02))), neg(mul(l21, w12)))
    ok2 = w22[0] > 1e-9 * a22[0]
    b0 = m00
    b1 = add(m01, neg(mul(l10, b0)))
    z1 = tuple(jnp.where(ok1, a, 0.0) for a in div(b1, w11))
    b2 = add(add(m11, neg(mul(l20, b0))), neg(mul(l21, b1)))
    z2 = tuple(jnp.where(ok2, a, 0.0) for a in div(b2, w22))
    y2 = z2
    y1 = add(z1, neg(mul(l21, y2)))
    y0 = add(div(b0, a00), neg(add(mul(l10, y1), mul(l20, y2))))
    rows, cols = r.shape
    shape = (rows // 8, 8, cols // 128, 128)
    for i in range(rows // 8):
        for j in range(cols // 128):
            at = (slice(8 * i, 8 * i + 8), slice(128 * j, 128 * j + 128))
            x_ref[at] = y0[0] * r[at] + (y1[0] * p1[at] + y2[0] * p2[at])


def shards(tracer_adj_next, tracer, u_east, v_north, surf_adj_next, diag, land, bottom):
    levels, rows, cols = tracer.shape
    planes = 2 * levels + 4
    size = lax.axis_size("row") * lax.axis_size("col")
    twice = lambda *arrays: [a for a in arrays for _ in range(2)]

    def ends(shape3, shape2, dim):
        count = (rows // 8, cols // 128)[dim]
        specs = []
        for s in (shape3, shape3, shape2, shape2, shape2, shape2, shape2):
            for end in (0, count - 1):
                place = tuple(end if d == len(s) - 2 + dim else 0 for d in range(len(s)))
                specs.append(pl.BlockSpec(s, lambda i, place=place: place))
        return specs

    g, c = tracer_adj_next, tracer
    row_bufs = pl.pallas_call(
        pack_rows,
        grid=(1,),
        in_specs=ends((levels, 8, cols), (8, cols), 0),
        out_specs=[pl.BlockSpec((4 * planes, cols), lambda i: (0, 0))] * 2,
        out_shape=[jax.ShapeDtypeStruct((4 * planes, cols), F32)] * 2,
        compiler_params=PARAMS,
        name="pack_rows",
    )(*twice(g, c, land, bottom, surf_adj_next, diag, v_north))
    row_got = swap(row_bufs, "row")
    col_part = pl.pallas_call(
        pack_cols,
        grid=(1,),
        in_specs=ends((levels, rows, 128), (rows, 128), 1),
        out_specs=[pl.BlockSpec((rows, 128), lambda i: (0, 0))] * 2,
        out_shape=[jax.ShapeDtypeStruct((rows, 128), F32)] * 2,
        compiler_params=PARAMS,
        name="pack_cols",
    )(*twice(g, c, land, bottom, surf_adj_next, diag, u_east))
    col_bufs = pl.pallas_call(
        join_cols,
        in_specs=[VMEM] * 4,
        out_specs=[VMEM] * 2,
        out_shape=[jax.ShapeDtypeStruct((rows + 8, 128), F32)] * 2,
        compiler_params=PARAMS,
        name="join_cols",
    )(*col_part, *row_got)
    col_got = swap(col_bufs, "col")
    r, p1, p2, mom = pl.pallas_call(
        krylov,
        in_specs=[VMEM] * 10,
        out_specs=[VMEM] * 4,
        out_shape=[jax.ShapeDtypeStruct((rows, cols), F32)] * 3
        + [jax.ShapeDtypeStruct((size, 128), F32)],
        compiler_params=PARAMS,
        name="krylov",
    )(g, c, land, bottom, surf_adj_next, diag, *row_got, *col_got)
    mom = lax.all_to_all(mom, ("row", "col"), 0, 0, tiled=True)
    tracer_adj = pl.pallas_call(
        tracer_kernel,
        in_specs=[VMEM] * 9,
        out_specs=VMEM,
        out_shape=jax.ShapeDtypeStruct(g.shape, F32),
        compiler_params=PARAMS,
        cost_estimate=pl.CostEstimate(flops=20 * g.size, bytes_accessed=12 * g.size, transcendentals=0),
        name="tracer",
    )(g, land, bottom, u_east, v_north, *row_got, *col_got)
    surf_adj = pl.pallas_call(
        combine,
        in_specs=[VMEM] * 4,
        out_specs=VMEM,
        out_shape=jax.ShapeDtypeStruct((rows, cols), F32),
        compiler_params=PARAMS,
        name="combine",
    )(mom, r, p1, p2)
    return tracer_adj, surf_adj


def solution(mesh):
    three, two = P(None, "row", "col"), P("row", "col")
    return jax.shard_map(
        shards,
        mesh=mesh,
        in_specs=(three, three, two, two, two, two, two, two),
        out_specs=(three, two),
        check_vma=False,
    )
```

time: 499 us -> 63.9 us (0.13)
  blocking collectives: 336 us -> 0 us
  starting transfers between devices: 68.1 us -> 25.8 us
  other arithmetic: 34.3 us -> 0 us
  local copies, waits for them, and re-layouts: 31.9 us -> 14.4 us
  Pallas kernels: 0 us -> 12.8 us
  waiting for transfers between devices: 18.7 us -> 9.51 us
  between operations: 8.01 us -> 0.75 us
    psum x5 -> x0, blocking collectives: 336 us -> none  [the longest x3 200 us: squares(): return lax.psum(jnp.sum(residual * residual), ('row', 'col'))]
    ppermute x24 -> x4, starting transfers between devices: 68.1 us -> 9.57 us  [swap(): lax.ppermute(b, axis, swap_pairs(axis, first))]
    reduce_sum x6 -> x0, other arithmetic: 20.4 us -> none  [the longest x1 12.6 us: shards(): jnp.sum(face_v * flux_v * (c_north[:, :-1, :] + c_north[:, 1:, :]) * 0.5,...]
    all_to_all x0 -> x1, starting transfers between devices: none -> 16.3 us  [shards(): mom = lax.all_to_all(mom, ('row', 'col'), 0, 0, tiled=True)]
    ppermute x24 -> x4, waiting for transfers between devices: 18.7 us -> 4.34 us  [swap(): lax.ppermute(b, axis, swap_pairs(axis, first))]
    pallas_call x0 -> x6, Pallas kernels: none -> 12.8 us  [the longest x1 5.86 us: shards(): pl.pallas_call(krylov, in_specs=[VMEM] * 10, out_specs=[VMEM] * 4, out_sh...]
    add x5 -> x0, other arithmetic: 9.43 us -> none  [the longest x1 5.99 us: shards(): tracer_adj = tracer_adj_next + push_u + push_u_prev + push_v + push_v_prev]
    slice x11 -> x0, local copies, waits for them, and re-layouts: 8.56 us -> none  [the longest x2 4.23 us: shards(): push_v[:, -1, :]]
  transfers between devices with their start and end apart: 24 -> 5, of which waited for: 6 -> 3; matrix products, arithmetic and copies ran while one was open for 6% -> 0% of each run, Pallas kernels for 0% -> 7%
where the time goes in v1:
time: 63.9 us; the launch traced here: 63.3 us
  starting transfers between devices  25.8 us (40%)
  local copies, waits for them, and re-layouts  14.4 us (23%)
  Pallas kernels  12.8 us (20%)
  waiting for transfers between devices  9.51 us (15%)
  between operations  0.75 us (1%)
    all_to_all x1, starting transfers between devices, shards(): mom = lax.all_to_all(mom, ('row', 'col'), 0, 0, tiled=True)  16.3 us
    unnamed x42, local copies, waits for them, and re-layouts  14.4 us
    ppermute x4, starting transfers between devices, swap(): lax.ppermute(b, axis, swap_pairs(axis, first))  9.57 us
    pallas_call x1, Pallas kernels, shards(): pl.pallas_call(krylov, in_specs=[VMEM] * 10, out_specs=[VMEM] * 4, out_sh...  5.86 us
    all_to_all x1, waiting for transfers between devices, shards(): mom = lax.all_to_all(mom, ('row', 'col'), 0, 0, tiled=True)  5.17 us
    ppermute x4, waiting for transfers between devices, swap(): lax.ppermute(b, axis, swap_pairs(axis, first))  4.34 us
    pallas_call x1, Pallas kernels, shards(): pl.pallas_call(tracer_kernel, in_specs=[VMEM] * 9, out_specs=VMEM, out_sh...  3.65 us
    pallas_call x1, Pallas kernels, shards(): pl.pallas_call(combine, in_specs=[VMEM] * 4, out_specs=VMEM, out_shape=ja...  2.4 us
  transfers between devices with their start and end apart: 5, of which 3 were waited for; matrix products, arithmetic and copies ran while one was open for 0% of the time, Pallas kernels for 7%

profile of v1, /device:TPU:1, one launch (start us, length us, event | category | flops | bytes accessed | tf_op | source)
XLA Modules:
  0.0 63.3 jit_solution(5025421480246016198)
XLA Ops:
  0.6 1.6 %copy-done = f32[8,128,512]{2,1,0:T(8,128)S(1)} copy-done((f32[8,128,512]{2,1,0:T(8,128)S(1)}, f32[8,128,512]{2,1,0:T(8,128)}, u32[]{:S(2)}) %copy-start) | copy-done | bytes 2097176
  2.2 1.6 %copy-done.2 = f32[8,128,512]{2,1,0:T(8,128)S(1)} copy-done((f32[8,128,512]{2,1,0:T(8,128)S(1)}, f32[8,128,512]{2,1,0:T(8,128)}, u32[]{:S(2)}) %copy-start.2) | copy-done | bytes 2097176
  3.8 0.9 %copy-done.3 = s32[128,512]{1,0:T(8,128)S(1)} copy-done((s32[128,512]{1,0:T(8,128)S(1)}, s32[128,512]{1,0:T(8,128)}, u32[]{:S(2)}) %copy-start.3) | copy-done | bytes 262168
  4.8 0.9 %copy-done.5 = s32[128,512]{1,0:T(8,128)S(1)} copy-done((s32[128,512]{1,0:T(8,128)S(1)}, s32[128,512]{1,0:T(8,128)}, u32[]{:S(2)}) %copy-start.5) | copy-done | bytes 262168
  5.7 0.9 %copy-done.7 = f32[128,512]{1,0:T(8,128)S(1)} copy-done((f32[128,512]{1,0:T(8,128)S(1)}, f32[128,512]{1,0:T(8,128)}, u32[]{:S(2)}) %copy-start.7) | copy-done | bytes 262168
  6.7 0.9 %copy-done.8 = f32[128,512]{1,0:T(8,128)S(1)} copy-done((f32[128,512]{1,0:T(8,128)S(1)}, f32[128,512]{1,0:T(8,128)}, u32[]{:S(2)}) %copy-start.8) | copy-done | bytes 262168
  7.6 0.9 %copy-done.10 = f32[128,512]{1,0:T(8,128)S(1)} copy-done((f32[128,512]{1,0:T(8,128)S(1)}, f32[128,512]{1,0:T(8,128)}, u32[]{:S(2)}) %copy-start.10) | copy-done | bytes 262168
  8.6 2.2 %collective-permute-start = (f32[80,512]{1,0:T(8,128)S(1)}, f32[80,512]{1,0:T(8,128)S(1)}, u32[]{:S(2)}, u32[]{:S(2)}) collective-permute-start(f32[80,512]{1,0:T(8,128)S(1)} %get-tuple-element.12), channel_id=1, source_target_pairs={{0,16},{16,0},{32,48},{48,32},{64,80},{80,64},{96,112},{112,96},{1... | collective-permute-start | bytes 491528 | tf_op jit(solution)/shard_map/ppermute | solution.py:29
  10.8 0.8 %collective-permute-start.1 = (f32[80,512]{1,0:T(8,128)S(1)}, f32[80,512]{1,0:T(8,128)S(1)}, u32[]{:S(2)}, u32[]{:S(2)}) collective-permute-start(f32[80,512]{1,0:T(8,128)S(1)} %get-tuple-element.13), channel_id=1, source_target_pairs={{16,32},{32,16},{48,64},{64,48},{80,96},{96,80},{17,33},{33,17},{4... | collective-permute-start | bytes 491528 | tf_op jit(solution)/shard_map/ppermute | solution.py:29
  11.6 0.7 %pack_cols.1 = (f32[128,128]{1,0:T(8,128)S(1)}, f32[128,128]{1,0:T(8,128)S(1)}) custom-call(f32[8,128,512]{2,1,0:T(8,128)S(1)} %copy-done, f32[8,128,512]{2,1,0:T(8,128)S(1)} %copy-done, f32[8,128,512]{2,1,0:T(8,128)S(1)} %copy-done.2, f32[8,128,512]{2,1,0:T(8,128)S(1)} %copy-done.2, s32[128,512]{1,0:T(8,128)S(1)} %copy-done.3, s32[128,512]{1,0:T(8,128)S(1)} %copy-done.3, ...), custom_call_target="tpu_custom_call" | custom-call | tf_op jit(solution)/shard_map/pack_cols/pallas_call | solution.py:319
  12.4 2.0 %collective-permute-done.near.rn = f32[80,512]{1,0:T(8,128)S(1)} collective-permute-done((f32[80,512]{1,0:T(8,128)S(1)}, f32[80,512]{1,0:T(8,128)S(1)}, u32[]{:S(2)}, u32[]{:S(2)}) %collective-permute-start) | collective-permute-done | bytes 163872 | tf_op jit(solution)/shard_map/ppermute | solution.py:29
  14.5 1.7 %collective-permute-start.2 = (f32[136,128]{1,0:T(8,128)S(1)}, f32[136,128]{1,0:T(8,128)S(1)}, u32[]{:S(2)}, u32[]{:S(2)}) collective-permute-start(f32[136,128]{1,0:T(8,128)S(1)} %get-tuple-element.16), channel_id=1, source_target_pairs={{0,1},{1,0},{2,3},{3,2},{4,5},{5,4},{6,7},{7,6},{8,9},{9,8},{10,11... | collective-permute-start | bytes 208904 | tf_op jit(solution)/shard_map/ppermute | solution.py:29
  16.2 4.9 %collective-permute-start.3 = (f32[136,128]{1,0:T(8,128)S(1)}, f32[136,128]{1,0:T(8,128)S(1)}, u32[]{:S(2)}, u32[]{:S(2)}) collective-permute-start(f32[136,128]{1,0:T(8,128)S(1)} %get-tuple-element.17), channel_id=1, source_target_pairs={{1,2},{2,1},{3,4},{4,3},{5,6},{6,5},{7,8},{8,7},{9,10},{10,9},{11,... | collective-permute-start | bytes 208904 | tf_op jit(solution)/shard_map/ppermute | solution.py:29
  21.1 2.4 %collective-permute-done.3.cf = f32[136,128]{1,0:T(8,128)S(1)} collective-permute-done((f32[136,128]{1,0:T(8,128)S(1)}, f32[136,128]{1,0:T(8,128)S(1)}, u32[]{:S(2)}, u32[]{:S(2)}) %collective-permute-start.3) | collective-permute-done | bytes 69664 | tf_op jit(solution)/shard_map/ppermute | solution.py:29
  23.5 5.9 %krylov.1 = (f32[128,512]{1,0:T(8,128)S(1)}, f32[128,512]{1,0:T(8,128)S(1)}, f32[128,512]{1,0:T(8,128)S(1)}, f32[128,128]{1,0:T(8,128)S(1)}) custom-call(f32[8,128,512]{2,1,0:T(8,128)S(1)} %copy-done.1, f32[8,128,512]{2,1,0:T(8,128)} %c.1, s32[128,512]{1,0:T(8,128)S(1)} %copy-done.4, s32[128,512]{1,0:T(8,128)S(1)} %copy-done.6, f32[128,512]{1,0:T(8,128)S(1)} %copy-done.7, ...), custom_call_target="tpu_custom_call" | custom-call | tf_op jit(solution)/shard_map/krylov/pallas_call | solution.py:337
  30.7 0.7 %copy-done.18 = f32[128,512]{1,0:T(8,128)} copy-done((f32[128,512]{1,0:T(8,128)}, f32[128,512]{1,0:T(8,128)S(1)}, u32[]{:S(2)}) %copy-start.18) | copy-done | bytes 262168
  32.1 16.3 %all-to-all-start = ((f32[128,1,128]{2,1,0:T(1,128)}), f32[128,1,128]{2,1,0:T(1,128)}, u32[]{:S(2)}, u32[]{:S(2)}) async-start(f32[128,1,128]{2,1,0:T(1,128)} %bitcast.4), calls=%async_computation | async-start | bytes 131072 | tf_op jit(solution)/shard_map/all_to_all | solution.py:346
  48.4 0.9 %copy-done.13 = f32[136,128]{1,0:T(8,128)S(1)} copy-done((f32[136,128]{1,0:T(8,128)S(1)}, f32[136,128]{1,0:T(8,128)}, u32[]{:S(2)}) %copy-start.13) | copy-done | bytes 69656
  49.2 3.6 %tracer.1 = f32[8,128,512]{2,1,0:T(8,128)} custom-call(f32[8,128,512]{2,1,0:T(8,128)S(1)} %copy-done.1, s32[128,512]{1,0:T(8,128)S(1)} %copy-done.4, s32[128,512]{1,0:T(8,128)S(1)} %copy-done.6, f32[128,512]{1,0:T(8,128)S(1)} %copy-done.9, f32[128,512]{1,0:T(8,128)S(1)} %copy-done.11, f32[80,512]{1,0:T(8,128)S(1)} %collective-permute-done.near.rn, ...), custom_call_target="tpu_custom_call" | custom-call | flops 10485760 | bytes 6291456 | tf_op jit(solution)/shard_map/tracer/pallas_call | solution.py:347
  52.9 5.2 %all-to-all-done = f32[128,1,128]{2,1,0:T(1,128)} async-done(((f32[128,1,128]{2,1,0:T(1,128)}), f32[128,1,128]{2,1,0:T(1,128)}, u32[]{:S(2)}, u32[]{:S(2)}) %all-to-all-start) | async-done | bytes 65568 | tf_op jit(solution)/shard_map/all_to_all | solution.py:346
  58.1 0.9 %copy-done.15 = f32[128,512]{1,0:T(8,128)S(1)} copy-done((f32[128,512]{1,0:T(8,128)S(1)}, f32[128,512]{1,0:T(8,128)}, u32[]{:S(2)}) %copy-start.15) | copy-done | bytes 262168
  59.0 0.9 %copy-done.17 = f32[128,512]{1,0:T(8,128)S(1)} copy-done((f32[128,512]{1,0:T(8,128)S(1)}, f32[128,512]{1,0:T(8,128)}, u32[]{:S(2)}) %copy-start.17) | copy-done | bytes 262168
  60.0 0.9 %copy-done.19 = f32[128,512]{1,0:T(8,128)S(1)} copy-done((f32[128,512]{1,0:T(8,128)S(1)}, f32[128,512]{1,0:T(8,128)}, u32[]{:S(2)}) %copy-start.19) | copy-done | bytes 262168
  60.9 2.4 %combine.1 = f32[128,512]{1,0:T(8,128)} custom-call(f32[128,128]{1,0:T(8,128)} %bitcast.2.mom, f32[128,512]{1,0:T(8,128)S(1)} %copy-done.15, f32[128,512]{1,0:T(8,128)S(1)} %copy-done.17, f32[128,512]{1,0:T(8,128)S(1)} %copy-done.19), custom_call_target="tpu_custom_call" | custom-call | tf_op jit(solution)/shard_map/combine/pallas_call | solution.py:356
  (34 shorter events, 2.2 us)
Async XLA Ops:
  0.6 1.6 %copy-start = (f32[8,128,512]{2,1,0:T(8,128)S(1)}, f32[8,128,512]{2,1,0:T(8,128)}, u32[]{:S(2)}) copy-start(f32[8,128,512]{2,1,0:T(8,128)} %g.3) | copy-start | bytes 6291460
  2.2 1.6 %copy-start.2 = (f32[8,128,512]{2,1,0:T(8,128)S(1)}, f32[8,128,512]{2,1,0:T(8,128)}, u32[]{:S(2)}) copy-start(f32[8,128,512]{2,1,0:T(8,128)} %c.1) | copy-start | bytes 6291460
  3.8 0.9 %copy-start.3 = (s32[128,512]{1,0:T(8,128)S(1)}, s32[128,512]{1,0:T(8,128)}, u32[]{:S(2)}) copy-start(s32[128,512]{1,0:T(8,128)} %land.3) | copy-start | bytes 786436
  4.8 0.9 %copy-start.5 = (s32[128,512]{1,0:T(8,128)S(1)}, s32[128,512]{1,0:T(8,128)}, u32[]{:S(2)}) copy-start(s32[128,512]{1,0:T(8,128)} %bottom.3) | copy-start | bytes 786436
  5.7 0.9 %copy-start.7 = (f32[128,512]{1,0:T(8,128)S(1)}, f32[128,512]{1,0:T(8,128)}, u32[]{:S(2)}) copy-start(f32[128,512]{1,0:T(8,128)} %surf.1) | copy-start | bytes 786436
  6.7 0.9 %copy-start.8 = (f32[128,512]{1,0:T(8,128)S(1)}, f32[128,512]{1,0:T(8,128)}, u32[]{:S(2)}) copy-start(f32[128,512]{1,0:T(8,128)} %diag.1) | copy-start | bytes 786436
  7.6 0.9 %copy-start.10 = (f32[128,512]{1,0:T(8,128)S(1)}, f32[128,512]{1,0:T(8,128)}, u32[]{:S(2)}) copy-start(f32[128,512]{1,0:T(8,128)} %v.1) | copy-start | bytes 786436
  8.6 3.1 %copy-start.9 = (f32[128,512]{1,0:T(8,128)S(1)}, f32[128,512]{1,0:T(8,128)}, u32[]{:S(2)}) copy-start(f32[128,512]{1,0:T(8,128)} %u.1) | copy-start | bytes 786436
  8.6 5.7 %collective-permute-start = (f32[80,512]{1,0:T(8,128)S(1)}, f32[80,512]{1,0:T(8,128)S(1)}, u32[]{:S(2)}, u32[]{:S(2)}) collective-permute-start(f32[80,512]{1,0:T(8,128)S(1)} %get-tuple-element.12), channel_id=1, source_target_pairs={{0,16},{16,0},{32,48},{48,32},{64,80},{80,64},{96,112},{112,96},{1... | collective-permute-start | bytes 491528 | tf_op jit(solution)/shard_map/ppermute | solution.py:29
  10.8 12.6 %copy-start.1 = (f32[8,128,512]{2,1,0:T(8,128)S(1)}, f32[8,128,512]{2,1,0:T(8,128)}, u32[]{:S(2)}) copy-start(f32[8,128,512]{2,1,0:T(8,128)} %g.3) | copy-start | bytes 6291460
  10.8 12.6 %copy-start.4 = (s32[128,512]{1,0:T(8,128)S(1)}, s32[128,512]{1,0:T(8,128)}, u32[]{:S(2)}) copy-start(s32[128,512]{1,0:T(8,128)} %land.3) | copy-start | bytes 786436
  10.8 12.6 %copy-start.6 = (s32[128,512]{1,0:T(8,128)S(1)}, s32[128,512]{1,0:T(8,128)}, u32[]{:S(2)}) copy-start(s32[128,512]{1,0:T(8,128)} %bottom.3) | copy-start | bytes 786436
  10.8 3.5 %collective-permute-start.1 = (f32[80,512]{1,0:T(8,128)S(1)}, f32[80,512]{1,0:T(8,128)S(1)}, u32[]{:S(2)}, u32[]{:S(2)}) collective-permute-start(f32[80,512]{1,0:T(8,128)S(1)} %get-tuple-element.13), channel_id=1, source_target_pairs={{16,32},{32,16},{48,64},{64,48},{80,96},{96,80},{17,33},{33,17},{4... | collective-permute-start | bytes 491528 | tf_op jit(solution)/shard_map/ppermute | solution.py:29
  14.5 6.6 %collective-permute-start.2 = (f32[136,128]{1,0:T(8,128)S(1)}, f32[136,128]{1,0:T(8,128)S(1)}, u32[]{:S(2)}, u32[]{:S(2)}) collective-permute-start(f32[136,128]{1,0:T(8,128)S(1)} %get-tuple-element.16), channel_id=1, source_target_pairs={{0,1},{1,0},{2,3},{3,2},{4,5},{5,4},{6,7},{7,6},{8,9},{9,8},{10,11... | collective-permute-start | bytes 208904 | tf_op jit(solution)/shard_map/ppermute | solution.py:29
  16.2 32.2 %copy-start.11 = (f32[128,512]{1,0:T(8,128)S(1)}, f32[128,512]{1,0:T(8,128)}, u32[]{:S(2)}) copy-start(f32[128,512]{1,0:T(8,128)} %v.1) | copy-start | bytes 786436
  16.2 7.3 %collective-permute-start.3 = (f32[136,128]{1,0:T(8,128)S(1)}, f32[136,128]{1,0:T(8,128)S(1)}, u32[]{:S(2)}, u32[]{:S(2)}) collective-permute-start(f32[136,128]{1,0:T(8,128)S(1)} %get-tuple-element.17), channel_id=1, source_target_pairs={{1,2},{2,1},{3,4},{4,3},{5,6},{6,5},{7,8},{8,7},{9,10},{10,9},{11,... | collective-permute-start | bytes 208904 | tf_op jit(solution)/shard_map/ppermute | solution.py:29
  23.4 5.9 %copy-start.12 = (f32[136,128]{1,0:T(8,128)}, f32[136,128]{1,0:T(8,128)S(1)}, u32[]{:S(2)}) copy-start(f32[136,128]{1,0:T(8,128)S(1)} %collective-permute-done.3.cf) | copy-start | bytes 208900
  29.3 0.7 %copy-start.14 = (f32[128,512]{1,0:T(8,128)}, f32[128,512]{1,0:T(8,128)S(1)}, u32[]{:S(2)}) copy-start(f32[128,512]{1,0:T(8,128)S(1)} %get-tuple-element.19.r) | copy-start | bytes 786436
  30.7 0.7 %copy-start.18 = (f32[128,512]{1,0:T(8,128)}, f32[128,512]{1,0:T(8,128)S(1)}, u32[]{:S(2)}) copy-start(f32[128,512]{1,0:T(8,128)S(1)} %get-tuple-element.21.p2) | copy-start | bytes 786436
  32.1 26.0 %all-to-all-start = ((f32[128,1,128]{2,1,0:T(1,128)}), f32[128,1,128]{2,1,0:T(1,128)}, u32[]{:S(2)}, u32[]{:S(2)}) async-start(f32[128,1,128]{2,1,0:T(1,128)} %bitcast.4), calls=%async_computation | async-start | bytes 131072 | tf_op jit(solution)/shard_map/all_to_all | solution.py:346
  48.4 0.9 %copy-start.13 = (f32[136,128]{1,0:T(8,128)S(1)}, f32[136,128]{1,0:T(8,128)}, u32[]{:S(2)}) copy-start(f32[136,128]{1,0:T(8,128)} %copy-done.12) | copy-start | bytes 208900
  58.1 1.0 %copy-start.15 = (f32[128,512]{1,0:T(8,128)S(1)}, f32[128,512]{1,0:T(8,128)}, u32[]{:S(2)}) copy-start(f32[128,512]{1,0:T(8,128)} %copy-done.14) | copy-start | bytes 786436
  59.0 0.9 %copy-start.17 = (f32[128,512]{1,0:T(8,128)S(1)}, f32[128,512]{1,0:T(8,128)}, u32[]{:S(2)}) copy-start(f32[128,512]{1,0:T(8,128)} %copy-done.16) | copy-start | bytes 786436
  60.0 0.9 %copy-start.19 = (f32[128,512]{1,0:T(8,128)S(1)}, f32[128,512]{1,0:T(8,128)}, u32[]{:S(2)}) copy-start(f32[128,512]{1,0:T(8,128)} %copy-done.18) | copy-start | bytes 786436
  (2 other events, 1.3 us)

commit v2 on v1

v2 whole, which is shorter than its diff:
```python
import jax
import jax.numpy as jnp
from jax import lax
from jax.experimental import pallas as pl
from jax.experimental.pallas import tpu as pltpu
from jax.sharding import PartitionSpec as P

LEV = 8
DEEP = 4
SHIFT = 1.0
F32 = jnp.float32
VMEM = pl.BlockSpec(memory_space=pltpu.VMEM)
HBM = pl.BlockSpec(memory_space=pltpu.HBM)
PARAMS = pltpu.CompilerParams(vmem_limit_bytes=32 * 1024 * 1024)


CODE, SURF, DIAG, SPEED = 16, 17, 18, 19


def code_of(land, bottom):
    return jnp.where(land == 1, bottom, 0).astype(F32)


def swap_pairs(axis, first):
    count = lax.axis_size(axis)
    pairs = []
    for low in range(first, count - 1, 2):
        pairs += [(low, low + 1), (low + 1, low)]
    return pairs


def swap(buffers, axis):
    return [lax.ppermute(b, axis, swap_pairs(axis, first)) for first, b in enumerate(buffers)]


def is_even(axis):
    return lax.rem(lax.axis_index(axis), 2) == 0


def iota(shape, dim):
    return lax.broadcasted_iota(jnp.int32, shape, dim)


def turn(x, by, dim):
    by = by % x.shape[dim]
    return pltpu.roll(x, by, dim) if by else x


def next_col(a):
    return turn(a, -1, 1)


def prev_col(a):
    return turn(a, 1, 1)


def next_row(a):
    return turn(a, -1, 0)


def prev_row(a):
    return turn(a, 1, 0)


def pick(even, one, two):
    return jnp.where(even, one, two), jnp.where(even, two, one)


def start_all(copies):
    for copy in copies:
        copy.start()


def wait_all(copies):
    for copy in copies:
        copy.wait()


def pack_rows(g, c, land, bottom, surf, diag, v, a_ref, b_ref, g0, g1, c0, c1, l0, l1, b0, b1, s0, s1, d0, d1, v0, v1, sems):
    rows = surf.shape[0]
    copies = []
    for src, low, high in ((g, g0, g1), (c, c0, c1), (land, l0, l1), (bottom, b0, b1), (surf, s0, s1), (diag, d0, d1), (v, v0, v1)):
        for dst, at in ((low, slice(0, 8)), (high, slice(rows - 8, rows))):
            part = src.at[:, at, :] if len(src.shape) == 3 else src.at[at, :]
            copies.append(pltpu.make_async_copy(part, dst, sems.at[len(copies)]))
    start_all(copies)
    wait_all(copies)

    def planes(g, c, land, bottom, surf, diag, v):
        pairs = [x for k in range(LEV) for x in (g[k], c[k])]
        return pairs + [code_of(land[...], bottom[...]), surf[...], diag[...], v[...]]

    first = planes(g0, c0, l0, b0, s0, d0, v0)
    last = planes(g1, c1, l1, b1, s1, d1, v1)
    upper = iota(first[0].shape, 0) < DEEP
    even = is_even("row")
    for t in range(len(first) // 2):
        high = jnp.where(upper, turn(last[2 * t], DEEP, 0), last[2 * t + 1])
        low = jnp.where(upper, first[2 * t], turn(first[2 * t + 1], DEEP, 0))
        a_ref[8 * t : 8 * t + 8, :], b_ref[8 * t : 8 * t + 8, :] = pick(even, high, low)


def lane_pack(g, c, code, rest, of_last):
    group = iota(code.shape, 1) // DEEP
    base = DEEP if of_last else 0
    out = jnp.where(group == 16, turn(code, 64 + base, 1), 0.0)
    for by in (8, 16, 32):
        out = out + turn(out, by, 1)
    for k in range(LEV):
        out = jnp.where(group == 2 * k, turn(g[k], 8 * k + base, 1), out)
        out = jnp.where(group == 2 * k + 1, turn(c[k], 8 * k + 4 + base, 1), out)
    for n, x in enumerate(rest):
        out = jnp.where(group == 17 + 2 * n, turn(x, 68 + 8 * n + base, 1), out)
    return out


def local(g, c, land, bottom, surf, diag, u, s_ref, code_ref, diag_ref, a_ref, b_ref, gv, cv, lv, bv, sv, uv, sems, band_sems):
    rows, cols = surf.shape
    bands = band_sems.shape[0]
    tall = rows // bands
    flat = [
        pltpu.make_async_copy(src, dst, sems.at[n])
        for n, (src, dst) in enumerate(((land, lv), (bottom, bv), (surf, sv), (diag, diag_ref), (u, uv)))
    ]
    deep = []
    for b in range(bands):
        at = slice(b * tall, (b + 1) * tall)
        for n, (src, dst) in enumerate(((g, gv), (c, cv))):
            deep.append(pltpu.make_async_copy(src.at[:, at, :], dst.at[:, at, :], band_sems.at[b, n]))
    start_all(flat[:2] + deep[:2] + flat[2:] + deep[2:])
    wait_all(flat)
    code_ref[...] = code_of(lv[...], bv[...])
    even = is_even("col")
    lane, sub = iota((8, cols), 1), iota((8, cols), 0)
    vb_before = jnp.zeros((8, cols), F32)
    for i in range(rows // 8):
        at = slice(8 * i, 8 * i + 8)
        after = slice(8 * i + 8, 8 * i + 16)
        is_last = i == rows // 8 - 1
        if i == 0:
            wait_all(deep[:2])
        if (8 * i + 8) % tall == 0 and not is_last:
            b = (8 * i + 8) // tall
            wait_all(deep[2 * b : 2 * b + 2])

        def down(here, there):
            return turn(jnp.where(sub == 0, there, here), -1, 0)

        code = code_ref[at, :]
        cu = jnp.where(lane < cols - 1, jnp.minimum(code, next_col(code)), 0.0)
        if is_last:
            co = jnp.where(sub < 7, jnp.minimum(code, next_row(code)), 0.0)
        else:
            co = jnp.minimum(code, down(code, code_ref[after, :]))
        ub = jnp.zeros((8, cols), F32)
        vb = jnp.zeros((8, cols), F32)
        gs, cs = [], []
        for k in range(LEV):
            gk, ck = gv[k, at, :], cv[k, at, :]
            gs.append(gk)
            cs.append(ck)
            gn = next_row(gk) if is_last else down(gk, gv[k, after, :])
            cn = next_row(ck) if is_last else down(ck, cv[k, after, :])
            ub = ub + jnp.where(cu > k + 0.5, next_col(gk) - gk, 0.0) * (next_col(ck) + ck)
            vb = vb + jnp.where(co > k + 0.5, gn - gk, 0.0) * (cn + ck)
        vb_prev = turn(jnp.where(sub == 7, vb_before, vb), 1, 0)
        vb_before = vb
        s_ref[at, :] = sv[at, :] + 0.0625 * ((ub - prev_col(ub)) + (vb - vb_prev))
        rest = (sv[at, :], diag_ref[at, :], uv[at, :])
        packs = []
        for of_last, lanes in ((True, slice(cols - 128, cols)), (False, slice(0, 128))):
            cut = lambda xs: [x[:, lanes] for x in xs]
            packs.append(lane_pack(cut(gs), cut(cs), code[:, lanes], cut(rest), of_last))
        a_ref[at, :], b_ref[at, :] = pick(even, *packs)


def row_halo(near, far, lanes):
    even = is_even("row")

    def plane(p):
        at = slice(8 * (p // 2), 8 * (p // 2) + 8)
        north, south = pick(even, near[at, lanes], far[at, lanes])
        upper = iota(north.shape, 0) < DEEP
        if p % 2 == 0:
            return jnp.where(upper, north, turn(south, DEEP, 0))
        return jnp.where(upper, turn(north, DEEP, 0), south)

    return plane


def join_cols(a_in, b_in, near, far, a_ref, b_ref):
    rows, width = a_in.shape[0], near.shape[1]
    packs = []
    for of_last, lanes in ((True, slice(width - 128, width)), (False, slice(0, 128))):
        halo = row_halo(near, far, lanes)
        packs.append(
            lane_pack(
                [halo(2 * k) for k in range(LEV)],
                [halo(2 * k + 1) for k in range(LEV)],
                halo(CODE),
                [halo(SURF), halo(DIAG)],
                of_last,
            )
        )
    a_ref[:rows, :] = a_in[...]
    b_ref[:rows, :] = b_in[...]
    a_ref[rows:, :], b_ref[rows:, :] = pick(is_even("col"), *packs)


def halo_rows(s, code, diag, sent_a, sent_b, near, far, s_ref, code_ref, diag_ref):
    rows, cols = s.shape
    even = is_even("row")
    lane, sub = iota((8, cols), 1), iota((8, cols), 0)
    upper = sub < DEEP

    def strips(t):
        at = slice(8 * t, 8 * t + 8)
        high, low = pick(even, sent_a[at, :], sent_b[at, :])
        north, south = pick(even, near[at, :], far[at, :])
        one = [jnp.where(upper, x, turn(y, DEEP, 0)) for x, y in ((high, north), (south, low))]
        two = [jnp.where(upper, turn(x, DEEP, 0), y) for x, y in ((high, north), (south, low))]
        return one, two

    codes, surfs = strips(LEV)
    cus = [jnp.where(lane < cols - 1, jnp.minimum(x, next_col(x)), 0.0) for x in codes]
    cos = [jnp.where(sub < 7, jnp.minimum(x, next_row(x)), 0.0) for x in codes]
    ubs = [jnp.zeros((8, cols), F32)] * 2
    vbs = [jnp.zeros((8, cols), F32)] * 2
    for k in range(LEV):
        gs, cs = strips(k)
        for n in range(2):
            gk, ck = gs[n], cs[n]
            ubs[n] = ubs[n] + jnp.where(cus[n] > k + 0.5, next_col(gk) - gk, 0.0) * (next_col(ck) + ck)
            vbs[n] = vbs[n] + jnp.where(cos[n] > k + 0.5, next_row(gk) - gk, 0.0) * (next_row(ck) + ck)
    north, south = [
        surfs[n] + 0.0625 * ((ubs[n] - prev_col(ubs[n])) + (vbs[n] - prev_row(vbs[n]))) for n in range(2)
    ]
    s_ref[:rows, :] = s[...]
    code_ref[:rows, :] = code[...]
    diag_ref[:rows, :] = diag[...]
    s_ref[rows - 8 : rows, :] = s[rows - 8 :, :] + jnp.where(sub == 7, turn(0.0625 * vbs[0], 4, 0), 0.0)
    s_ref[:8, :] = s[:8, :] - jnp.where(sub == 0, turn(0.0625 * vbs[1], -3, 0), 0.0)
    s_ref[rows:, :] = turn(jnp.where(upper, south, north), DEEP, 0)
    halo = row_halo(near, far, slice(0, cols))
    code_ref[rows:, :] = halo(CODE)
    diag_ref[rows:, :] = halo(DIAG)


def col_halo(near, far):
    east, west = pick(is_even("col"), near[...], far[...])
    left = iota(east.shape, 1) < 64

    def plane(at):
        return jnp.where(left, turn(east, -at, 1), turn(west, 124 - at, 1))

    return plane


def krylov(s, code, diag, sent_a, sent_b, near, far, r_ref, p1_ref, p2_ref, mom_ref, r_v, p1_v, p2_v, sems):
    rows, cols = r_v.shape
    even = is_even("col")
    high, low = pick(even, sent_a[...], sent_b[...])
    east, west = pick(even, near[...], far[...])
    lane = iota(high.shape, 1)
    own, left = lane % 8 < DEEP, lane < 64

    def strip(one, two):
        return jnp.where(left, one, turn(two, 64, 1))

    gs = strip(*[jnp.where(own, x, turn(y, 4, 1)) for x, y in ((high, east), (west, low))])
    cs = strip(*[jnp.where(own, turn(x, -4, 1), y) for x, y in ((high, east), (west, low))])
    ks = strip(*[jnp.where(own, turn(x, -64, 1), turn(y, -60, 1)) for x, y in ((high, east), (west, low))])
    level = ((lane % 64) // 8).astype(F32) + 0.5
    open_u = (jnp.minimum(ks, next_col(ks)) > level) & (lane % 8 < 7)
    open_v = jnp.minimum(ks, next_row(ks)) > level
    ub = jnp.where(open_u, next_col(gs) - gs, 0.0) * (next_col(cs) + cs)
    vb = jnp.where(open_v, next_row(gs) - gs, 0.0) * (next_row(cs) + cs)
    for by in (8, 16, 32):
        ub = ub + turn(ub, -by, 1)
        vb = vb + turn(vb, -by, 1)
    ub, vb = 0.0625 * ub, 0.0625 * vb
    terms = (ub - prev_col(ub)) + (vb - prev_row(vb))
    halo = col_halo(near, far)
    r_side = jnp.where(left, turn(terms, -4, 1), turn(terms, 60, 1)) + halo(68)
    r = jnp.concatenate(
        [
            s[:, :128] - jnp.where(lane == 0, turn(ub, -67, 1), 0.0),
            s[:, 128 : cols - 128],
            s[:, cols - 128 :] + jnp.where(lane == 127, turn(ub, 124, 1), 0.0),
            r_side,
        ],
        axis=1,
    )
    code = 0.125 * jnp.concatenate([code[...], halo(64)], axis=1)
    dg = jnp.concatenate([diag[...], halo(76)], axis=1)
    cu, cv = jnp.minimum(code, next_col(code)), jnp.minimum(code, next_row(code))

    def shifted(v):
        fu, fv = cu * (v - next_col(v)), cv * (v - next_row(v))
        return (dg - SHIFT) * v + ((fu - prev_col(fu)) + (fv - prev_row(fv)))

    copies = []

    def send(x, own, out):
        own[...] = x[:rows, :cols]
        copies.append(pltpu.make_async_copy(own, out, sems.at[len(copies)]))
        copies[-1].start()

    send(r, r_v, r_ref)
    p1 = shifted(r)
    send(p1, p1_v, p1_ref)
    p2 = shifted(p1)
    send(p2, p2_v, p2_ref)
    eu, ev = p2 - next_col(p2), p2 - next_row(p2)
    energy = dg * p2 * p2 + (cu * eu * eu + cv * ev * ev)
    r, p1, p2, energy = [a[:rows, :cols] for a in (r, p1, p2, energy)]
    lane = iota((8, 128), 1)
    packed = jnp.zeros((8, 128), F32)
    for m, prod in enumerate((r * r, r * p1, p1 * p1, p1 * p2, p2 * p2, energy)):
        tiles = [
            prod[8 * i : 8 * i + 8, 128 * j : 128 * j + 128]
            for i in range(rows // 8)
            for j in range(cols // 128)
        ]
        while len(tiles) > 1:
            tiles = [sum(tiles[i : i + 2][1:], tiles[i]) for i in range(0, len(tiles), 2)]
        part = tiles[0]
        for by in (4, 2, 1):
            part = part + pltpu.roll(part, by, 0)
        for by in (64, 32, 16):
            part = part + pltpu.roll(part, by, 1)
        packed = jnp.where(lane // 16 == m, part, packed)
    for i in range(mom_ref.shape[0] // 8):
        mom_ref[8 * i : 8 * i + 8, :] = packed
    wait_all(copies)


def tracer_kernel(g, land, bottom, u, v, rn, rf, cn, cf, out_ref):
    rows, cols = u.shape
    rh, ch = row_halo(rn, rf, slice(0, cols)), col_halo(cn, cf)

    def wide(own, p, lane):
        return jnp.concatenate([jnp.concatenate([own, rh(p)], axis=0), ch(lane)], axis=1)

    code = wide(code_of(land[...], bottom[...]), CODE, 64)
    cu, cv = jnp.minimum(code, next_col(code)), jnp.minimum(code, next_row(code))
    uw = 0.125 * wide(u[...], SPEED, 84)
    vw = 0.125 * wide(v[...], SPEED, 84)
    for k in range(LEV):
        gk = wide(g[k], 2 * k, 8 * k)
        pu = jnp.where(cu > k + 0.5, next_col(gk) - gk, 0.0) * uw
        pv = jnp.where(cv > k + 0.5, next_row(gk) - gk, 0.0) * vw
        total = gk + pu + prev_col(pu) + pv + prev_row(pv)
        out_ref[k] = total[:rows, :cols]


def two_sum(a, b):
    s = a + b
    t = s - a
    return s, (a - (s - t)) + (b - t)


def quick(a, b):
    s = a + b
    return s, b - (s - a)


def split(a):
    t = a * 4097.0
    high = t - (t - a)
    return high, a - high


def add(x, y):
    s, e = two_sum(x[0], y[0])
    return quick(s, e + (x[1] + y[1]))


def neg(x):
    return -x[0], -x[1]


def mul(x, y):
    p = x[0] * y[0]
    (ah, al), (bh, bl) = split(x[0]), split(y[0])
    e = ((ah * bh - p) + ah * bl + al * bh) + al * bl
    return quick(p, e + (x[0] * y[1] + x[1] * y[0]))


def div(x, y):
    q = x[0] / y[0]
    rest = add(x, neg(mul((q, jnp.zeros_like(q)), y)))
    return quick(q, rest[0] / y[0])


def combine(mom_in, r_in, p1_in, p2_in, x_ref, mom, r, p1, p2, sems):
    copies = [
        pltpu.make_async_copy(src, dst, sems.at[n])
        for n, (src, dst) in enumerate(((mom_in, mom), (r_in, r), (p1_in, p1), (p2_in, p2)))
    ]
    start_all(copies)
    copies[0].wait()
    zero = jnp.zeros((8, 128), F32)
    tiles = [(mom[8 * i : 8 * i + 8, :], zero) for i in range(mom.shape[0] // 8)]
    while len(tiles) > 1:
        tiles = [add(tiles[i], tiles[i + 1]) for i in range(0, len(tiles), 2)]
    total = tiles[0]
    for by in (4, 2, 1):
        total = add(total, tuple(pltpu.roll(a, by, 0) for a in total))
    lane = iota((8, 128), 1)
    sums = []
    for m in range(6):
        mine = tuple(jnp.where(lane // 16 == m, a, 0.0) for a in total)
        for by in (64, 32, 16, 8, 4, 2, 1):
            mine = add(mine, tuple(pltpu.roll(a, by, 1) for a in mine))
        sums.append(mine)
    m00, m01, m11, m12, m22, e22 = sums
    a00, a01, a02 = add(m01, m00), add(m11, m01), add(m12, m11)
    a11, a12, a22 = a02, add(m22, m12), e22
    l10 = div(a01, a00)
    l20 = div(a02, a00)
    w11 = add(a11, neg(mul(l10, a01)))
    w12 = add(a12, neg(mul(l10, a02)))
    ok1 = w11[0] > 1e-9 * a11[0]
    l21 = tuple(jnp.where(ok1, a, 0.0) for a in div(w12, w11))
    w22 = add(add(a22, neg(mul(l20, a02))), neg(mul(l21, w12)))
    ok2 = w22[0] > 1e-9 * a22[0]
    b0 = m00
    b1 = add(m01, neg(mul(l10, b0)))
    z1 = tuple(jnp.where(ok1, a, 0.0) for a in div(b1, w11))
    b2 = add(add(m11, neg(mul(l20, b0))), neg(mul(l21, b1)))
    z2 = tuple(jnp.where(ok2, a, 0.0) for a in div(b2, w22))
    y2 = z2
    y1 = add(z1, neg(mul(l21, y2)))
    y0 = add(div(b0, a00), neg(add(mul(l10, y1), mul(l20, y2))))
    wait_all(copies[1:])
    rows, cols = r.shape
    for i in range(rows // 8):
        for j in range(cols // 128):
            at = (slice(8 * i, 8 * i + 8), slice(128 * j, 128 * j + 128))
            x_ref[at] = y0[0] * r[at] + (y1[0] * p1[at] + y2[0] * p2[at])


def call(kernel, ins, outs, scratch=(), name=None, cost=None):
    return pl.pallas_call(
        kernel,
        in_specs=list(ins),
        out_specs=[spec for spec, _ in outs],
        out_shape=[jax.ShapeDtypeStruct(shape, F32) for _, shape in outs],
        scratch_shapes=list(scratch),
        compiler_params=PARAMS,
        cost_estimate=cost,
        name=name,
    )


def shards(tracer_adj_next, tracer, u_east, v_north, surf_adj_next, diag, land, bottom):
    levels, rows, cols = tracer.shape
    planes = 2 * levels + 4
    size = lax.axis_size("row") * lax.axis_size("col")
    g, c = tracer_adj_next, tracer
    dma = pltpu.SemaphoreType.DMA
    two, wide, side = (rows, cols), (rows + 8, cols), (rows + 8, 128)
    whole = lambda kind=F32: pltpu.VMEM(two, kind)
    edges = [pltpu.VMEM((levels, 8, cols), F32)] * 4 + [pltpu.VMEM((8, cols), jnp.int32)] * 4 + [pltpu.VMEM((8, cols), F32)] * 6
    row_sent = call(
        pack_rows, [HBM] * 7, [(VMEM, (4 * planes, cols))] * 2, edges + [dma((14,))], name="pack_rows"
    )(g, c, land, bottom, surf_adj_next, diag, v_north)
    row_got = swap(row_sent, "row")
    deep = pltpu.VMEM(g.shape, F32)
    s, code, dg, a, b = call(
        local,
        [HBM] * 7,
        [(VMEM, two)] * 3 + [(VMEM, (rows, 128))] * 2,
        [deep, deep, whole(jnp.int32), whole(jnp.int32), whole(), whole(), dma((5,)), dma((4, 2))],
        name="local",
        cost=pl.CostEstimate(flops=24 * g.size, bytes_accessed=8 * g.size, transcendentals=0),
    )(g, c, land, bottom, surf_adj_next, diag, u_east)
    col_sent = call(join_cols, [VMEM] * 4, [(VMEM, side)] * 2, name="join_cols")(a, b, *row_got)
    col_got = swap(col_sent, "col")
    s, code, dg = call(halo_rows, [VMEM] * 7, [(VMEM, wide)] * 3, name="halo_rows")(
        s, code, dg, *row_sent, *row_got
    )
    r, p1, p2, mom = call(
        krylov,
        [VMEM] * 7,
        [(HBM, two)] * 3 + [(VMEM, (size, 128))],
        [whole(), whole(), whole(), dma((3,))],
        name="krylov",
    )(s, code, dg, *col_sent, *col_got)
    mom = lax.all_to_all(mom, ("row", "col"), 0, 0, tiled=True)
    (tracer_adj,) = call(
        tracer_kernel,
        [VMEM] * 9,
        [(VMEM, g.shape)],
        name="tracer",
        cost=pl.CostEstimate(flops=20 * g.size, bytes_accessed=12 * g.size, transcendentals=0),
    )(g, land, bottom, u_east, v_north, *row_got, *col_got)
    (surf_adj,) = call(
        combine,
        [HBM] * 4,
        [(VMEM, two)],
        [pltpu.VMEM((size, 128), F32), whole(), whole(), whole(), dma((4,))],
        name="combine",
    )(mom, r, p1, p2)
    return tracer_adj, surf_adj


def solution(mesh):
    three, two = P(None, "row", "col"), P("row", "col")
    return jax.shard_map(
        shards,
        mesh=mesh,
        in_specs=(three, three, two, two, two, two, two, two),
        out_specs=(three, two),
        check_vma=False,
    )
```

time: 63.9 us -> 61.9 us (0.969)
  Pallas kernels: 12.8 us -> 16.9 us
  starting transfers between devices: 25.8 us -> 22.2 us
  waiting for transfers between devices: 9.51 us -> 7.08 us
    pallas_call x6 -> x7, Pallas kernels: 12.8 us -> 16.9 us  [the longest x1 7.45 us: shards(): call(local, [HBM] * 7, [(VMEM, two)] * 3 + [(VMEM, (rows, 128))] * 2, [de...]
    all_to_all x1, starting transfers between devices: 16.3 us -> 13.6 us  [shards(): mom = lax.all_to_all(mom, ('row', 'col'), 0, 0, tiled=True)]
    ppermute x4, waiting for transfers between devices: 4.34 us -> 2.1 us  [swap(): lax.ppermute(b, axis, swap_pairs(axis, first))]
    ppermute x4, starting transfers between devices: 9.57 us -> 8.58 us  [swap(): lax.ppermute(b, axis, swap_pairs(axis, first))]
  transfers between devices with their start and end apart: 5 -> 5, of which waited for: 3 -> 2; matrix products, arithmetic and copies ran while one was open for 0% -> 0% of each run, Pallas kernels for 7% -> 19%
where the time goes in v2:
time: 61.9 us; the launch traced here: 61.4 us
  starting transfers between devices  22.2 us (36%)
  Pallas kernels  16.9 us (27%)
  local copies, waits for them, and re-layouts  14.4 us (23%)
  waiting for transfers between devices  7.08 us (11%)
  between operations  0.84 us (1%)
    unnamed x42, local copies, waits for them, and re-layouts  14.4 us
    all_to_all x1, starting transfers between devices, shards(): mom = lax.all_to_all(mom, ('row', 'col'), 0, 0, tiled=True)  13.6 us
    ppermute x4, starting transfers between devices, swap(): lax.ppermute(b, axis, swap_pairs(axis, first))  8.58 us
    pallas_call x1, Pallas kernels, shards(): call(local, [HBM] * 7, [(VMEM, two)] * 3 + [(VMEM, (rows, 128))] * 2, [de...  7.45 us
    all_to_all x1, waiting for transfers between devices, shards(): mom = lax.all_to_all(mom, ('row', 'col'), 0, 0, tiled=True)  4.98 us
    pallas_call x1, Pallas kernels, shards(): call(tracer_kernel, [VMEM] * 9, [(VMEM, g.shape)], name='tracer', cost=pl...  3.64 us
    pallas_call x1, Pallas kernels, shards(): call(combine, [HBM] * 4, [(VMEM, two)], [pltpu.VMEM((size, 128), F32), wh...  2.46 us
    pallas_call x1, Pallas kernels, shards(): call(krylov, [VMEM] * 7, [(HBM, two)] * 3 + [(VMEM, (size, 128))], [whole...  2.21 us
  transfers between devices with their start and end apart: 5, of which 2 were waited for; matrix products, arithmetic and copies ran while one was open for 0% of the time, Pallas kernels for 19%

profile of v2, /device:TPU:1, one launch (start us, length us, event | category | flops | bytes accessed | tf_op | source)
XLA Modules:
  0.0 61.4 jit_solution(7244024703696668956)
XLA Ops:
  0.6 1.6 %copy-done = f32[8,128,512]{2,1,0:T(8,128)S(1)} copy-done((f32[8,128,512]{2,1,0:T(8,128)S(1)}, f32[8,128,512]{2,1,0:T(8,128)}, u32[]{:S(2)}) %copy-start) | copy-done | bytes 2097176
  2.2 1.6 %copy-done.2 = f32[8,128,512]{2,1,0:T(8,128)S(1)} copy-done((f32[8,128,512]{2,1,0:T(8,128)S(1)}, f32[8,128,512]{2,1,0:T(8,128)}, u32[]{:S(2)}) %copy-start.2) | copy-done | bytes 2097176
  3.8 0.9 %copy-done.3 = s32[128,512]{1,0:T(8,128)S(1)} copy-done((s32[128,512]{1,0:T(8,128)S(1)}, s32[128,512]{1,0:T(8,128)}, u32[]{:S(2)}) %copy-start.3) | copy-done | bytes 262168
  4.8 0.9 %copy-done.5 = s32[128,512]{1,0:T(8,128)S(1)} copy-done((s32[128,512]{1,0:T(8,128)S(1)}, s32[128,512]{1,0:T(8,128)}, u32[]{:S(2)}) %copy-start.5) | copy-done | bytes 262168
  5.7 0.9 %copy-done.8 = f32[128,512]{1,0:T(8,128)S(1)} copy-done((f32[128,512]{1,0:T(8,128)S(1)}, f32[128,512]{1,0:T(8,128)}, u32[]{:S(2)}) %copy-start.8) | copy-done | bytes 262168
  6.7 0.9 %copy-done.10 = f32[128,512]{1,0:T(8,128)S(1)} copy-done((f32[128,512]{1,0:T(8,128)S(1)}, f32[128,512]{1,0:T(8,128)}, u32[]{:S(2)}) %copy-start.10) | copy-done | bytes 262168
  7.6 0.9 %copy-done.11 = f32[128,512]{1,0:T(8,128)S(1)} copy-done((f32[128,512]{1,0:T(8,128)S(1)}, f32[128,512]{1,0:T(8,128)}, u32[]{:S(2)}) %copy-start.11) | copy-done | bytes 262168
  9.1 2.2 %collective-permute-start = (f32[80,512]{1,0:T(8,128)S(1)}, f32[80,512]{1,0:T(8,128)S(1)}, u32[]{:S(2)}, u32[]{:S(2)}) collective-permute-start(f32[80,512]{1,0:T(8,128)S(1)} %get-tuple-element.18.sent_a), channel_id=1, source_target_pairs={{0,16},{16,0},{32,48},{48,32},{64,80},{80,64},{96,112},{112,96},{1... | collective-permute-start | bytes 491528 | tf_op jit(solution)/shard_map/ppermute | solution.py:33
  11.9 7.5 %local.1 = (f32[128,512]{1,0:T(8,128)S(1)}, f32[128,512]{1,0:T(8,128)S(1)}, f32[128,512]{1,0:T(8,128)S(1)}, f32[128,128]{1,0:T(8,128)S(1)}, f32[128,128]{1,0:T(8,128)S(1)}) custom-call(f32[8,128,512]{2,1,0:T(8,128)S(1)} %copy-done, f32[8,128,512]{2,1,0:T(8,128)S(1)} %copy-done.2, s32[128,512]{1,0:T(8,128)S(1)} %copy-done.3, s32[128,512]{1,0:T(8,128)S(1)} %copy-done.5, ...), custom_call_target="tpu_custom_call" | custom-call | flops 12582912 | bytes 4194304 | tf_op jit(solution)/shard_map/local/pallas_call | solution.py:471
  19.8 1.0 %collective-permute-start.2 = (f32[136,128]{1,0:T(8,128)S(1)}, f32[136,128]{1,0:T(8,128)S(1)}, u32[]{:S(2)}, u32[]{:S(2)}) collective-permute-start(f32[136,128]{1,0:T(8,128)S(1)} %get-tuple-element.22.sent_a), channel_id=1, source_target_pairs={{0,1},{1,0},{2,3},{3,2},{4,5},{5,4},{6,7},{7,6},{8,9},{9,8},{10,11... | collective-permute-start | bytes 208904 | tf_op jit(solution)/shard_map/ppermute | solution.py:33
  20.8 4.7 %collective-permute-start.3 = (f32[136,128]{1,0:T(8,128)S(1)}, f32[136,128]{1,0:T(8,128)S(1)}, u32[]{:S(2)}, u32[]{:S(2)}) collective-permute-start(f32[136,128]{1,0:T(8,128)S(1)} %get-tuple-element.23.sent_b), channel_id=1, source_target_pairs={{1,2},{2,1},{3,4},{4,3},{5,6},{6,5},{7,8},{8,7},{9,10},{10,9},{11,... | collective-permute-start | bytes 208904 | tf_op jit(solution)/shard_map/ppermute | solution.py:33
  25.8 2.1 %collective-permute-done.3.cf.far = f32[136,128]{1,0:T(8,128)S(1)} collective-permute-done((f32[136,128]{1,0:T(8,128)S(1)}, f32[136,128]{1,0:T(8,128)S(1)}, u32[]{:S(2)}, u32[]{:S(2)}) %collective-permute-start.3) | collective-permute-done | bytes 69664 | tf_op jit(solution)/shard_map/ppermute | solution.py:33
  27.9 2.2 %krylov.1 = (f32[128,512]{1,0:T(8,128)S(1)}, f32[128,512]{1,0:T(8,128)S(1)}, f32[128,512]{1,0:T(8,128)S(1)}, f32[128,128]{1,0:T(8,128)S(1)}) custom-call(f32[136,512]{1,0:T(8,128)S(1)} %get-tuple-element.27.s, f32[136,512]{1,0:T(8,128)S(1)} %get-tuple-element.28.code, f32[136,512]{1,0:T(8,128)S(1)} %get-tuple-element.29.diag, ...), custom_call_target="tpu_custom_call" | custom-call | tf_op jit(solution)/shard_map/krylov/pallas_call | solution.py:484
  30.2 0.7 %copy-done.14 = f32[128,512]{1,0:T(8,128)} copy-done((f32[128,512]{1,0:T(8,128)}, f32[128,512]{1,0:T(8,128)S(1)}, u32[]{:S(2)}) %copy-start.14) | copy-done | bytes 262168
  30.9 0.7 %copy-done.16 = f32[128,512]{1,0:T(8,128)} copy-done((f32[128,512]{1,0:T(8,128)}, f32[128,512]{1,0:T(8,128)S(1)}, u32[]{:S(2)}) %copy-start.16) | copy-done | bytes 262168
  31.6 0.7 %copy-done.18 = f32[128,512]{1,0:T(8,128)} copy-done((f32[128,512]{1,0:T(8,128)}, f32[128,512]{1,0:T(8,128)S(1)}, u32[]{:S(2)}) %copy-start.18) | copy-done | bytes 262168
  32.9 13.6 %all-to-all-start = ((f32[128,1,128]{2,1,0:T(1,128)}), f32[128,1,128]{2,1,0:T(1,128)}, u32[]{:S(2)}, u32[]{:S(2)}) async-start(f32[128,1,128]{2,1,0:T(1,128)} %bitcast.4), calls=%async_computation | async-start | bytes 131072 | tf_op jit(solution)/shard_map/all_to_all | solution.py:491
  46.6 0.9 %copy-done.13 = f32[136,128]{1,0:T(8,128)S(1)} copy-done((f32[136,128]{1,0:T(8,128)S(1)}, f32[136,128]{1,0:T(8,128)}, u32[]{:S(2)}) %copy-start.13) | copy-done | bytes 69656
  47.4 3.6 %tracer.1 = f32[8,128,512]{2,1,0:T(8,128)} custom-call(f32[8,128,512]{2,1,0:T(8,128)S(1)} %copy-done.1, s32[128,512]{1,0:T(8,128)S(1)} %copy-done.4, s32[128,512]{1,0:T(8,128)S(1)} %copy-done.6, f32[128,512]{1,0:T(8,128)S(1)} %copy-done.7, f32[128,512]{1,0:T(8,128)S(1)} %copy-done.9, f32[80,512]{1,0:T(8,128)S(1)} %collective-permute-done.near.rn, ...), custom_call_target="tpu_custom_call" | custom-call | flops 10485760 | bytes 6291456 | tf_op jit(solution)/shard_map/tracer/pallas_call | solution.py:492
  51.1 5.0 %all-to-all-done = f32[128,1,128]{2,1,0:T(1,128)} async-done(((f32[128,1,128]{2,1,0:T(1,128)}), f32[128,1,128]{2,1,0:T(1,128)}, u32[]{:S(2)}, u32[]{:S(2)}) %all-to-all-start) | async-done | bytes 65568 | tf_op jit(solution)/shard_map/all_to_all | solution.py:491
  56.1 0.9 %copy-done.15 = f32[128,512]{1,0:T(8,128)S(1)} copy-done((f32[128,512]{1,0:T(8,128)S(1)}, f32[128,512]{1,0:T(8,128)}, u32[]{:S(2)}) %copy-start.15) | copy-done | bytes 262168
  57.0 0.9 %copy-done.17 = f32[128,512]{1,0:T(8,128)S(1)} copy-done((f32[128,512]{1,0:T(8,128)S(1)}, f32[128,512]{1,0:T(8,128)}, u32[]{:S(2)}) %copy-start.17) | copy-done | bytes 262168
  58.0 0.9 %copy-done.19 = f32[128,512]{1,0:T(8,128)S(1)} copy-done((f32[128,512]{1,0:T(8,128)S(1)}, f32[128,512]{1,0:T(8,128)}, u32[]{:S(2)}) %copy-start.19) | copy-done | bytes 262168
  58.9 2.5 %combine.1 = f32[128,512]{1,0:T(8,128)} custom-call(f32[128,128]{1,0:T(8,128)} %bitcast.2.mom_in, f32[128,512]{1,0:T(8,128)S(1)} %copy-done.15, f32[128,512]{1,0:T(8,128)S(1)} %copy-done.17, f32[128,512]{1,0:T(8,128)S(1)} %copy-done.19), custom_call_target="tpu_custom_call" | custom-call | tf_op jit(solution)/shard_map/combine/pallas_call | solution.py:499
  (35 shorter events, 2.4 us)
Async XLA Ops:
  0.6 1.6 %copy-start = (f32[8,128,512]{2,1,0:T(8,128)S(1)}, f32[8,128,512]{2,1,0:T(8,128)}, u32[]{:S(2)}) copy-start(f32[8,128,512]{2,1,0:T(8,128)} %g.5) | copy-start | bytes 6291460
  2.2 1.6 %copy-start.2 = (f32[8,128,512]{2,1,0:T(8,128)S(1)}, f32[8,128,512]{2,1,0:T(8,128)}, u32[]{:S(2)}) copy-start(f32[8,128,512]{2,1,0:T(8,128)} %c.3) | copy-start | bytes 6291460
  3.8 0.9 %copy-start.3 = (s32[128,512]{1,0:T(8,128)S(1)}, s32[128,512]{1,0:T(8,128)}, u32[]{:S(2)}) copy-start(s32[128,512]{1,0:T(8,128)} %land.5) | copy-start | bytes 786436
  4.8 0.9 %copy-start.5 = (s32[128,512]{1,0:T(8,128)S(1)}, s32[128,512]{1,0:T(8,128)}, u32[]{:S(2)}) copy-start(s32[128,512]{1,0:T(8,128)} %bottom.5) | copy-start | bytes 786436
  5.7 0.9 %copy-start.8 = (f32[128,512]{1,0:T(8,128)S(1)}, f32[128,512]{1,0:T(8,128)}, u32[]{:S(2)}) copy-start(f32[128,512]{1,0:T(8,128)} %v.3) | copy-start | bytes 786436
  6.7 0.9 %copy-start.10 = (f32[128,512]{1,0:T(8,128)S(1)}, f32[128,512]{1,0:T(8,128)}, u32[]{:S(2)}) copy-start(f32[128,512]{1,0:T(8,128)} %surf.3) | copy-start | bytes 786436
  7.6 0.9 %copy-start.11 = (f32[128,512]{1,0:T(8,128)S(1)}, f32[128,512]{1,0:T(8,128)}, u32[]{:S(2)}) copy-start(f32[128,512]{1,0:T(8,128)} %diag.3) | copy-start | bytes 786436
  8.6 3.4 %copy-start.7 = (f32[128,512]{1,0:T(8,128)S(1)}, f32[128,512]{1,0:T(8,128)}, u32[]{:S(2)}) copy-start(f32[128,512]{1,0:T(8,128)} %u.3) | copy-start | bytes 786436
  9.1 10.4 %collective-permute-start = (f32[80,512]{1,0:T(8,128)S(1)}, f32[80,512]{1,0:T(8,128)S(1)}, u32[]{:S(2)}, u32[]{:S(2)}) collective-permute-start(f32[80,512]{1,0:T(8,128)S(1)} %get-tuple-element.18.sent_a), channel_id=1, source_target_pairs={{0,16},{16,0},{32,48},{48,32},{64,80},{80,64},{96,112},{112,96},{1... | collective-permute-start | bytes 491528 | tf_op jit(solution)/shard_map/ppermute | solution.py:33
  11.3 8.2 %collective-permute-start.1 = (f32[80,512]{1,0:T(8,128)S(1)}, f32[80,512]{1,0:T(8,128)S(1)}, u32[]{:S(2)}, u32[]{:S(2)}) collective-permute-start(f32[80,512]{1,0:T(8,128)S(1)} %get-tuple-element.19.sent_b), channel_id=1, source_target_pairs={{16,32},{32,16},{48,64},{64,48},{80,96},{96,80},{17,33},{33,17},{4... | collective-permute-start | bytes 491528 | tf_op jit(solution)/shard_map/ppermute | solution.py:33
  19.4 27.1 %copy-start.1 = (f32[8,128,512]{2,1,0:T(8,128)S(1)}, f32[8,128,512]{2,1,0:T(8,128)}, u32[]{:S(2)}) copy-start(f32[8,128,512]{2,1,0:T(8,128)} %g.5) | copy-start | bytes 6291460
  19.4 27.1 %copy-start.4 = (s32[128,512]{1,0:T(8,128)S(1)}, s32[128,512]{1,0:T(8,128)}, u32[]{:S(2)}) copy-start(s32[128,512]{1,0:T(8,128)} %land.5) | copy-start | bytes 786436
  19.4 27.1 %copy-start.6 = (s32[128,512]{1,0:T(8,128)S(1)}, s32[128,512]{1,0:T(8,128)}, u32[]{:S(2)}) copy-start(s32[128,512]{1,0:T(8,128)} %bottom.5) | copy-start | bytes 786436
  19.4 27.1 %copy-start.9 = (f32[128,512]{1,0:T(8,128)S(1)}, f32[128,512]{1,0:T(8,128)}, u32[]{:S(2)}) copy-start(f32[128,512]{1,0:T(8,128)} %v.3) | copy-start | bytes 786436
  19.8 6.1 %collective-permute-start.2 = (f32[136,128]{1,0:T(8,128)S(1)}, f32[136,128]{1,0:T(8,128)S(1)}, u32[]{:S(2)}, u32[]{:S(2)}) collective-permute-start(f32[136,128]{1,0:T(8,128)S(1)} %get-tuple-element.22.sent_a), channel_id=1, source_target_pairs={{0,1},{1,0},{2,3},{3,2},{4,5},{5,4},{6,7},{7,6},{8,9},{9,8},{10,11... | collective-permute-start | bytes 208904 | tf_op jit(solution)/shard_map/ppermute | solution.py:33
  20.8 7.1 %collective-permute-start.3 = (f32[136,128]{1,0:T(8,128)S(1)}, f32[136,128]{1,0:T(8,128)S(1)}, u32[]{:S(2)}, u32[]{:S(2)}) collective-permute-start(f32[136,128]{1,0:T(8,128)S(1)} %get-tuple-element.23.sent_b), channel_id=1, source_target_pairs={{1,2},{2,1},{3,4},{4,3},{5,6},{6,5},{7,8},{8,7},{9,10},{10,9},{11,... | collective-permute-start | bytes 208904 | tf_op jit(solution)/shard_map/ppermute | solution.py:33
  27.9 2.2 %copy-start.12 = (f32[136,128]{1,0:T(8,128)}, f32[136,128]{1,0:T(8,128)S(1)}, u32[]{:S(2)}) copy-start(f32[136,128]{1,0:T(8,128)S(1)} %collective-permute-done.3.cf.far) | copy-start | bytes 208900
  30.2 0.7 %copy-start.14 = (f32[128,512]{1,0:T(8,128)}, f32[128,512]{1,0:T(8,128)S(1)}, u32[]{:S(2)}) copy-start(f32[128,512]{1,0:T(8,128)S(1)} %get-tuple-element.31.r_in) | copy-start | bytes 786436
  31.6 0.7 %copy-start.18 = (f32[128,512]{1,0:T(8,128)}, f32[128,512]{1,0:T(8,128)S(1)}, u32[]{:S(2)}) copy-start(f32[128,512]{1,0:T(8,128)S(1)} %get-tuple-element.33.p2_in) | copy-start | bytes 786436
  32.9 23.1 %all-to-all-start = ((f32[128,1,128]{2,1,0:T(1,128)}), f32[128,1,128]{2,1,0:T(1,128)}, u32[]{:S(2)}, u32[]{:S(2)}) async-start(f32[128,1,128]{2,1,0:T(1,128)} %bitcast.4), calls=%async_computation | async-start | bytes 131072 | tf_op jit(solution)/shard_map/all_to_all | solution.py:491
  46.6 0.9 %copy-start.13 = (f32[136,128]{1,0:T(8,128)S(1)}, f32[136,128]{1,0:T(8,128)}, u32[]{:S(2)}) copy-start(f32[136,128]{1,0:T(8,128)} %copy-done.12) | copy-start | bytes 208900
  56.1 1.0 %copy-start.15 = (f32[128,512]{1,0:T(8,128)S(1)}, f32[128,512]{1,0:T(8,128)}, u32[]{:S(2)}) copy-start(f32[128,512]{1,0:T(8,128)} %copy-done.14) | copy-start | bytes 786436
  57.0 0.9 %copy-start.17 = (f32[128,512]{1,0:T(8,128)S(1)}, f32[128,512]{1,0:T(8,128)}, u32[]{:S(2)}) copy-start(f32[128,512]{1,0:T(8,128)} %copy-done.16) | copy-start | bytes 786436
  58.0 0.9 %copy-start.19 = (f32[128,512]{1,0:T(8,128)S(1)}, f32[128,512]{1,0:T(8,128)}, u32[]{:S(2)}) copy-start(f32[128,512]{1,0:T(8,128)} %copy-done.18) | copy-start | bytes 786436
  (2 other events, 1.3 us)

commit v3 on v2

--- a/solution.py
+++ b/solution.py
@@ -114,64 +114,42 @@
     return out
 
 
-def local(g, c, land, bottom, surf, diag, u, s_ref, code_ref, diag_ref, a_ref, b_ref, gv, cv, lv, bv, sv, uv, sems, band_sems):
+def local(g, c, land, bottom, surf, diag, u, s_ref, code_ref, diag_ref, a_ref, b_ref, gv, cv, lv, bv, sv, uv, sems, deep_sems):
     rows, cols = surf.shape
-    bands = band_sems.shape[0]
-    tall = rows // bands
     flat = [
         pltpu.make_async_copy(src, dst, sems.at[n])
         for n, (src, dst) in enumerate(((land, lv), (bottom, bv), (surf, sv), (diag, diag_ref), (u, uv)))
     ]
-    deep = []
-    for b in range(bands):
-        at = slice(b * tall, (b + 1) * tall)
-        for n, (src, dst) in enumerate(((g, gv), (c, cv))):
-            deep.append(pltpu.make_async_copy(src.at[:, at, :], dst.at[:, at, :], band_sems.at[b, n]))
-    start_all(flat[:2] + deep[:2] + flat[2:] + deep[2:])
-    wait_all(flat)
-    code_ref[...] = code_of(lv[...], bv[...])
-    even = is_even("col")
-    lane, sub = iota((8, cols), 1), iota((8, cols), 0)
-    vb_before = jnp.zeros((8, cols), F32)
-    for i in range(rows // 8):
-        at = slice(8 * i, 8 * i + 8)
-        after = slice(8 * i + 8, 8 * i + 16)
-        is_last = i == rows // 8 - 1
-        if i == 0:
-            wait_all(deep[:2])
-        if (8 * i + 8) % tall == 0 and not is_last:
-            b = (8 * i + 8) // tall
-            wait_all(deep[2 * b : 2 * b + 2])
-
-        def down(here, there):
-            return turn(jnp.where(sub == 0, there, here), -1, 0)
-
-        code = code_ref[at, :]
-        cu = jnp.where(lane < cols - 1, jnp.minimum(code, next_col(code)), 0.0)
-        if is_last:
-            co = jnp.where(sub < 7, jnp.minimum(code, next_row(code)), 0.0)
-        else:
-            co = jnp.minimum(code, down(code, code_ref[after, :]))
-        ub = jnp.zeros((8, cols), F32)
-        vb = jnp.zeros((8, cols), F32)
-        gs, cs = [], []
-        for k in range(LEV):
-            gk, ck = gv[k, at, :], cv[k, at, :]
-            gs.append(gk)
-            cs.append(ck)
-            gn = next_row(gk) if is_last else down(gk, gv[k, after, :])
-            cn = next_row(ck) if is_last else down(ck, cv[k, after, :])
-            ub = ub + jnp.where(cu > k + 0.5, next_col(gk) - gk, 0.0) * (next_col(ck) + ck)
-            vb = vb + jnp.where(co > k + 0.5, gn - gk, 0.0) * (cn + ck)
-        vb_prev = turn(jnp.where(sub == 7, vb_before, vb), 1, 0)
-        vb_before = vb
-        s_ref[at, :] = sv[at, :] + 0.0625 * ((ub - prev_col(ub)) + (vb - vb_prev))
-        rest = (sv[at, :], diag_ref[at, :], uv[at, :])
-        packs = []
-        for of_last, lanes in ((True, slice(cols - 128, cols)), (False, slice(0, 128))):
-            cut = lambda xs: [x[:, lanes] for x in xs]
-            packs.append(lane_pack(cut(gs), cut(cs), code[:, lanes], cut(rest), of_last))
-        a_ref[at, :], b_ref[at, :] = pick(even, *packs)
+    deep = [
+        pltpu.make_async_copy(src.at[k], dst.at[k], deep_sems.at[k, n])
+        for k in range(LEV)
+        for n, (src, dst) in enumerate(((g, gv), (c, cv)))
+    ]
+    start_all(flat[:2] + deep + flat[2:])
+    wait_all(flat[:2])
+    code = code_of(lv[...], bv[...])
+    code_ref[...] = code
+    cu = jnp.where(iota(code.shape, 1) < cols - 1, jnp.minimum(code, next_col(code)), 0.0)
+    co = jnp.where(iota(code.shape, 0) < rows - 1, jnp.minimum(code, next_row(code)), 0.0)
+    ub, vb = jnp.zeros_like(cu), jnp.zeros_like(co)
+    for k in range(LEV):
+        wait_all(deep[2 * k : 2 * k + 2])
+        gk, ck = gv[k], cv[k]
+        ub = ub + jnp.where(cu > k + 0.5, next_col(gk) - gk, 0.0) * (next_col(ck) + ck)
+        vb = vb + jnp.where(co > k + 0.5, next_row(gk) - gk, 0.0) * (next_row(ck) + ck)
+    wait_all(flat[2:])
+    s_ref[...] = sv[...] + 0.0625 * ((ub - prev_col(ub)) + (vb - prev_row(vb)))
+    packs = [
+        lane_pack(
+            [gv[k, :, lanes] for k in range(LEV)],
+            [cv[k, :, lanes] for k in range(LEV)],
+            code_ref[:, lanes],
+            [x[:, lanes] for x in (sv, diag_ref, uv)],
+            of_last,
+        )
+        for of_last, lanes in ((True, slice(cols - 128, cols)), (False, slice(0, 128)))
+    ]
+    a_ref[...], b_ref[...] = pick(is_even("col"), *packs)
 
 
 def row_halo(near, far, lanes):
@@ -256,8 +234,8 @@
     return plane
 
 
-def krylov(s, code, diag, sent_a, sent_b, near, far, r_ref, p1_ref, p2_ref, mom_ref, r_v, p1_v, p2_v, sems):
-    rows, cols = r_v.shape
+def krylov(s, code, diag, sent_a, sent_b, near, far, r_ref, p1_ref, p2_ref, mom_ref):
+    rows, cols = r_ref.shape
     even = is_even("col")
     high, low = pick(even, sent_a[...], sent_b[...])
     east, west = pick(even, near[...], far[...])
@@ -299,21 +277,14 @@
         fu, fv = cu * (v - next_col(v)), cv * (v - next_row(v))
         return (dg - SHIFT) * v + ((fu - prev_col(fu)) + (fv - prev_row(fv)))
 
-    copies = []
-
-    def send(x, own, out):
-        own[...] = x[:rows, :cols]
-        copies.append(pltpu.make_async_copy(own, out, sems.at[len(copies)]))
-        copies[-1].start()
-
-    send(r, r_v, r_ref)
     p1 = shifted(r)
-    send(p1, p1_v, p1_ref)
     p2 = shifted(p1)
-    send(p2, p2_v, p2_ref)
     eu, ev = p2 - next_col(p2), p2 - next_row(p2)
     energy = dg * p2 * p2 + (cu * eu * eu + cv * ev * ev)
     r, p1, p2, energy = [a[:rows, :cols] for a in (r, p1, p2, energy)]
+    r_ref[...] = r
+    p1_ref[...] = p1
+    p2_ref[...] = p2
     lane = iota((8, 128), 1)
     packed = jnp.zeros((8, 128), F32)
     for m, prod in enumerate((r * r, r * p1, p1 * p1, p1 * p2, p2 * p2, energy)):
@@ -332,10 +303,17 @@
         packed = jnp.where(lane // 16 == m, part, packed)
     for i in range(mom_ref.shape[0] // 8):
         mom_ref[8 * i : 8 * i + 8, :] = packed
-    wait_all(copies)
-
-
-def tracer_kernel(g, land, bottom, u, v, rn, rf, cn, cf, out_ref):
+
+
+def tracer_kernel(g_in, land_in, bottom_in, u_in, v_in, rn, rf, cn, cf, out_ref, g, land, bottom, u, v, out, sems, g_sems, out_sems):
+    flat = [
+        pltpu.make_async_copy(src, dst, sems.at[n])
+        for n, (src, dst) in enumerate(((land_in, land), (bottom_in, bottom), (u_in, u), (v_in, v)))
+    ]
+    deep = [pltpu.make_async_copy(g_in.at[k], g.at[k], g_sems.at[k]) for k in range(LEV)]
+    done = [pltpu.make_async_copy(out.at[k], out_ref.at[k], out_sems.at[k]) for k in range(LEV)]
+    start_all(flat + deep)
+    wait_all(flat)
     rows, cols = u.shape
     rh, ch = row_halo(rn, rf, slice(0, cols)), col_halo(cn, cf)
 
@@ -347,11 +325,14 @@
     uw = 0.125 * wide(u[...], SPEED, 84)
     vw = 0.125 * wide(v[...], SPEED, 84)
     for k in range(LEV):
+        deep[k].wait()
         gk = wide(g[k], 2 * k, 8 * k)
         pu = jnp.where(cu > k + 0.5, next_col(gk) - gk, 0.0) * uw
         pv = jnp.where(cv > k + 0.5, next_row(gk) - gk, 0.0) * vw
         total = gk + pu + prev_col(pu) + pv + prev_row(pv)
-        out_ref[k] = total[:rows, :cols]
+        out[k] = total[:rows, :cols]
+        done[k].start()
+    wait_all(done)
 
 
 def two_sum(a, b):
@@ -393,13 +374,10 @@
     return quick(q, rest[0] / y[0])
 
 
-def combine(mom_in, r_in, p1_in, p2_in, x_ref, mom, r, p1, p2, sems):
-    copies = [
-        pltpu.make_async_copy(src, dst, sems.at[n])
-        for n, (src, dst) in enumerate(((mom_in, mom), (r_in, r), (p1_in, p1), (p2_in, p2)))
-    ]
-    start_all(copies)
-    copies[0].wait()
+def combine(mom_in, r, p1, p2, x_ref, mom, x, sems):
+    load = pltpu.make_async_copy(mom_in, mom, sems.at[0])
+    load.start()
+    load.wait()
     zero = jnp.zeros((8, 128), F32)
     tiles = [(mom[8 * i : 8 * i + 8, :], zero) for i in range(mom.shape[0] // 8)]
     while len(tiles) > 1:
@@ -433,25 +411,33 @@
     y2 = z2
     y1 = add(z1, neg(mul(l21, y2)))
     y0 = add(div(b0, a00), neg(add(mul(l10, y1), mul(l20, y2))))
-    wait_all(copies[1:])
     rows, cols = r.shape
-    for i in range(rows // 8):
-        for j in range(cols // 128):
-            at = (slice(8 * i, 8 * i + 8), slice(128 * j, 128 * j + 128))
-            x_ref[at] = y0[0] * r[at] + (y1[0] * p1[at] + y2[0] * p2[at])
+    bands = sems.shape[0] - 1
+    tall = rows // bands
+    done = []
+    for b in range(bands):
+        band = slice(b * tall, (b + 1) * tall)
+        for i in range(b * tall // 8, (b + 1) * tall // 8):
+            for j in range(cols // 128):
+                at = (slice(8 * i, 8 * i + 8), slice(128 * j, 128 * j + 128))
+                x[at] = y0[0] * r[at] + (y1[0] * p1[at] + y2[0] * p2[at])
+        done.append(pltpu.make_async_copy(x.at[band, :], x_ref.at[band, :], sems.at[1 + b]))
+        done[-1].start()
+    wait_all(done)
 
 
 def call(kernel, ins, outs, scratch=(), name=None, cost=None):
-    return pl.pallas_call(
+    run = pl.pallas_call(
         kernel,
         in_specs=list(ins),
         out_specs=[spec for spec, _ in outs],
-        out_shape=[jax.ShapeDtypeStruct(shape, F32) for _, shape in outs],
+        out_shape=[spec.memory_space(shape, F32) for spec, shape in outs],
         scratch_shapes=list(scratch),
         compiler_params=PARAMS,
         cost_estimate=cost,
         name=name,
     )
+    return lambda *args: run(*[pltpu.with_memory_space_constraint(x, spec.memory_space) for x, spec in zip(args, ins)])
 
 
 def shards(tracer_adj_next, tracer, u_east, v_north, surf_adj_next, diag, land, bottom):
@@ -472,7 +458,7 @@
         local,
         [HBM] * 7,
         [(VMEM, two)] * 3 + [(VMEM, (rows, 128))] * 2,
-        [deep, deep, whole(jnp.int32), whole(jnp.int32), whole(), whole(), dma((5,)), dma((4, 2))],
+        [deep, deep, whole(jnp.int32), whole(jnp.int32), whole(), whole(), dma((5,)), dma((levels, 2))],
         name="local",
         cost=pl.CostEstimate(flops=24 * g.size, bytes_accessed=8 * g.size, transcendentals=0),
     )(g, c, land, bottom, surf_adj_next, diag, u_east)
@@ -484,23 +470,23 @@
     r, p1, p2, mom = call(
         krylov,
         [VMEM] * 7,
-        [(HBM, two)] * 3 + [(VMEM, (size, 128))],
-        [whole(), whole(), whole(), dma((3,))],
+        [(VMEM, two)] * 3 + [(VMEM, (size, 128))],
         name="krylov",
     )(s, code, dg, *col_sent, *col_got)
     mom = lax.all_to_all(mom, ("row", "col"), 0, 0, tiled=True)
     (tracer_adj,) = call(
         tracer_kernel,
-        [VMEM] * 9,
-        [(VMEM, g.shape)],
+        [HBM] * 5 + [VMEM] * 4,
+        [(HBM, g.shape)],
+        [deep, whole(jnp.int32), whole(jnp.int32), whole(), whole(), deep, dma((4,)), dma((levels,)), dma((levels,))],
         name="tracer",
         cost=pl.CostEstimate(flops=20 * g.size, bytes_accessed=12 * g.size, transcendentals=0),
     )(g, land, bottom, u_east, v_north, *row_got, *col_got)
     (surf_adj,) = call(
         combine,
-        [HBM] * 4,
-        [(VMEM, two)],
-        [pltpu.VMEM((size, 128), F32), whole(), whole(), whole(), dma((4,))],
+        [HBM] + [VMEM] * 3,
+        [(HBM, two)],
+        [pltpu.VMEM((size, 128), F32), whole(), dma((5,))],
         name="combine",
     )(mom, r, p1, p2)
     return tracer_adj, surf_adj

time: 61.9 us -> 47.9 us (0.77)
  local copies, waits for them, and re-layouts: 14.4 us -> 0.62 us
  Pallas kernels: 16.9 us -> 17.8 us
    unnamed x42 -> x2, local copies, waits for them, and re-layouts: 14.4 us -> 0.62 us
    pallas_call x7, Pallas kernels: 16.9 us -> 17.8 us  [call(): run(*[pltpu.with_memory_space_constraint(x, spec.memory_space) for x, spe...]
    all_to_all x1, waiting for transfers between devices: 4.98 us -> 4.15 us  [shards(): mom = lax.all_to_all(mom, ('row', 'col'), 0, 0, tiled=True)]
  transfers between devices with their start and end apart: 5 -> 5, of which waited for: 2 -> 2; matrix products, arithmetic and copies ran while one was open for 0% -> 0% of each run, Pallas kernels for 19% -> 23%
where the time goes in v3:
time: 47.9 us; the launch traced here: 47.6 us
  starting transfers between devices  22 us (46%)
  Pallas kernels  17.8 us (37%)
  waiting for transfers between devices  6.47 us (14%)
  between operations  0.72 us (2%)
  local copies, waits for them, and re-layouts  0.62 us (1%)
    pallas_call x7, Pallas kernels, call(): run(*[pltpu.with_memory_space_constraint(x, spec.memory_space) for x, spe...  17.8 us
    all_to_all x1, starting transfers between devices, shards(): mom = lax.all_to_all(mom, ('row', 'col'), 0, 0, tiled=True)  13.5 us
    ppermute x4, starting transfers between devices, swap(): lax.ppermute(b, axis, swap_pairs(axis, first))  8.45 us
    all_to_all x1, waiting for transfers between devices, shards(): mom = lax.all_to_all(mom, ('row', 'col'), 0, 0, tiled=True)  4.15 us
    ppermute x4, waiting for transfers between devices, swap(): lax.ppermute(b, axis, swap_pairs(axis, first))  2.33 us
  transfers between devices with their start and end apart: 5, of which 2 were waited for; matrix products, arithmetic and copies ran while one was open for 0% of the time, Pallas kernels for 23%

profile of v3, /device:TPU:1, one launch (start us, length us, event | category | flops | bytes accessed | tf_op | source)
XLA Modules:
  0.0 47.6 jit_solution(10238193296164161232)
XLA Ops:
  0.6 1.3 %pack_rows.1 = (f32[80,512]{1,0:T(8,128)S(1)}, f32[80,512]{1,0:T(8,128)S(1)}) custom-call(f32[8,128,512]{2,1,0:T(8,128)} %g_in.1, f32[8,128,512]{2,1,0:T(8,128)} %c.3, s32[128,512]{1,0:T(8,128)} %land_in.1, s32[128,512]{1,0:T(8,128)} %bottom_in.1, f32[128,512]{1,0:T(8,128)} %surf.3, f32[128,512]{1,0:T(8,128)} %diag.3, f32[128,512]{1,0:T(8,128)} %v_in.1), custom_call_target="tpu_custom_call" | custom-call | tf_op jit(solution)/shard_map/pack_rows/pallas_call | solution.py:440
  1.9 2.2 %collective-permute-start = (f32[80,512]{1,0:T(8,128)S(1)}, f32[80,512]{1,0:T(8,128)S(1)}, u32[]{:S(2)}, u32[]{:S(2)}) collective-permute-start(f32[80,512]{1,0:T(8,128)S(1)} %get-tuple-element.18.sent_a), channel_id=1, source_target_pairs={{0,16},{16,0},{32,48},{48,32},{64,80},{80,64},{96,112},{112,96},{1... | collective-permute-start | bytes 491528 | tf_op jit(solution)/shard_map/ppermute | solution.py:33
  4.1 0.7 %collective-permute-start.1 = (f32[80,512]{1,0:T(8,128)S(1)}, f32[80,512]{1,0:T(8,128)S(1)}, u32[]{:S(2)}, u32[]{:S(2)}) collective-permute-start(f32[80,512]{1,0:T(8,128)S(1)} %get-tuple-element.19.sent_b), channel_id=1, source_target_pairs={{16,32},{32,16},{48,64},{64,48},{80,96},{96,80},{17,33},{33,17},{4... | collective-permute-start | bytes 491528 | tf_op jit(solution)/shard_map/ppermute | solution.py:33
  4.8 5.4 %local.1 = (f32[128,512]{1,0:T(8,128)S(1)}, f32[128,512]{1,0:T(8,128)S(1)}, f32[128,512]{1,0:T(8,128)S(1)}, f32[128,128]{1,0:T(8,128)S(1)}, f32[128,128]{1,0:T(8,128)S(1)}) custom-call(f32[8,128,512]{2,1,0:T(8,128)} %g_in.1, f32[8,128,512]{2,1,0:T(8,128)} %c.3, s32[128,512]{1,0:T(8,128)} %land_in.1, s32[128,512]{1,0:T(8,128)} %bottom_in.1, f32[128,512]{1,0:T(8,128)} %surf.3, ...), custom_call_target="tpu_custom_call" | custom-call | flops 12582912 | bytes 4194304 | tf_op jit(solution)/shard_map/local/pallas_call | solution.py:440
  10.2 0.0 collective-permute-done.near.rn
  10.2 0.0 collective-permute-done.1.far.rf
  10.2 0.3 join_cols.1
  10.5 1.0 %collective-permute-start.2 = (f32[136,128]{1,0:T(8,128)S(1)}, f32[136,128]{1,0:T(8,128)S(1)}, u32[]{:S(2)}, u32[]{:S(2)}) collective-permute-start(f32[136,128]{1,0:T(8,128)S(1)} %get-tuple-element.22.sent_a), channel_id=1, source_target_pairs={{0,1},{1,0},{2,3},{3,2},{4,5},{5,4},{6,7},{7,6},{8,9},{9,8},{10,11... | collective-permute-start | bytes 208904 | tf_op jit(solution)/shard_map/ppermute | solution.py:33
  11.5 4.6 %collective-permute-start.3 = (f32[136,128]{1,0:T(8,128)S(1)}, f32[136,128]{1,0:T(8,128)S(1)}, u32[]{:S(2)}, u32[]{:S(2)}) collective-permute-start(f32[136,128]{1,0:T(8,128)S(1)} %get-tuple-element.23.sent_b), channel_id=1, source_target_pairs={{1,2},{2,1},{3,4},{4,3},{5,6},{6,5},{7,8},{8,7},{9,10},{10,9},{11,... | collective-permute-start | bytes 208904 | tf_op jit(solution)/shard_map/ppermute | solution.py:33
  16.1 0.3 halo_rows.1
  16.4 0.0 collective-permute-done.2.cn.near
  16.4 2.3 %collective-permute-done.3.cf.far = f32[136,128]{1,0:T(8,128)S(1)} collective-permute-done((f32[136,128]{1,0:T(8,128)S(1)}, f32[136,128]{1,0:T(8,128)S(1)}, u32[]{:S(2)}, u32[]{:S(2)}) %collective-permute-start.3) | collective-permute-done | bytes 69664 | tf_op jit(solution)/shard_map/ppermute | solution.py:33
  18.8 2.7 %krylov.1 = (f32[128,512]{1,0:T(8,128)S(1)}, f32[128,512]{1,0:T(8,128)S(1)}, f32[128,512]{1,0:T(8,128)S(1)}, f32[128,128]{1,0:T(8,128)}) custom-call(f32[136,512]{1,0:T(8,128)S(1)} %get-tuple-element.27.s, f32[136,512]{1,0:T(8,128)S(1)} %get-tuple-element.28.code, f32[136,512]{1,0:T(8,128)S(1)} %get-tuple-element.29.diag, ...), custom_call_target="tpu_custom_call" | custom-call | tf_op jit(solution)/shard_map/krylov/pallas_call | solution.py:440
  21.5 13.5 %all-to-all-start = ((f32[128,1,128]{2,1,0:T(1,128)}), f32[128,1,128]{2,1,0:T(1,128)S(1)}, u32[]{:S(2)}, u32[]{:S(2)}) async-start(f32[128,1,128]{2,1,0:T(1,128)} %bitcast.1), calls=%async_computation | async-start | bytes 131072 | tf_op jit(solution)/shard_map/all_to_all | solution.py:476
  35.0 5.4 %tracer.1 = f32[8,128,512]{2,1,0:T(8,128)} custom-call(f32[8,128,512]{2,1,0:T(8,128)} %g_in.1, s32[128,512]{1,0:T(8,128)} %land_in.1, s32[128,512]{1,0:T(8,128)} %bottom_in.1, f32[128,512]{1,0:T(8,128)} %u_in.1, f32[128,512]{1,0:T(8,128)} %v_in.1, f32[80,512]{1,0:T(8,128)S(1)} %collective-permute-done.near.rn, f32[80,512]{1,0:T(8,128)S(1)} %collective-permute-done.1.far.rf, ...), custom_call_target="tpu_custom_call" | custom-call | flops 10485760 | bytes 6291456 | tf_op jit(solution)/shard_map/tracer/pallas_call | solution.py:440
  40.5 4.1 %all-to-all-done = f32[128,1,128]{2,1,0:T(1,128)S(1)} async-done(((f32[128,1,128]{2,1,0:T(1,128)}), f32[128,1,128]{2,1,0:T(1,128)S(1)}, u32[]{:S(2)}, u32[]{:S(2)}) %all-to-all-start) | async-done | bytes 65568 | tf_op jit(solution)/shard_map/all_to_all | solution.py:476
  44.6 0.0 copy-start
  44.6 0.6 %copy-done = f32[128,1,128]{2,1,0:T(1,128)} copy-done((f32[128,1,128]{2,1,0:T(1,128)}, f32[128,1,128]{2,1,0:T(1,128)S(1)}, u32[]{:S(2)}) %copy-start) | copy-done | bytes 65560
  45.2 2.4 %combine.1 = f32[128,512]{1,0:T(8,128)} custom-call(f32[128,128]{1,0:T(8,128)} %bitcast.4, f32[128,512]{1,0:T(8,128)S(1)} %get-tuple-element.31.r, f32[128,512]{1,0:T(8,128)S(1)} %get-tuple-element.32.p1, f32[128,512]{1,0:T(8,128)S(1)} %get-tuple-element.33.p2), custom_call_target="tpu_custom_call" | custom-call | tf_op jit(solution)/shard_map/combine/pallas_call | solution.py:440
Async XLA Ops:
  1.9 8.3 %collective-permute-start = (f32[80,512]{1,0:T(8,128)S(1)}, f32[80,512]{1,0:T(8,128)S(1)}, u32[]{:S(2)}, u32[]{:S(2)}) collective-permute-start(f32[80,512]{1,0:T(8,128)S(1)} %get-tuple-element.18.sent_a), channel_id=1, source_target_pairs={{0,16},{16,0},{32,48},{48,32},{64,80},{80,64},{96,112},{112,96},{1... | collective-permute-start | bytes 491528 | tf_op jit(solution)/shard_map/ppermute | solution.py:33
  4.1 6.1 %collective-permute-start.1 = (f32[80,512]{1,0:T(8,128)S(1)}, f32[80,512]{1,0:T(8,128)S(1)}, u32[]{:S(2)}, u32[]{:S(2)}) collective-permute-start(f32[80,512]{1,0:T(8,128)S(1)} %get-tuple-element.19.sent_b), channel_id=1, source_target_pairs={{16,32},{32,16},{48,64},{64,48},{80,96},{96,80},{17,33},{33,17},{4... | collective-permute-start | bytes 491528 | tf_op jit(solution)/shard_map/ppermute | solution.py:33
  10.5 5.9 %collective-permute-start.2 = (f32[136,128]{1,0:T(8,128)S(1)}, f32[136,128]{1,0:T(8,128)S(1)}, u32[]{:S(2)}, u32[]{:S(2)}) collective-permute-start(f32[136,128]{1,0:T(8,128)S(1)} %get-tuple-element.22.sent_a), channel_id=1, source_target_pairs={{0,1},{1,0},{2,3},{3,2},{4,5},{5,4},{6,7},{7,6},{8,9},{9,8},{10,11... | collective-permute-start | bytes 208904 | tf_op jit(solution)/shard_map/ppermute | solution.py:33
  11.5 7.2 %collective-permute-start.3 = (f32[136,128]{1,0:T(8,128)S(1)}, f32[136,128]{1,0:T(8,128)S(1)}, u32[]{:S(2)}, u32[]{:S(2)}) collective-permute-start(f32[136,128]{1,0:T(8,128)S(1)} %get-tuple-element.23.sent_b), channel_id=1, source_target_pairs={{1,2},{2,1},{3,4},{4,3},{5,6},{6,5},{7,8},{8,7},{9,10},{10,9},{11,... | collective-permute-start | bytes 208904 | tf_op jit(solution)/shard_map/ppermute | solution.py:33
  21.5 23.1 %all-to-all-start = ((f32[128,1,128]{2,1,0:T(1,128)}), f32[128,1,128]{2,1,0:T(1,128)S(1)}, u32[]{:S(2)}, u32[]{:S(2)}) async-start(f32[128,1,128]{2,1,0:T(1,128)} %bitcast.1), calls=%async_computation | async-start | bytes 131072 | tf_op jit(solution)/shard_map/all_to_all | solution.py:476
  44.6 0.6 %copy-start = (f32[128,1,128]{2,1,0:T(1,128)}, f32[128,1,128]{2,1,0:T(1,128)S(1)}, u32[]{:S(2)}) copy-start(f32[128,1,128]{2,1,0:T(1,128)S(1)} %all-to-all-done) | copy-start | bytes 196612

commit v4 on v3

--- a/solution.py
+++ b/solution.py
@@ -14,7 +14,7 @@
 PARAMS = pltpu.CompilerParams(vmem_limit_bytes=32 * 1024 * 1024)
 
 
-CODE, SURF, DIAG, SPEED = 16, 17, 18, 19
+G, C, RHS, CODE, DIAG = 0, 1, 4, 5, 6
 
 
 def code_of(land, bottom):
@@ -86,18 +86,50 @@
     start_all(copies)
     wait_all(copies)
 
-    def planes(g, c, land, bottom, surf, diag, v):
-        pairs = [x for k in range(LEV) for x in (g[k], c[k])]
-        return pairs + [code_of(land[...], bottom[...]), surf[...], diag[...], v[...]]
-
-    first = planes(g0, c0, l0, b0, s0, d0, v0)
-    last = planes(g1, c1, l1, b1, s1, d1, v1)
-    upper = iota(first[0].shape, 0) < DEEP
+    cols = surf.shape[1]
+    lane, sub = iota((8, cols), 1), iota((8, cols), 0)
+    upper = sub < DEEP
+
+    def tiles(g, c, land, bottom, surf, diag, v, of_last):
+        code = code_of(land[...], bottom[...])
+        g, c = [g[k] for k in range(LEV)], [c[k] for k in range(LEV)]
+        cu = jnp.where(lane < cols - 1, jnp.minimum(code, next_col(code)), 0.0)
+        cv = jnp.where(sub < 7, jnp.minimum(code, next_row(code)), 0.0)
+        ub, vb = faces(g, c, cu, cv)
+        rhs = surf[...] + 0.0625 * ((ub - prev_col(ub)) + (vb - prev_row(vb)))
+        edge = 7 if of_last else 0
+
+        def outermost(x):
+            out = turn(x[0], -edge, 0)
+            for k in range(1, LEV):
+                out = jnp.where(sub == k, turn(x[k], k - edge, 0), out)
+            return out
+
+        half = DEEP if of_last else 0
+        one = jnp.where(upper, turn(rhs, half, 0), turn(code, DEEP - half, 0))
+        two = jnp.where(upper, turn(diag[...], half, 0), turn(v[...], DEEP - edge, 0))
+        ends = []
+        for high, lanes in ((False, slice(0, 128)), (True, slice(cols - 128, cols))):
+            cut = lambda xs: [x[:, lanes] for x in xs]
+            corner = lane_pack(cut(g), cut(c), code[:, lanes], cut([surf, diag]), high)
+            ends.append(jnp.where(sub[:, :128] < 5, two[:, lanes], corner if of_last else turn(corner, 5, 0)))
+        two = jnp.concatenate([ends[0], two[:, 128 : cols - 128], ends[1]], axis=1)
+        return outermost(g), outermost(c), one, two
+
+    first = tiles(g0, c0, l0, b0, s0, d0, v0, False)
+    last = tiles(g1, c1, l1, b1, s1, d1, v1, True)
     even = is_even("row")
-    for t in range(len(first) // 2):
-        high = jnp.where(upper, turn(last[2 * t], DEEP, 0), last[2 * t + 1])
-        low = jnp.where(upper, first[2 * t], turn(first[2 * t + 1], DEEP, 0))
-        a_ref[8 * t : 8 * t + 8, :], b_ref[8 * t : 8 * t + 8, :] = pick(even, high, low)
+    for t in range(4):
+        a_ref[8 * t : 8 * t + 8, :], b_ref[8 * t : 8 * t + 8, :] = pick(even, last[t], first[t])
+
+
+def faces(g, c, cu, cv):
+    ub, vb = jnp.zeros_like(cu), jnp.zeros_like(cv)
+    for k in range(LEV):
+        gk, ck = g[k], c[k]
+        ub = ub + jnp.where(cu > k + 0.5, next_col(gk) - gk, 0.0) * (next_col(ck) + ck)
+        vb = vb + jnp.where(cv > k + 0.5, next_row(gk) - gk, 0.0) * (next_row(ck) + ck)
+    return ub, vb
 
 
 def lane_pack(g, c, code, rest, of_last):
@@ -114,11 +146,61 @@
     return out
 
 
-def local(g, c, land, bottom, surf, diag, u, s_ref, code_ref, diag_ref, a_ref, b_ref, gv, cv, lv, bv, sv, uv, sems, deep_sems):
+def pack_cols(g, c, land, bottom, surf, diag, u, a_ref, b_ref, gv, cv, lv, bv, fv, sems):
+    cols = surf.shape[1]
+    copies = []
+    for n, (src, dst) in enumerate(((land, lv), (bottom, bv), (surf, fv), (diag, fv), (u, fv), (g, gv), (c, cv))):
+        for end, lanes in enumerate((slice(0, 128), slice(cols - 128, cols))):
+            part = src.at[:, :, lanes] if len(src.shape) == 3 else src.at[:, lanes]
+            there = dst.at[n - 2, end] if dst is fv else dst.at[end]
+            copies.append(pltpu.make_async_copy(part, there, sems.at[n, end]))
+    start_all(copies)
+    wait_all(copies)
+    low, high = [
+        lane_pack(
+            [gv[end, k] for k in range(LEV)],
+            [cv[end, k] for k in range(LEV)],
+            code_of(lv[end], bv[end]),
+            [fv[n, end] for n in range(3)],
+            end == 1,
+        )
+        for end in range(2)
+    ]
+    a_ref[...], b_ref[...] = pick(is_even("col"), high, low)
+
+
+def row_halo(near, far, lanes):
+    even = is_even("row")
+
+    def plane(p):
+        at = slice(8 * (p // 2), 8 * (p // 2) + 8)
+        north, south = pick(even, near[at, lanes], far[at, lanes])
+        upper = iota(north.shape, 0) < DEEP
+        if p % 2 == 0:
+            return jnp.where(upper, north, turn(south, DEEP, 0))
+        return jnp.where(upper, turn(north, DEEP, 0), south)
+
+    return plane
+
+
+def join_cols(a_in, b_in, near, far, a_ref, b_ref):
+    rows, width = a_in.shape[0], near.shape[1]
+    even = is_even("row")
+    packs = []
+    for lanes in (slice(width - 128, width), slice(0, 128)):
+        north, south = pick(even, near[24:, lanes], far[24:, lanes])
+        sub = iota(north.shape, 0)
+        packs.append(jnp.where(sub < 3, turn(north, -5, 0), jnp.where(sub < 5, 0.0, south)))
+    a_ref[:rows, :] = a_in[...]
+    b_ref[:rows, :] = b_in[...]
+    a_ref[rows:, :], b_ref[rows:, :] = pick(is_even("col"), *packs)
+
+
+def rhs_rows(g, c, land, bottom, surf, diag, sent_a, sent_b, near, far, s_ref, code_ref, diag_ref, gv, cv, lv, bv, sv, sems, deep_sems):
     rows, cols = surf.shape
     flat = [
         pltpu.make_async_copy(src, dst, sems.at[n])
-        for n, (src, dst) in enumerate(((land, lv), (bottom, bv), (surf, sv), (diag, diag_ref), (u, uv)))
+        for n, (src, dst) in enumerate(((land, lv), (bottom, bv), (surf, sv), (diag, diag_ref.at[:rows, :])))
     ]
     deep = [
         pltpu.make_async_copy(src.at[k], dst.at[k], deep_sems.at[k, n])
@@ -126,102 +208,47 @@
         for n, (src, dst) in enumerate(((g, gv), (c, cv)))
     ]
     start_all(flat[:2] + deep + flat[2:])
-    wait_all(flat[:2])
-    code = code_of(lv[...], bv[...])
-    code_ref[...] = code
-    cu = jnp.where(iota(code.shape, 1) < cols - 1, jnp.minimum(code, next_col(code)), 0.0)
-    co = jnp.where(iota(code.shape, 0) < rows - 1, jnp.minimum(code, next_row(code)), 0.0)
-    ub, vb = jnp.zeros_like(cu), jnp.zeros_like(co)
-    for k in range(LEV):
-        wait_all(deep[2 * k : 2 * k + 2])
-        gk, ck = gv[k], cv[k]
-        ub = ub + jnp.where(cu > k + 0.5, next_col(gk) - gk, 0.0) * (next_col(ck) + ck)
-        vb = vb + jnp.where(co > k + 0.5, next_row(gk) - gk, 0.0) * (next_row(ck) + ck)
-    wait_all(flat[2:])
-    s_ref[...] = sv[...] + 0.0625 * ((ub - prev_col(ub)) + (vb - prev_row(vb)))
-    packs = [
-        lane_pack(
-            [gv[k, :, lanes] for k in range(LEV)],
-            [cv[k, :, lanes] for k in range(LEV)],
-            code_ref[:, lanes],
-            [x[:, lanes] for x in (sv, diag_ref, uv)],
-            of_last,
-        )
-        for of_last, lanes in ((True, slice(cols - 128, cols)), (False, slice(0, 128)))
-    ]
-    a_ref[...], b_ref[...] = pick(is_even("col"), *packs)
-
-
-def row_halo(near, far, lanes):
-    even = is_even("row")
-
-    def plane(p):
-        at = slice(8 * (p // 2), 8 * (p // 2) + 8)
-        north, south = pick(even, near[at, lanes], far[at, lanes])
-        upper = iota(north.shape, 0) < DEEP
-        if p % 2 == 0:
-            return jnp.where(upper, north, turn(south, DEEP, 0))
-        return jnp.where(upper, turn(north, DEEP, 0), south)
-
-    return plane
-
-
-def join_cols(a_in, b_in, near, far, a_ref, b_ref):
-    rows, width = a_in.shape[0], near.shape[1]
-    packs = []
-    for of_last, lanes in ((True, slice(width - 128, width)), (False, slice(0, 128))):
-        halo = row_halo(near, far, lanes)
-        packs.append(
-            lane_pack(
-                [halo(2 * k) for k in range(LEV)],
-                [halo(2 * k + 1) for k in range(LEV)],
-                halo(CODE),
-                [halo(SURF), halo(DIAG)],
-                of_last,
-            )
-        )
-    a_ref[:rows, :] = a_in[...]
-    b_ref[:rows, :] = b_in[...]
-    a_ref[rows:, :], b_ref[rows:, :] = pick(is_even("col"), *packs)
-
-
-def halo_rows(s, code, diag, sent_a, sent_b, near, far, s_ref, code_ref, diag_ref):
-    rows, cols = s.shape
     even = is_even("row")
     lane, sub = iota((8, cols), 1), iota((8, cols), 0)
     upper = sub < DEEP
 
-    def strips(t):
-        at = slice(8 * t, 8 * t + 8)
-        high, low = pick(even, sent_a[at, :], sent_b[at, :])
-        north, south = pick(even, near[at, :], far[at, :])
-        one = [jnp.where(upper, x, turn(y, DEEP, 0)) for x, y in ((high, north), (south, low))]
-        two = [jnp.where(upper, turn(x, DEEP, 0), y) for x, y in ((high, north), (south, low))]
-        return one, two
-
-    codes, surfs = strips(LEV)
-    cus = [jnp.where(lane < cols - 1, jnp.minimum(x, next_col(x)), 0.0) for x in codes]
-    cos = [jnp.where(sub < 7, jnp.minimum(x, next_row(x)), 0.0) for x in codes]
-    ubs = [jnp.zeros((8, cols), F32)] * 2
-    vbs = [jnp.zeros((8, cols), F32)] * 2
-    for k in range(LEV):
-        gs, cs = strips(k)
-        for n in range(2):
-            gk, ck = gs[n], cs[n]
-            ubs[n] = ubs[n] + jnp.where(cus[n] > k + 0.5, next_col(gk) - gk, 0.0) * (next_col(ck) + ck)
-            vbs[n] = vbs[n] + jnp.where(cos[n] > k + 0.5, next_row(gk) - gk, 0.0) * (next_row(ck) + ck)
-    north, south = [
-        surfs[n] + 0.0625 * ((ubs[n] - prev_col(ubs[n])) + (vbs[n] - prev_row(vbs[n]))) for n in range(2)
-    ]
-    s_ref[:rows, :] = s[...]
-    code_ref[:rows, :] = code[...]
-    diag_ref[:rows, :] = diag[...]
-    s_ref[rows - 8 : rows, :] = s[rows - 8 :, :] + jnp.where(sub == 7, turn(0.0625 * vbs[0], 4, 0), 0.0)
-    s_ref[:8, :] = s[:8, :] - jnp.where(sub == 0, turn(0.0625 * vbs[1], -3, 0), 0.0)
-    s_ref[rows:, :] = turn(jnp.where(upper, south, north), DEEP, 0)
+    high, low = pick(even, sent_a[...], sent_b[...])
+    north, south = pick(even, near[...], far[...])
+
+    def across(below, above, here, there):
+        pair = [x[16 + at : 17 + at, :] for x, at in ((below, here), (above, there))]
+        open_v = jnp.minimum(*pair) > sub.astype(F32) + 0.5
+        total = jnp.where(open_v, above[:8] - below[:8], 0.0) * (above[8:16] + below[8:16])
+        for by in (4, 2, 1):
+            total = total + turn(total, by, 0)
+        return 0.0625 * total
+
+    up = across(high, north, 7, 4)
+    down = across(south, low, 7, 4)
     halo = row_halo(near, far, slice(0, cols))
+    s_ref[rows:, :] = halo(RHS) + jnp.where(sub == 0, -up, jnp.where(sub == 7, down, 0.0))
     code_ref[rows:, :] = halo(CODE)
     diag_ref[rows:, :] = halo(DIAG)
+    wait_all(flat[:2])
+    code = code_of(lv[...], bv[...])
+    code_ref[:rows, :] = code
+    cu = jnp.where(iota(code.shape, 1) < cols - 1, jnp.minimum(code, next_col(code)), 0.0)
+    co = jnp.where(iota(code.shape, 0) < rows - 1, jnp.minimum(code, next_row(code)), 0.0)
+
+    class Levels:
+        def __init__(self, ref, n):
+            self.ref, self.n = ref, n
+
+        def __getitem__(self, k):
+            deep[2 * k + self.n].wait()
+            return self.ref[k]
+
+    ub, vb = faces(Levels(gv, 0), Levels(cv, 1), cu, co)
+    wait_all(flat[2:])
+    s = sv[...] + 0.0625 * ((ub - prev_col(ub)) + (vb - prev_row(vb)))
+    s_ref[:8, :] = s[:8, :] - jnp.where(sub == 0, down, 0.0)
+    s_ref[8 : rows - 8, :] = s[8 : rows - 8, :]
+    s_ref[rows - 8 : rows, :] = s[rows - 8 :, :] + jnp.where(sub == 7, up, 0.0)
 
 
 def col_halo(near, far):
@@ -315,18 +342,26 @@
     start_all(flat + deep)
     wait_all(flat)
     rows, cols = u.shape
-    rh, ch = row_halo(rn, rf, slice(0, cols)), col_halo(cn, cf)
-
-    def wide(own, p, lane):
-        return jnp.concatenate([jnp.concatenate([own, rh(p)], axis=0), ch(lane)], axis=1)
-
-    code = wide(code_of(land[...], bottom[...]), CODE, 64)
+    ch = col_halo(cn, cf)
+    sub = iota((8, cols), 0)
+    north, south = pick(is_even("row"), rn[...], rf[...])
+
+    def wide(own, lane, above, below):
+        at = [8 * (x // 8) for x in (above, below)]
+        halo = jnp.where(
+            sub == 0,
+            turn(north[at[0] : at[0] + 8], -(above % 8), 0),
+            turn(south[at[1] : at[1] + 8], 7 - below % 8, 0),
+        )
+        return jnp.concatenate([jnp.concatenate([own, halo], axis=0), ch(lane)], axis=1)
+
+    code = wide(code_of(land[...], bottom[...]), 64, 20, 23)
     cu, cv = jnp.minimum(code, next_col(code)), jnp.minimum(code, next_row(code))
-    uw = 0.125 * wide(u[...], SPEED, 84)
-    vw = 0.125 * wide(v[...], SPEED, 84)
+    uw = 0.125 * wide(u[...], 84, 28, 28)
+    vw = 0.125 * wide(v[...], 84, 28, 28)
     for k in range(LEV):
         deep[k].wait()
-        gk = wide(g[k], 2 * k, 8 * k)
+        gk = wide(g[k], 8 * k, k, k)
         pu = jnp.where(cu > k + 0.5, next_col(gk) - gk, 0.0) * uw
         pv = jnp.where(cv > k + 0.5, next_row(gk) - gk, 0.0) * vw
         total = gk + pu + prev_col(pu) + pv + prev_row(pv)
@@ -374,10 +409,7 @@
     return quick(q, rest[0] / y[0])
 
 
-def combine(mom_in, r, p1, p2, x_ref, mom, x, sems):
-    load = pltpu.make_async_copy(mom_in, mom, sems.at[0])
-    load.start()
-    load.wait()
+def combine(mom, r, p1, p2, x_ref, x, sems):
     zero = jnp.zeros((8, 128), F32)
     tiles = [(mom[8 * i : 8 * i + 8, :], zero) for i in range(mom.shape[0] // 8)]
     while len(tiles) > 1:
@@ -412,7 +444,7 @@
     y1 = add(z1, neg(mul(l21, y2)))
     y0 = add(div(b0, a00), neg(add(mul(l10, y1), mul(l20, y2))))
     rows, cols = r.shape
-    bands = sems.shape[0] - 1
+    bands = sems.shape[0]
     tall = rows // bands
     done = []
     for b in range(bands):
@@ -421,7 +453,7 @@
             for j in range(cols // 128):
                 at = (slice(8 * i, 8 * i + 8), slice(128 * j, 128 * j + 128))
                 x[at] = y0[0] * r[at] + (y1[0] * p1[at] + y2[0] * p2[at])
-        done.append(pltpu.make_async_copy(x.at[band, :], x_ref.at[band, :], sems.at[1 + b]))
+        done.append(pltpu.make_async_copy(x.at[band, :], x_ref.at[band, :], sems.at[b]))
         done[-1].start()
     wait_all(done)
 
@@ -442,7 +474,6 @@
 
 def shards(tracer_adj_next, tracer, u_east, v_north, surf_adj_next, diag, land, bottom):
     levels, rows, cols = tracer.shape
-    planes = 2 * levels + 4
     size = lax.axis_size("row") * lax.axis_size("col")
     g, c = tracer_adj_next, tracer
     dma = pltpu.SemaphoreType.DMA
@@ -450,23 +481,30 @@
     whole = lambda kind=F32: pltpu.VMEM(two, kind)
     edges = [pltpu.VMEM((levels, 8, cols), F32)] * 4 + [pltpu.VMEM((8, cols), jnp.int32)] * 4 + [pltpu.VMEM((8, cols), F32)] * 6
     row_sent = call(
-        pack_rows, [HBM] * 7, [(VMEM, (4 * planes, cols))] * 2, edges + [dma((14,))], name="pack_rows"
+        pack_rows, [HBM] * 7, [(VMEM, (32, cols))] * 2, edges + [dma((14,))], name="pack_rows"
     )(g, c, land, bottom, surf_adj_next, diag, v_north)
     row_got = swap(row_sent, "row")
-    deep = pltpu.VMEM(g.shape, F32)
-    s, code, dg, a, b = call(
-        local,
+    deep, ends = pltpu.VMEM(g.shape, F32), (2, levels, rows, 128)
+    a, b = call(
+        pack_cols,
         [HBM] * 7,
-        [(VMEM, two)] * 3 + [(VMEM, (rows, 128))] * 2,
-        [deep, deep, whole(jnp.int32), whole(jnp.int32), whole(), whole(), dma((5,)), dma((levels, 2))],
-        name="local",
-        cost=pl.CostEstimate(flops=24 * g.size, bytes_accessed=8 * g.size, transcendentals=0),
+        [(VMEM, (rows, 128))] * 2,
+        [pltpu.VMEM(ends, F32)] * 2
+        + [pltpu.VMEM((2, rows, 128), jnp.int32)] * 2
+        + [pltpu.VMEM((3, 2, rows, 128), F32), dma((7, 2))],
+        name="pack_cols",
+        cost=pl.CostEstimate(flops=4 * g.size, bytes_accessed=4 * g.size, transcendentals=0),
     )(g, c, land, bottom, surf_adj_next, diag, u_east)
     col_sent = call(join_cols, [VMEM] * 4, [(VMEM, side)] * 2, name="join_cols")(a, b, *row_got)
     col_got = swap(col_sent, "col")
-    s, code, dg = call(halo_rows, [VMEM] * 7, [(VMEM, wide)] * 3, name="halo_rows")(
-        s, code, dg, *row_sent, *row_got
-    )
+    s, code, dg = call(
+        rhs_rows,
+        [HBM] * 6 + [VMEM] * 4,
+        [(VMEM, wide)] * 3,
+        [deep, deep, whole(jnp.int32), whole(jnp.int32), whole(), dma((4,)), dma((levels, 2))],
+        name="rhs_rows",
+        cost=pl.CostEstimate(flops=24 * g.size, bytes_accessed=8 * g.size, transcendentals=0),
+    )(g, c, land, bottom, surf_adj_next, diag, *row_sent, *row_got)
     r, p1, p2, mom = call(
         krylov,
         [VMEM] * 7,
@@ -484,9 +522,9 @@
     )(g, land, bottom, u_east, v_north, *row_got, *col_got)
     (surf_adj,) = call(
         combine,
-        [HBM] + [VMEM] * 3,
+        [VMEM] * 4,
         [(HBM, two)],
-        [pltpu.VMEM((size, 128), F32), whole(), dma((5,))],
+        [whole(), dma((2,))],
         name="combine",
     )(mom, r, p1, p2)
     return tracer_adj, surf_adj

time: 47.9 us -> 45.2 us (0.944)
  waiting for transfers between devices: 6.47 us -> 4.18 us
  Pallas kernels: 17.8 us -> 18.8 us
  starting transfers between devices: 22 us -> 21.3 us
  local copies, waits for them, and re-layouts: 0.62 us -> 0 us
    ppermute x4, waiting for transfers between devices: 2.33 us -> 0.01 us  [swap(): lax.ppermute(b, axis, swap_pairs(axis, first))]
    pallas_call x7, Pallas kernels: 17.8 us -> 18.8 us  [call(): run(*[pltpu.with_memory_space_constraint(x, spec.memory_space) for x, spe...]
    all_to_all x1, starting transfers between devices: 13.5 us -> 12.8 us  [shards(): mom = lax.all_to_all(mom, ('row', 'col'), 0, 0, tiled=True)]
    unnamed x2 -> x0, local copies, waits for them, and re-layouts: 0.62 us -> none
  transfers between devices with their start and end apart: 5 -> 5, of which waited for: 2 -> 1; matrix products, arithmetic and copies ran while one was open for 0% -> 0% of each run, Pallas kernels for 23% -> 28%
where the time goes in v4:
time: 45.2 us; the launch traced here: 45 us
  starting transfers between devices  21.3 us (47%)
  Pallas kernels  18.8 us (42%)
  waiting for transfers between devices  4.18 us (9%)
  between operations  0.73 us (2%)
    pallas_call x7, Pallas kernels, call(): run(*[pltpu.with_memory_space_constraint(x, spec.memory_space) for x, spe...  18.8 us
    all_to_all x1, starting transfers between devices, shards(): mom = lax.all_to_all(mom, ('row', 'col'), 0, 0, tiled=True)  12.8 us
    ppermute x4, starting transfers between devices, swap(): lax.ppermute(b, axis, swap_pairs(axis, first))  8.44 us
    all_to_all x1, waiting for transfers between devices, shards(): mom = lax.all_to_all(mom, ('row', 'col'), 0, 0, tiled=True)  4.17 us
  transfers between devices with their start and end apart: 5, of which 1 were waited for; matrix products, arithmetic and copies ran while one was open for 0% of the time, Pallas kernels for 28%

profile of v4, /device:TPU:1, one launch (start us, length us, event | category | flops | bytes accessed | tf_op | source)
XLA Modules:
  0.0 45.0 jit_solution(8460641671354462731)
XLA Ops:
  0.6 1.7 %pack_rows.1 = (f32[32,512]{1,0:T(8,128)S(1)}, f32[32,512]{1,0:T(8,128)S(1)}) custom-call(f32[8,128,512]{2,1,0:T(8,128)} %g.5, f32[8,128,512]{2,1,0:T(8,128)} %c.5, s32[128,512]{1,0:T(8,128)} %land.5, s32[128,512]{1,0:T(8,128)} %bottom.5, f32[128,512]{1,0:T(8,128)} %surf.5, f32[128,512]{1,0:T(8,128)} %diag.5, f32[128,512]{1,0:T(8,128)} %v_in.1), custom_call_target="tpu_custom_call" | custom-call | tf_op jit(solution)/shard_map/pack_rows/pallas_call | solution.py:472
  2.4 2.2 %collective-permute-start = (f32[32,512]{1,0:T(8,128)S(1)}, f32[32,512]{1,0:T(8,128)S(1)}, u32[]{:S(2)}, u32[]{:S(2)}) collective-permute-start(f32[32,512]{1,0:T(8,128)S(1)} %get-tuple-element.15.sent_a), channel_id=1, source_target_pairs={{0,16},{16,0},{32,48},{48,32},{64,80},{80,64},{96,112},{112,96},{1... | collective-permute-start | bytes 196616 | tf_op jit(solution)/shard_map/ppermute | solution.py:33
  4.6 0.7 %collective-permute-start.1 = (f32[32,512]{1,0:T(8,128)S(1)}, f32[32,512]{1,0:T(8,128)S(1)}, u32[]{:S(2)}, u32[]{:S(2)}) collective-permute-start(f32[32,512]{1,0:T(8,128)S(1)} %get-tuple-element.16.sent_b), channel_id=1, source_target_pairs={{16,32},{32,16},{48,64},{64,48},{80,96},{96,80},{17,33},{33,17},{4... | collective-permute-start | bytes 196616 | tf_op jit(solution)/shard_map/ppermute | solution.py:33
  5.2 3.0 %pack_cols.1 = (f32[128,128]{1,0:T(8,128)S(1)}, f32[128,128]{1,0:T(8,128)S(1)}) custom-call(f32[8,128,512]{2,1,0:T(8,128)} %g.5, f32[8,128,512]{2,1,0:T(8,128)} %c.5, s32[128,512]{1,0:T(8,128)} %land.5, s32[128,512]{1,0:T(8,128)} %bottom.5, f32[128,512]{1,0:T(8,128)} %surf.5, f32[128,512]{1,0:T(8,128)} %diag.5, f32[128,512]{1,0:T(8,128)} %u_in.1), custom_call_target="tpu_custom_call" | custom-call | flops 2097152 | bytes 2097152 | tf_op jit(solution)/shard_map/pack_cols/pallas_call | solution.py:472
  8.2 0.0 collective-permute-done.near.rn
  8.3 0.0 collective-permute-done.1.far.rf
  8.3 1.0 %collective-permute-start.2 = (f32[136,128]{1,0:T(8,128)S(1)}, f32[136,128]{1,0:T(8,128)S(1)}, u32[]{:S(2)}, u32[]{:S(2)}) collective-permute-start(f32[136,128]{1,0:T(8,128)S(1)} %get-tuple-element.19.sent_a), channel_id=1, source_target_pairs={{0,1},{1,0},{2,3},{3,2},{4,5},{5,4},{6,7},{7,6},{8,9},{9,8},{10,11... | collective-permute-start | bytes 208904 | tf_op jit(solution)/shard_map/ppermute | solution.py:33
  9.3 4.6 %collective-permute-start.3 = (f32[136,128]{1,0:T(8,128)S(1)}, f32[136,128]{1,0:T(8,128)S(1)}, u32[]{:S(2)}, u32[]{:S(2)}) collective-permute-start(f32[136,128]{1,0:T(8,128)S(1)} %get-tuple-element.20.sent_b), channel_id=1, source_target_pairs={{1,2},{2,1},{3,4},{4,3},{5,6},{6,5},{7,8},{8,7},{9,10},{10,9},{11,... | collective-permute-start | bytes 208904 | tf_op jit(solution)/shard_map/ppermute | solution.py:33
  13.9 4.4 %rhs_rows.1 = (f32[136,512]{1,0:T(8,128)S(1)}, f32[136,512]{1,0:T(8,128)S(1)}, f32[136,512]{1,0:T(8,128)S(1)}) custom-call(f32[8,128,512]{2,1,0:T(8,128)} %g.5, f32[8,128,512]{2,1,0:T(8,128)} %c.5, s32[128,512]{1,0:T(8,128)} %land.5, s32[128,512]{1,0:T(8,128)} %bottom.5, f32[128,512]{1,0:T(8,128)} %surf.5, f32[128,512]{1,0:T(8,128)} %diag.5, ...), custom_call_target="tpu_custom_call" | custom-call | flops 12582912 | bytes 4194304 | tf_op jit(solution)/shard_map/rhs_rows/pallas_call | solution.py:472
  18.3 0.0 collective-permute-done.2.cn.near
  18.3 0.0 collective-permute-done.3.cf.far
  18.3 2.7 %krylov.1 = (f32[128,512]{1,0:T(8,128)S(1)}, f32[128,512]{1,0:T(8,128)S(1)}, f32[128,512]{1,0:T(8,128)S(1)}, f32[128,128]{1,0:T(8,128)}) custom-call(f32[136,512]{1,0:T(8,128)S(1)} %get-tuple-element.21.s, f32[136,512]{1,0:T(8,128)S(1)} %get-tuple-element.22.code, f32[136,512]{1,0:T(8,128)S(1)} %get-tuple-element.23.diag, ...), custom_call_target="tpu_custom_call" | custom-call | tf_op jit(solution)/shard_map/krylov/pallas_call | solution.py:472
  21.0 12.8 %all-to-all-start = ((f32[128,1,128]{2,1,0:T(1,128)}), f32[128,1,128]{2,1,0:T(1,128)S(1)}, u32[]{:S(2)}, u32[]{:S(2)}) async-start(f32[128,1,128]{2,1,0:T(1,128)} %bitcast.1), calls=%async_computation | async-start | bytes 131072 | tf_op jit(solution)/shard_map/all_to_all | solution.py:514
  33.8 5.4 %tracer.1 = f32[8,128,512]{2,1,0:T(8,128)} custom-call(f32[8,128,512]{2,1,0:T(8,128)} %g.5, s32[128,512]{1,0:T(8,128)} %land.5, s32[128,512]{1,0:T(8,128)} %bottom.5, f32[128,512]{1,0:T(8,128)} %u_in.1, f32[128,512]{1,0:T(8,128)} %v_in.1, f32[32,512]{1,0:T(8,128)S(1)} %collective-permute-done.near.rn, f32[32,512]{1,0:T(8,128)S(1)} %collective-permute-done.1.far.rf, ...), custom_call_target="tpu_custom_call" | custom-call | flops 10485760 | bytes 6291456 | tf_op jit(solution)/shard_map/tracer/pallas_call | solution.py:472
  39.2 4.2 %all-to-all-done = f32[128,1,128]{2,1,0:T(1,128)S(1)} async-done(((f32[128,1,128]{2,1,0:T(1,128)}), f32[128,1,128]{2,1,0:T(1,128)S(1)}, u32[]{:S(2)}, u32[]{:S(2)}) %all-to-all-start) | async-done | bytes 65568 | tf_op jit(solution)/shard_map/all_to_all | solution.py:514
  43.4 1.6 %combine.1 = f32[128,512]{1,0:T(8,128)} custom-call(f32[128,128]{1,0:T(8,128)S(1)} %bitcast.4, f32[128,512]{1,0:T(8,128)S(1)} %get-tuple-element.25.r, f32[128,512]{1,0:T(8,128)S(1)} %get-tuple-element.26.p1, f32[128,512]{1,0:T(8,128)S(1)} %get-tuple-element.27.p2), custom_call_target="tpu_custom_call" | custom-call | tf_op jit(solution)/shard_map/combine/pallas_call | solution.py:472
  (1 shorter events, 0.0 us)
Async XLA Ops:
  2.4 5.9 %collective-permute-start = (f32[32,512]{1,0:T(8,128)S(1)}, f32[32,512]{1,0:T(8,128)S(1)}, u32[]{:S(2)}, u32[]{:S(2)}) collective-permute-start(f32[32,512]{1,0:T(8,128)S(1)} %get-tuple-element.15.sent_a), channel_id=1, source_target_pairs={{0,16},{16,0},{32,48},{48,32},{64,80},{80,64},{96,112},{112,96},{1... | collective-permute-start | bytes 196616 | tf_op jit(solution)/shard_map/ppermute | solution.py:33
  4.6 3.7 %collective-permute-start.1 = (f32[32,512]{1,0:T(8,128)S(1)}, f32[32,512]{1,0:T(8,128)S(1)}, u32[]{:S(2)}, u32[]{:S(2)}) collective-permute-start(f32[32,512]{1,0:T(8,128)S(1)} %get-tuple-element.16.sent_b), channel_id=1, source_target_pairs={{16,32},{32,16},{48,64},{64,48},{80,96},{96,80},{17,33},{33,17},{4... | collective-permute-start | bytes 196616 | tf_op jit(solution)/shard_map/ppermute | solution.py:33
  8.3 10.0 %collective-permute-start.2 = (f32[136,128]{1,0:T(8,128)S(1)}, f32[136,128]{1,0:T(8,128)S(1)}, u32[]{:S(2)}, u32[]{:S(2)}) collective-permute-start(f32[136,128]{1,0:T(8,128)S(1)} %get-tuple-element.19.sent_a), channel_id=1, source_target_pairs={{0,1},{1,0},{2,3},{3,2},{4,5},{5,4},{6,7},{7,6},{8,9},{9,8},{10,11... | collective-permute-start | bytes 208904 | tf_op jit(solution)/shard_map/ppermute | solution.py:33
  9.3 8.9 %collective-permute-start.3 = (f32[136,128]{1,0:T(8,128)S(1)}, f32[136,128]{1,0:T(8,128)S(1)}, u32[]{:S(2)}, u32[]{:S(2)}) collective-permute-start(f32[136,128]{1,0:T(8,128)S(1)} %get-tuple-element.20.sent_b), channel_id=1, source_target_pairs={{1,2},{2,1},{3,4},{4,3},{5,6},{6,5},{7,8},{8,7},{9,10},{10,9},{11,... | collective-permute-start | bytes 208904 | tf_op jit(solution)/shard_map/ppermute | solution.py:33
  21.0 22.4 %all-to-all-start = ((f32[128,1,128]{2,1,0:T(1,128)}), f32[128,1,128]{2,1,0:T(1,128)S(1)}, u32[]{:S(2)}, u32[]{:S(2)}) async-start(f32[128,1,128]{2,1,0:T(1,128)} %bitcast.1), calls=%async_computation | async-start | bytes 131072 | tf_op jit(solution)/shard_map/all_to_all | solution.py:514

commit v5 on v4

v5 whole, which is shorter than its diff:
```python
import functools

import jax
import jax.numpy as jnp
from jax import lax
from jax.experimental import pallas as pl
from jax.experimental.pallas import tpu as pltpu
from jax.sharding import PartitionSpec as P

LEV = 8
DEEP = 4
NEAR = 32
SHIFT = 1.0
F32 = jnp.float32
VMEM = pl.BlockSpec(memory_space=pltpu.VMEM)
HBM = pl.BlockSpec(memory_space=pltpu.HBM)
PARAMS = pltpu.CompilerParams(vmem_limit_bytes=32 * 1024 * 1024)


G, C, RHS, CODE, DIAG = 0, 1, 4, 5, 6


def code_of(land, bottom):
    return jnp.where(land == 1, bottom, 0).astype(F32)


def swap_pairs(axis, first):
    count = lax.axis_size(axis)
    pairs = []
    for low in range(first, count - 1, 2):
        pairs += [(low, low + 1), (low + 1, low)]
    return pairs


def is_even(axis):
    return lax.rem(lax.axis_index(axis), 2) == 0


def iota(shape, dim):
    return lax.broadcasted_iota(jnp.int32, shape, dim)


def turn(x, by, dim):
    by = by % x.shape[dim]
    return pltpu.roll(x, by, dim) if by else x


def next_col(a):
    return turn(a, -1, 1)


def prev_col(a):
    return turn(a, 1, 1)


def next_row(a):
    return turn(a, -1, 0)


def prev_row(a):
    return turn(a, 1, 0)


def pick(even, one, two):
    return jnp.where(even, one, two), jnp.where(even, two, one)


def start_all(copies):
    for copy in copies:
        copy.start()


def wait_all(copies):
    for copy in copies:
        copy.wait()


def pack_rows(g, c, land, bottom, surf, diag, v, a_ref, b_ref, g0, g1, c0, c1, l0, l1, b0, b1, s0, s1, d0, d1, v0, v1, sems):
    rows = surf.shape[0]
    copies = []
    for src, low, high in ((g, g0, g1), (c, c0, c1), (land, l0, l1), (bottom, b0, b1), (surf, s0, s1), (diag, d0, d1), (v, v0, v1)):
        for dst, at in ((low, slice(0, 8)), (high, slice(rows - 8, rows))):
            part = src.at[:, at, :] if len(src.shape) == 3 else src.at[at, :]
            copies.append(pltpu.make_async_copy(part, dst, sems.at[len(copies)]))
    start_all(copies)
    wait_all(copies)

    cols = surf.shape[1]
    lane, sub = iota((8, cols), 1), iota((8, cols), 0)
    upper = sub < DEEP

    def tiles(g, c, land, bottom, surf, diag, v, of_last):
        code = code_of(land[...], bottom[...])
        g, c = [g[k] for k in range(LEV)], [c[k] for k in range(LEV)]
        cu = jnp.where(lane < cols - 1, jnp.minimum(code, next_col(code)), 0.0)
        cv = jnp.where(sub < 7, jnp.minimum(code, next_row(code)), 0.0)
        ub, vb = faces(g, c, cu, cv)
        rhs = surf[...] + 0.0625 * ((ub - prev_col(ub)) + (vb - prev_row(vb)))
        edge = 7 if of_last else 0

        def outermost(x):
            out = turn(x[0], -edge, 0)
            for k in range(1, LEV):
                out = jnp.where(sub == k, turn(x[k], k - edge, 0), out)
            return out

        half = DEEP if of_last else 0
        one = jnp.where(upper, turn(rhs, half, 0), turn(code, DEEP - half, 0))
        two = jnp.where(upper, turn(diag[...], half, 0), turn(v[...], DEEP - edge, 0))
        ends = []
        for high, lanes in ((False, slice(0, 128)), (True, slice(cols - 128, cols))):
            cut = lambda xs: [x[:, lanes] for x in xs]
            corner = lane_pack(cut(g), cut(c), code[:, lanes], cut([surf, diag]), high)
            ends.append(jnp.where(sub[:, :128] < 5, two[:, lanes], corner if of_last else turn(corner, 5, 0)))
        two = jnp.concatenate([ends[0], two[:, 128 : cols - 128], ends[1]], axis=1)
        return outermost(g), outermost(c), one, two

    first = tiles(g0, c0, l0, b0, s0, d0, v0, False)
    last = tiles(g1, c1, l1, b1, s1, d1, v1, True)
    even = is_even("row")
    for t in range(4):
        a_ref[8 * t : 8 * t + 8, :], b_ref[8 * t : 8 * t + 8, :] = pick(even, last[t], first[t])


def faces(g, c, cu, cv):
    ub, vb = jnp.zeros_like(cu), jnp.zeros_like(cv)
    for k in range(LEV):
        gk, ck = g[k], c[k]
        ub = ub + jnp.where(cu > k + 0.5, next_col(gk) - gk, 0.0) * (next_col(ck) + ck)
        vb = vb + jnp.where(cv > k + 0.5, next_row(gk) - gk, 0.0) * (next_row(ck) + ck)
    return ub, vb


def operator(cu, cv, dg):
    west, south = prev_col(cu), prev_row(cv)
    center = (dg - SHIFT) + ((cu + west) + (cv + south))

    def shifted(v):
        sides = (cu * next_col(v) + west * prev_col(v)) + (cv * next_row(v) + south * prev_row(v))
        return center * v - sides

    return shifted


def products(r, cu, cv, dg, rows):
    shifted = operator(cu, cv, dg)
    p1 = shifted(r)
    p2 = shifted(p1)
    eu, ev = p2 - next_col(p2), p2 - next_row(p2)
    energy = dg * p2 * p2 + (cu * eu * eu + cv * ev * ev)
    q, p, o = r[:rows], p1[:rows], p2[:rows]
    return p1, p2, (q * q, q * p, p * p, p * o, o * o, energy[:rows])


def fold(prod, lanes):
    tiles = [prod[8 * i : 8 * i + 8, lanes] for i in range(prod.shape[0] // 8)]
    while len(tiles) > 1:
        tiles = [sum(tiles[i : i + 2][1:], tiles[i]) for i in range(0, len(tiles), 2)]
    return tiles[0]


def lane_pack(g, c, code, rest, of_last):
    group = iota(code.shape, 1) // DEEP
    base, one, two = (DEEP, 0, 1) if of_last else (0, 1, 0)
    places = [(g[k], 2 * k + one) for k in range(LEV)] + [(c[k], 16 + 2 * k + one) for k in range(LEV)]
    places += [(code, 2 * k + two) for k in range(LEV)] + [(x, 16 + 2 * n + two) for n, x in enumerate(rest)]
    if of_last:
        places.append((code, 31))
    out = jnp.zeros_like(code)
    for x, at in places:
        out = jnp.where(group == at, turn(x, DEEP * at + base, 1), out)
    return out


def pack_cols(g, c, land, bottom, surf, diag, u, row_in, a_ref, b_ref, row_ref):
    row_ref[...] = row_in[...]
    cols = surf.shape[1]
    packs = [
        lane_pack(
            [g[k, :, lanes] for k in range(LEV)],
            [c[k, :, lanes] for k in range(LEV)],
            code_of(land[:, lanes], bottom[:, lanes]),
            [x[:, lanes] for x in (surf, diag, u)],
            of_last,
        )
        for of_last, lanes in ((True, slice(cols - 128, cols)), (False, slice(0, 128)))
    ]
    a_ref[...], b_ref[...] = pick(is_even("col"), *packs)


def row_halo(near, far, lanes):
    even = is_even("row")

    def plane(p):
        at = slice(8 * (p // 2), 8 * (p // 2) + 8)
        north, south = pick(even, near[at, lanes], far[at, lanes])
        upper = iota(north.shape, 0) < DEEP
        if p % 2 == 0:
            return jnp.where(upper, north, turn(south, DEEP, 0))
        return jnp.where(upper, turn(north, DEEP, 0), south)

    return plane


def join_cols(of_near, own, near, far, *refs):
    rows, width = own.shape[0], near.shape[1]
    out = refs[-1]
    even = is_even("row")
    packs = []
    for lanes in (slice(width - 128, width), slice(0, 128)):
        north, south = pick(even, near[24:, lanes], far[24:, lanes])
        sub = iota(north.shape, 0)
        packs.append(jnp.where(sub < 3, turn(north, -5, 0), jnp.where(sub < 5, 0.0, south)))
    out[:rows, :] = own[...]
    out[rows:, :] = pick(is_even("col"), *packs)[0 if of_near else 1]


def rhs_rows(g, c, land, bottom, surf, diag, sent_a, sent_b, near, far, r_ref, code_ref, diag_ref, rs_ref, codes_ref, diags_ref):
    rows, cols = surf.shape
    even = is_even("row")
    lane, sub = iota((8, cols), 1), iota((8, cols), 0)
    upper = sub < DEEP

    high, low = pick(even, sent_a[...], sent_b[...])
    north, south = pick(even, near[...], far[...])

    def across(below, above, here, there):
        pair = [x[16 + at : 17 + at, :] for x, at in ((below, here), (above, there))]
        open_v = jnp.minimum(*pair) > sub.astype(F32) + 0.5
        total = jnp.where(open_v, above[:8] - below[:8], 0.0) * (above[8:16] + below[8:16])
        for by in (4, 2, 1):
            total = total + turn(total, by, 0)
        return 0.0625 * total

    up = across(high, north, 7, 4)
    down = across(south, low, 7, 4)
    halo = row_halo(near, far, slice(0, cols))
    r_halo = halo(RHS) + jnp.where(sub == 0, -up, jnp.where(sub == 7, down, 0.0))
    code = code_of(land[...], bottom[...])
    cu = jnp.where(iota(code.shape, 1) < cols - 1, jnp.minimum(code, next_col(code)), 0.0)
    cv = jnp.where(iota(code.shape, 0) < rows - 1, jnp.minimum(code, next_row(code)), 0.0)
    ub, vb = faces(g, c, cu, cv)
    r = surf[...] + 0.0625 * ((ub - prev_col(ub)) + (vb - prev_row(vb)))
    low = r[:8] - jnp.where(sub == 0, down, 0.0)
    high = r[rows - 8 :] + jnp.where(sub == 7, up, 0.0)
    r = jnp.concatenate([low, r[8 : rows - 8], high, r_halo], axis=0)
    code = jnp.concatenate([code, halo(CODE)], axis=0)
    dg = jnp.concatenate([diag[...], halo(DIAG)], axis=0)
    left = iota((rows + 8, 128), 1) < 64
    for x, ref in ((r, rs_ref), (code, codes_ref), (dg, diags_ref)):
        ref[...] = jnp.where(left, turn(x[:, cols - 128 :], -68, 1), turn(x[:, :128], 68, 1))
    r_ref[...] = r
    code_ref[...] = code
    diag_ref[...] = dg


def inner(r_in, code_in, diag_in, r_ref, p1_ref, p2_ref, mom_ref, sem):
    rows, cols = p1_ref.shape
    copy = pltpu.make_async_copy(r_in.at[:rows, :], r_ref, sem)
    copy.start()
    code = 0.125 * code_in[...]
    cu = jnp.where(iota(code.shape, 1) < cols - 1, jnp.minimum(code, next_col(code)), 0.0)
    cv = jnp.minimum(code, next_row(code))
    p1, p2, prods = products(r_in[...], cu, cv, diag_in[...], rows)
    p1_ref[...] = p1[:rows]
    p2_ref[...] = p2[:rows]
    lane = iota((8, 128), 1)
    for m, prod in enumerate(prods):
        parts = [fold(prod, slice(128 * j, 128 * j + 128)) for j in range(cols // 128)]
        parts[0] = jnp.where(lane >= NEAR, parts[0], 0.0)
        parts[-1] = jnp.where(lane < 128 - NEAR, parts[-1], 0.0)
        mom_ref[8 * m : 8 * m + 8, :] = sum(parts[1:], parts[0])
    copy.wait()


def col_halo(near, far):
    east, west = pick(is_even("col"), near[...], far[...])
    left = iota(east.shape, 1) < 64

    def plane(of_east, of_west):
        return jnp.where(left, turn(east, -of_east, 1), turn(west, 124 - of_west, 1))

    return plane


def outer(rs, codes, diags, mom_in, sent_a, sent_b, near, far, r_ref, p1_ref, p2_ref, mom_ref):
    rows = rs.shape[0] - 8
    even = is_even("col")
    high, low = pick(even, sent_a[...], sent_b[...])
    east, west = pick(even, near[...], far[...])
    lane = iota(high.shape, 1)
    place = lane % 8
    own, left = place < DEEP, lane < 64
    level = (lane // 8).astype(F32) + 0.5

    def rhs_terms(first, second, u_from, v_from):
        gc = jnp.where(own, first, second)
        mixed = jnp.where(own, second, first)
        code = turn(mixed, 4, 1)
        one, two = turn(gc, -1, 1) - gc, turn(gc, 63, 1) + turn(gc, 64, 1)
        keep = (place >= u_from) & (place < u_from + 4)
        open_u = (jnp.minimum(code, turn(mixed, 3, 1)) > level) & keep
        ub = jnp.where(open_u, one, 0.0) * two
        one, two = gc - turn(gc, 1, 1), turn(gc, 64, 1) + turn(gc, 65, 1)
        keep = (place > u_from) & (place <= u_from + 4)
        open_u = (jnp.minimum(code, turn(mixed, 5, 1)) > level) & keep
        ub = ub - jnp.where(open_u, one, 0.0) * two
        keep = (place >= v_from) & (place < v_from + 4)
        open_v = (jnp.minimum(code, next_row(code)) > level) & keep
        c = turn(gc, 64, 1)
        vb = jnp.where(open_v, next_row(gc) - gc, 0.0) * (next_row(c) + c)
        return ub + (vb - prev_row(vb))

    at_east = rhs_terms(high, east, 3, 4)
    for by in (8, 16, 32):
        at_east = at_east + turn(at_east, by, 1)
    at_west = rhs_terms(west, low, 0, 0)
    at_west = turn(at_west, 64, 1) + turn(at_west, 56, 1)
    for by in (16, 32):
        at_west = at_west + turn(at_west, -by, 1)

    def filled(x, e, w):
        return jnp.where((lane < 60) | (lane >= 68), x, jnp.where(left, e, w))

    added = jnp.where((lane >= 59) & (lane < 69), jnp.where(left, at_east, at_west), 0.0)
    r = filled(rs[...], turn(east, -4, 1), turn(west, -4, 1)) + 0.0625 * added
    code = 0.125 * filled(codes[...], turn(east, 4, 1), turn(west, 4, 1))
    dg = filled(diags[...], turn(east, -12, 1), turn(west, -12, 1))
    cu, cv = jnp.minimum(code, next_col(code)), jnp.minimum(code, next_row(code))
    p1, p2, prods = products(r, cu, cv, dg, rows)
    r_ref[...] = r
    p1_ref[...] = p1
    p2_ref[...] = p2
    lane = iota((8, 128), 1)
    mine = ((lane >= 60 - NEAR) & (lane < 60)) | ((lane >= 68) & (lane < 68 + NEAR))
    packed = jnp.zeros((8, 128), F32)
    for m, prod in enumerate(prods):
        part = mom_in[8 * m : 8 * m + 8, :] + jnp.where(mine, fold(prod, slice(0, 128)), 0.0)
        for by in (4, 2, 1):
            part = part + turn(part, by, 0)
        part = ((part + turn(part, 16, 1)) + (turn(part, 32, 1) + turn(part, 48, 1))) + (
            (turn(part, 64, 1) + turn(part, 80, 1)) + (turn(part, 96, 1) + turn(part, 112, 1))
        )
        part = (part + turn(part, 4, 1)) + (turn(part, 8, 1) + turn(part, 12, 1))
        packed = jnp.where(lane // 4 == m, part, packed)
    for i in range(mom_ref.shape[0] // 8):
        mom_ref[8 * i : 8 * i + 8, :] = packed


def tracer_kernel(g_in, land_in, bottom_in, u_in, v_in, rn, rf, cn, cf, out_ref, g, land, bottom, u, v, out, sems, g_sems, out_sems):
    flat = [
        pltpu.make_async_copy(src, dst, sems.at[n])
        for n, (src, dst) in enumerate(((land_in, land), (bottom_in, bottom), (u_in, u), (v_in, v)))
    ]
    deep = [pltpu.make_async_copy(g_in.at[k], g.at[k], g_sems.at[k]) for k in range(LEV)]
    done = [pltpu.make_async_copy(out.at[k], out_ref.at[k], out_sems.at[k]) for k in range(LEV)]
    start_all(flat + deep)
    wait_all(flat)
    rows, cols = u.shape
    ch = col_halo(cn, cf)
    sub = iota((8, cols), 0)
    north, south = pick(is_even("row"), rn[...], rf[...])

    def wide(own, lanes, above, below):
        at = [8 * (x // 8) for x in (above, below)]
        halo = jnp.where(
            sub == 0,
            turn(north[at[0] : at[0] + 8], -(above % 8), 0),
            turn(south[at[1] : at[1] + 8], 7 - below % 8, 0),
        )
        return jnp.concatenate([jnp.concatenate([own, halo], axis=0), ch(*lanes)], axis=1)

    code = wide(code_of(land[...], bottom[...]), (0, 4), 20, 23)
    cu, cv = jnp.minimum(code, next_col(code)), jnp.minimum(code, next_row(code))
    uw = 0.125 * wide(u[...], (80, 84), 28, 28)
    vw = 0.125 * wide(v[...], (80, 84), 28, 28)
    for k in range(LEV):
        deep[k].wait()
        gk = wide(g[k], (8 * k + 4, 8 * k), k, k)
        pu = jnp.where(cu > k + 0.5, next_col(gk) - gk, 0.0) * uw
        pv = jnp.where(cv > k + 0.5, next_row(gk) - gk, 0.0) * vw
        total = gk + pu + prev_col(pu) + pv + prev_row(pv)
        out[k] = total[:rows, :cols]
        done[k].start()
    wait_all(done)


def two_sum(a, b):
    s = a + b
    t = s - a
    return s, (a - (s - t)) + (b - t)


def quick(a, b):
    s = a + b
    return s, b - (s - a)


def split(a):
    t = a * 4097.0
    high = t - (t - a)
    return high, a - high


def add(x, y):
    s, e = two_sum(x[0], y[0])
    return quick(s, e + (x[1] + y[1]))


def neg(x):
    return -x[0], -x[1]


def mul(x, y):
    p = x[0] * y[0]
    (ah, al), (bh, bl) = split(x[0]), split(y[0])
    e = ((ah * bh - p) + ah * bl + al * bh) + al * bl
    return quick(p, e + (x[0] * y[1] + x[1] * y[0]))


def div(x, y):
    q = x[0] / y[0]
    rest = add(x, neg(mul((q, jnp.zeros_like(q)), y)))
    return quick(q, rest[0] / y[0])


def combine(mom, r, p1, p2, rs, p1s, p2s, x_ref, x, sems):
    zero = jnp.zeros((8, 128), F32)
    tiles = [(mom[8 * i : 8 * i + 8, :], zero) for i in range(mom.shape[0] // 8)]
    while len(tiles) > 1:
        tiles = [add(tiles[i], tiles[i + 1]) for i in range(0, len(tiles), 2)]
    total = tiles[0]
    for by in (4, 2, 1):
        total = add(total, tuple(pltpu.roll(a, by, 0) for a in total))
    sums = []
    for m in range(6):
        four = [
            tuple(jnp.broadcast_to(a[:, at : at + 1], (8, 128)) for a in total)
            for at in range(4 * m, 4 * m + 4)
        ]
        sums.append(add(add(four[0], four[1]), add(four[2], four[3])))
    m00, m01, m11, m12, m22, e22 = sums
    a00, a01, a02 = add(m01, m00), add(m11, m01), add(m12, m11)
    a11, a12, a22 = a02, add(m22, m12), e22
    l10 = div(a01, a00)
    l20 = div(a02, a00)
    w11 = add(a11, neg(mul(l10, a01)))
    w12 = add(a12, neg(mul(l10, a02)))
    ok1 = w11[0] > 1e-9 * a11[0]
    l21 = tuple(jnp.where(ok1, a, 0.0) for a in div(w12, w11))
    w22 = add(add(a22, neg(mul(l20, a02))), neg(mul(l21, w12)))
    ok2 = w22[0] > 1e-9 * a22[0]
    b0 = m00
    b1 = add(m01, neg(mul(l10, b0)))
    z1 = tuple(jnp.where(ok1, a, 0.0) for a in div(b1, w11))
    b2 = add(add(m11, neg(mul(l20, b0))), neg(mul(l21, b1)))
    z2 = tuple(jnp.where(ok2, a, 0.0) for a in div(b2, w22))
    y2 = z2
    y1 = add(z1, neg(mul(l21, y2)))
    y0 = add(div(b0, a00), neg(add(mul(l10, y1), mul(l20, y2))))
    rows, cols = r.shape
    bands = sems.shape[0]
    tall = rows // bands
    done = []
    for b in range(bands):
        band = slice(b * tall, (b + 1) * tall)
        for i in range(b * tall // 8, (b + 1) * tall // 8):
            at = slice(8 * i, 8 * i + 8)
            lane = iota((8, 128), 1)
            side = y0[0] * rs[at, :] + (y1[0] * p1s[at, :] + y2[0] * p2s[at, :])
            for j in range(cols // 128):
                to = (at, slice(128 * j, 128 * j + 128))
                tile = y0[0] * r[to] + (y1[0] * p1[to] + y2[0] * p2[to])
                if j == 0:
                    tile = jnp.where(lane < NEAR, turn(side, -68, 1), tile)
                if j == cols // 128 - 1:
                    tile = jnp.where(lane >= 128 - NEAR, turn(side, 68, 1), tile)
                x[to] = tile
        done.append(pltpu.make_async_copy(x.at[band, :], x_ref.at[band, :], sems.at[b]))
        done[-1].start()
    wait_all(done)


def call(kernel, ins, outs, scratch=(), name=None, cost=None):
    run = pl.pallas_call(
        kernel,
        in_specs=list(ins),
        out_specs=[spec for spec, _ in outs],
        out_shape=[spec.memory_space(shape, F32) for spec, shape in outs],
        scratch_shapes=list(scratch),
        compiler_params=PARAMS,
        cost_estimate=cost,
        name=name,
    )
    return lambda *args: run(*[pltpu.with_memory_space_constraint(x, spec.memory_space) for x, spec in zip(args, ins)])


def shards(tracer_adj_next, tracer, u_east, v_north, surf_adj_next, diag, land, bottom):
    levels, rows, cols = tracer.shape
    size = lax.axis_size("row") * lax.axis_size("col")
    g, c = tracer_adj_next, tracer
    dma = pltpu.SemaphoreType.DMA
    two, side = (rows, cols), (rows + 8, 128)
    whole = lambda kind=F32: pltpu.VMEM(two, kind)
    edges = [pltpu.VMEM((levels, 8, cols), F32)] * 4 + [pltpu.VMEM((8, cols), jnp.int32)] * 4 + [pltpu.VMEM((8, cols), F32)] * 6
    row_a, row_b = call(
        pack_rows, [HBM] * 7, [(VMEM, (32, cols))] * 2, edges + [dma((14,))], name="pack_rows"
    )(g, c, land, bottom, surf_adj_next, diag, v_north)
    row_far = lax.ppermute(row_b, "row", swap_pairs("row", 1))
    deep = pltpu.VMEM(g.shape, F32)
    a, b, row_a = call(
        pack_cols,
        [VMEM] * 8,
        [(VMEM, (rows, 128))] * 2 + [(VMEM, (32, cols))],
        name="pack_cols",
        cost=pl.CostEstimate(flops=g.size, bytes_accessed=g.size, transcendentals=0),
    )(g, c, land, bottom, surf_adj_next, diag, u_east, row_a)
    row_near = lax.ppermute(row_a, "row", swap_pairs("row", 0))
    row_sent, row_got = (row_a, row_b), (row_near, row_far)
    (b,) = call(functools.partial(join_cols, False), [VMEM] * 3, [(VMEM, side)], name="join_far")(b, *row_got)
    far = lax.ppermute(b, "col", swap_pairs("col", 1))
    *fields, rs, codes, diags = call(
        rhs_rows,
        [VMEM] * 10,
        [(VMEM, (rows + 8, cols))] * 3 + [(VMEM, side)] * 3,
        name="rhs_rows",
        cost=pl.CostEstimate(flops=24 * g.size, bytes_accessed=8 * g.size, transcendentals=0),
    )(g, c, land, bottom, surf_adj_next, diag, *row_sent, *row_got)
    (a,) = call(functools.partial(join_cols, True), [VMEM] * 4, [(VMEM, side)], name="join_near")(a, *row_got, rs)
    near = lax.ppermute(a, "col", swap_pairs("col", 0))
    col_sent, col_got = (a, b), (near, far)
    r, p1, p2, mom = call(
        inner,
        [VMEM] * 3,
        [(HBM, two)] + [(VMEM, two)] * 2 + [(VMEM, (48, 128))],
        [dma],
        name="inner",
        cost=pl.CostEstimate(flops=12 * g.size, bytes_accessed=4 * g.size, transcendentals=0),
    )(*fields)
    *sides, mom = call(outer, [VMEM] * 8, [(VMEM, side)] * 3 + [(VMEM, (size, 128))], name="outer")(
        rs, codes, diags, mom, *col_sent, *col_got
    )
    mom = lax.all_to_all(mom, ("row", "col"), 0, 0, tiled=True)
    (tracer_adj,) = call(
        tracer_kernel,
        [HBM] * 5 + [VMEM] * 4,
        [(HBM, g.shape)],
        [deep, whole(jnp.int32), whole(jnp.int32), whole(), whole(), deep, dma((4,)), dma((levels,)), dma((levels,))],
        name="tracer",
        cost=pl.CostEstimate(flops=20 * g.size, bytes_accessed=12 * g.size, transcendentals=0),
    )(g, land, bottom, u_east, v_north, *row_got, *col_got)
    (surf_adj,) = call(
        combine,
        [VMEM] * 7,
        [(HBM, two)],
        [whole(), dma((2,))],
        name="combine",
    )(mom, r, p1, p2, *sides)
    return tracer_adj, surf_adj


def solution(mesh):
    three, two = P(None, "row", "col"), P("row", "col")
    return jax.shard_map(
        shards,
        mesh=mesh,
        in_specs=(three, three, two, two, two, two, two, two),
        out_specs=(three, two),
        check_vma=False,
    )
```

time: 45.2 us -> 42.4 us (0.938)
  Pallas kernels: 18.8 us -> 14.5 us
  waiting for transfers between devices: 4.18 us -> 6.14 us
  starting transfers between devices: 21.3 us -> 20.7 us
    pallas_call x7 -> x9, Pallas kernels: 18.8 us -> 14.5 us  [call(): run(*[pltpu.with_memory_space_constraint(x, spec.memory_space) for x, spe...]
    all_to_all x1, starting transfers between devices: 12.8 us -> 8.74 us  [shards(): mom = lax.all_to_all(mom, ('row', 'col'), 0, 0, tiled=True)]
    ppermute x4, starting transfers between devices: 8.44 us -> 11.9 us  [the longest x1 6.36 us: shards(): far = lax.ppermute(b, 'col', swap_pairs('col', 1))]
    ppermute x4, waiting for transfers between devices: 0.01 us -> 1.96 us  [the longest x1 1.65 us: shards(): row_near = lax.ppermute(row_a, 'row', swap_pairs('row', 0))]
  transfers between devices with their start and end apart: 5 -> 5, of which waited for: 1 -> 3; matrix products, arithmetic and copies ran while one was open for 0% -> 0% of each run, Pallas kernels for 28% -> 22%
where the time goes in v5:
time: 42.4 us; the launch traced here: 42.2 us
  starting transfers between devices  20.7 us (49%)
  Pallas kernels  14.5 us (34%)
  waiting for transfers between devices  6.14 us (14%)
  between operations  0.83 us (2%)
    pallas_call x9, Pallas kernels, call(): run(*[pltpu.with_memory_space_constraint(x, spec.memory_space) for x, spe...  14.5 us
    all_to_all x1, starting transfers between devices, shards(): mom = lax.all_to_all(mom, ('row', 'col'), 0, 0, tiled=True)  8.74 us
    ppermute x1, starting transfers between devices, shards(): far = lax.ppermute(b, 'col', swap_pairs('col', 1))  6.36 us
    ppermute x1, starting transfers between devices, shards(): row_near = lax.ppermute(row_a, 'row', swap_pairs('row', 0))  4.67 us
    all_to_all x1, waiting for transfers between devices, shards(): mom = lax.all_to_all(mom, ('row', 'col'), 0, 0, tiled=True)  4.18 us
    ppermute x1, waiting for transfers between devices, shards(): row_near = lax.ppermute(row_a, 'row', swap_pairs('row', 0))  1.65 us
  transfers between devices with their start and end apart: 5, of which 3 were waited for; matrix products, arithmetic and copies ran while one was open for 0% of the time, Pallas kernels for 22%

profile of v5, /device:TPU:1, one launch (start us, length us, event | category | flops | bytes accessed | tf_op | source)
XLA Modules:
  0.0 42.2 jit_solution(9391784580542665347)
XLA Ops:
  0.6 0.0 copy-start.3
  0.6 0.0 copy-start.2
  0.7 0.0 copy-start
  0.7 0.0 copy-start.5
  0.7 0.0 copy-start.6
  0.7 1.8 %pack_rows.1 = (f32[32,512]{1,0:T(8,128)S(1)}, f32[32,512]{1,0:T(8,128)S(1)}) custom-call(f32[8,128,512]{2,1,0:T(8,128)} %g_in.1, f32[8,128,512]{2,1,0:T(8,128)} %c.5, s32[128,512]{1,0:T(8,128)} %land_in.1, s32[128,512]{1,0:T(8,128)} %bottom_in.1, f32[128,512]{1,0:T(8,128)} %surf.5, f32[128,512]{1,0:T(8,128)} %diag.5, f32[128,512]{1,0:T(8,128)} %v_in.1), custom_call_target="tpu_custom_call" | custom-call | tf_op jit(solution)/shard_map/pack_rows/pallas_call | solution.py:495
  2.6 0.8 %collective-permute-start.1 = (f32[32,512]{1,0:T(8,128)S(1)}, f32[32,512]{1,0:T(8,128)S(1)}, u32[]{:S(2)}, u32[]{:S(2)}) collective-permute-start(f32[32,512]{1,0:T(8,128)S(1)} %get-tuple-element.23.sent_b), channel_id=1, source_target_pairs={{16,32},{32,16},{48,64},{64,48},{80,96},{96,80},{17,33},{33,17},{4... | collective-permute-start | bytes 196616 | tf_op jit(solution)/shard_map/ppermute | solution.py:509
  3.4 0.1 copy-done.1
  3.5 1.0 %pack_cols.1 = (f32[128,128]{1,0:T(8,128)S(1)}, f32[128,128]{1,0:T(8,128)S(1)}, f32[32,512]{1,0:T(8,128)S(1)}) custom-call(f32[8,128,512]{2,1,0:T(8,128)S(1)} %copy-done, f32[8,128,512]{2,1,0:T(8,128)S(1)} %copy-done.1, s32[128,512]{1,0:T(8,128)S(1)} %copy-done.2, s32[128,512]{1,0:T(8,128)S(1)} %copy-done.3, f32[128,512]{1,0:T(8,128)S(1)} %copy-done.4, ...), custom_call_target="tpu_custom_call" | custom-call | flops 524288 | bytes 524288 | tf_op jit(solution)/shard_map/pack_cols/pallas_call | solution.py:495
  4.5 4.7 %collective-permute-start = (f32[32,512]{1,0:T(8,128)S(1)}, f32[32,512]{1,0:T(8,128)S(1)}, u32[]{:S(2)}, u32[]{:S(2)}) collective-permute-start(f32[32,512]{1,0:T(8,128)S(1)} %get-tuple-element.22.sent_a), channel_id=1, source_target_pairs={{0,16},{16,0},{32,48},{48,32},{64,80},{80,64},{96,112},{112,96},{1... | collective-permute-start | bytes 196616 | tf_op jit(solution)/shard_map/ppermute | solution.py:518
  9.2 0.0 collective-permute-done.1.far.rf
  9.2 1.7 %collective-permute-done.near.rn = f32[32,512]{1,0:T(8,128)S(1)} collective-permute-done((f32[32,512]{1,0:T(8,128)S(1)}, f32[32,512]{1,0:T(8,128)S(1)}, u32[]{:S(2)}, u32[]{:S(2)}) %collective-permute-start) | collective-permute-done | bytes 65568 | tf_op jit(solution)/shard_map/ppermute | solution.py:518
  10.9 6.4 %collective-permute-start.3 = (f32[136,128]{1,0:T(8,128)S(1)}, f32[136,128]{1,0:T(8,128)S(1)}, u32[]{:S(2)}, u32[]{:S(2)}) collective-permute-start(f32[136,128]{1,0:T(8,128)S(1)} %join_far.1.sent_b), channel_id=1, source_target_pairs={{1,2},{2,1},{3,4},{4,3},{5,6},{6,5},{7,8},{8,7},{9,10},{10,9},{11,... | collective-permute-start | bytes 208904 | tf_op jit(solution)/shard_map/ppermute | solution.py:521
  17.2 2.1 %rhs_rows.1 = (f32[136,512]{1,0:T(8,128)S(1)}, f32[136,512]{1,0:T(8,128)S(1)}, f32[136,512]{1,0:T(8,128)S(1)}, f32[136,128]{1,0:T(8,128)S(1)}, f32[136,128]{1,0:T(8,128)S(1)}, /*index=5*/f32[136,128]{1,0:T(8,128)S(1)}) custom-call(f32[8,128,512]{2,1,0:T(8,128)S(1)} %copy-done, f32[8,128,512]{2,1,0:T(8,128)S(1)} %copy-done.1, s32[128,512]{1,0:T(8,128)S(1)} %copy-done.2, ...), custom_call_target="tpu_custom_call" | custom-call | flops 12582912 | bytes 4194304 | tf_op jit(solution)/shard_map/rhs_rows/pallas_call | solution.py:495
  19.4 0.1 collective-permute-start.2
  19.4 0.9 %inner.1 = (f32[128,512]{1,0:T(8,128)}, f32[128,512]{1,0:T(8,128)S(1)}, f32[128,512]{1,0:T(8,128)S(1)}, f32[48,128]{1,0:T(8,128)S(1)}) custom-call(f32[136,512]{1,0:T(8,128)S(1)} %get-tuple-element.29.r_in, f32[136,512]{1,0:T(8,128)S(1)} %get-tuple-element.30.code_in, f32[136,512]{1,0:T(8,128)S(1)} %get-tuple-element.31.diag_in), custom_call_target="tpu_custom_call" | custom-call | flops 6291456 | bytes 2097152 | tf_op jit(solution)/shard_map/inner/pallas_call | solution.py:495
  20.4 0.0 collective-permute-done.3.cf.far
  20.4 0.3 collective-permute-done.2.cn.near
  20.7 2.0 %outer.1 = (f32[136,128]{1,0:T(8,128)S(1)}, f32[136,128]{1,0:T(8,128)S(1)}, f32[136,128]{1,0:T(8,128)S(1)}, f32[128,128]{1,0:T(8,128)}) custom-call(f32[136,128]{1,0:T(8,128)S(1)} %get-tuple-element.25.refs_0_.rs, f32[136,128]{1,0:T(8,128)S(1)} %get-tuple-element.27.codes, f32[136,128]{1,0:T(8,128)S(1)} %get-tuple-element.28.diags, ...), custom_call_target="tpu_custom_call" | custom-call | tf_op jit(solution)/shard_map/outer/pallas_call | solution.py:495
  22.7 8.7 %all-to-all-start = ((f32[128,1,128]{2,1,0:T(1,128)}), f32[128,1,128]{2,1,0:T(1,128)S(1)}, u32[]{:S(2)}, u32[]{:S(2)}) async-start(f32[128,1,128]{2,1,0:T(1,128)} %bitcast.1), calls=%async_computation | async-start | bytes 131072 | tf_op jit(solution)/shard_map/all_to_all | solution.py:543
  31.4 0.0 copy-start.7
  31.4 5.4 %tracer.1 = f32[8,128,512]{2,1,0:T(8,128)} custom-call(f32[8,128,512]{2,1,0:T(8,128)} %g_in.1, s32[128,512]{1,0:T(8,128)} %land_in.1, s32[128,512]{1,0:T(8,128)} %bottom_in.1, f32[128,512]{1,0:T(8,128)} %u_in.1, f32[128,512]{1,0:T(8,128)} %v_in.1, f32[32,512]{1,0:T(8,128)S(1)} %collective-permute-done.near.rn, f32[32,512]{1,0:T(8,128)S(1)} %collective-permute-done.1.far.rf, ...), custom_call_target="tpu_custom_call" | custom-call | flops 10485760 | bytes 6291456 | tf_op jit(solution)/shard_map/tracer/pallas_call | solution.py:495
  36.9 4.2 %all-to-all-done = f32[128,1,128]{2,1,0:T(1,128)S(1)} async-done(((f32[128,1,128]{2,1,0:T(1,128)}), f32[128,1,128]{2,1,0:T(1,128)S(1)}, u32[]{:S(2)}, u32[]{:S(2)}) %all-to-all-start) | async-done | bytes 65568 | tf_op jit(solution)/shard_map/all_to_all | solution.py:543
  41.1 1.2 %combine.1 = f32[128,512]{1,0:T(8,128)} custom-call(f32[128,128]{1,0:T(8,128)S(1)} %bitcast.4, f32[128,512]{1,0:T(8,128)S(1)} %copy-done.7, f32[128,512]{1,0:T(8,128)S(1)} %get-tuple-element.35.p1, f32[128,512]{1,0:T(8,128)S(1)} %get-tuple-element.36.p2, f32[136,128]{1,0:T(8,128)S(1)} %get-tuple-element.37.rs, f32[136,128]{1,0:T(8,128)S(1)} %get-tuple-element.38.p1s, ...), custom_call_target="tpu_custom_call" | custom-call | tf_op jit(solution)/shard_map/combine/pallas_call | solution.py:495
  (11 shorter events, 0.1 us)
Async XLA Ops:
  0.6 2.7 %copy-start.3 = (s32[128,512]{1,0:T(8,128)S(1)}, s32[128,512]{1,0:T(8,128)}, u32[]{:S(2)}) copy-start(s32[128,512]{1,0:T(8,128)} %bottom_in.1) | copy-start | bytes 786436
  0.6 2.7 %copy-start.2 = (s32[128,512]{1,0:T(8,128)S(1)}, s32[128,512]{1,0:T(8,128)}, u32[]{:S(2)}) copy-start(s32[128,512]{1,0:T(8,128)} %land_in.1) | copy-start | bytes 786436
  0.7 2.7 %copy-start = (f32[8,128,512]{2,1,0:T(8,128)S(1)}, f32[8,128,512]{2,1,0:T(8,128)}, u32[]{:S(2)}) copy-start(f32[8,128,512]{2,1,0:T(8,128)} %g_in.1) | copy-start | bytes 6291460
  0.7 2.7 %copy-start.5 = (f32[128,512]{1,0:T(8,128)S(1)}, f32[128,512]{1,0:T(8,128)}, u32[]{:S(2)}) copy-start(f32[128,512]{1,0:T(8,128)} %diag.5) | copy-start | bytes 786436
  0.7 2.7 %copy-start.4 = (f32[128,512]{1,0:T(8,128)S(1)}, f32[128,512]{1,0:T(8,128)}, u32[]{:S(2)}) copy-start(f32[128,512]{1,0:T(8,128)} %surf.5) | copy-start | bytes 786436
  0.7 2.8 %copy-start.1 = (f32[8,128,512]{2,1,0:T(8,128)S(1)}, f32[8,128,512]{2,1,0:T(8,128)}, u32[]{:S(2)}) copy-start(f32[8,128,512]{2,1,0:T(8,128)} %c.5) | copy-start | bytes 6291460
  0.7 2.8 %copy-start.6 = (f32[128,512]{1,0:T(8,128)S(1)}, f32[128,512]{1,0:T(8,128)}, u32[]{:S(2)}) copy-start(f32[128,512]{1,0:T(8,128)} %u_in.1) | copy-start | bytes 786436
  2.6 6.6 %collective-permute-start.1 = (f32[32,512]{1,0:T(8,128)S(1)}, f32[32,512]{1,0:T(8,128)S(1)}, u32[]{:S(2)}, u32[]{:S(2)}) collective-permute-start(f32[32,512]{1,0:T(8,128)S(1)} %get-tuple-element.23.sent_b), channel_id=1, source_target_pairs={{16,32},{32,16},{48,64},{64,48},{80,96},{96,80},{17,33},{33,17},{4... | collective-permute-start | bytes 196616 | tf_op jit(solution)/shard_map/ppermute | solution.py:509
  4.5 6.3 %collective-permute-start = (f32[32,512]{1,0:T(8,128)S(1)}, f32[32,512]{1,0:T(8,128)S(1)}, u32[]{:S(2)}, u32[]{:S(2)}) collective-permute-start(f32[32,512]{1,0:T(8,128)S(1)} %get-tuple-element.22.sent_a), channel_id=1, source_target_pairs={{0,16},{16,0},{32,48},{48,32},{64,80},{80,64},{96,112},{112,96},{1... | collective-permute-start | bytes 196616 | tf_op jit(solution)/shard_map/ppermute | solution.py:518
  10.9 9.5 %collective-permute-start.3 = (f32[136,128]{1,0:T(8,128)S(1)}, f32[136,128]{1,0:T(8,128)S(1)}, u32[]{:S(2)}, u32[]{:S(2)}) collective-permute-start(f32[136,128]{1,0:T(8,128)S(1)} %join_far.1.sent_b), channel_id=1, source_target_pairs={{1,2},{2,1},{3,4},{4,3},{5,6},{6,5},{7,8},{8,7},{9,10},{10,9},{11,... | collective-permute-start | bytes 208904 | tf_op jit(solution)/shard_map/ppermute | solution.py:521
  19.4 1.3 %collective-permute-start.2 = (f32[136,128]{1,0:T(8,128)S(1)}, f32[136,128]{1,0:T(8,128)S(1)}, u32[]{:S(2)}, u32[]{:S(2)}) collective-permute-start(f32[136,128]{1,0:T(8,128)S(1)} %join_near.1.sent_a), channel_id=1, source_target_pairs={{0,1},{1,0},{2,3},{3,2},{4,5},{5,4},{6,7},{7,6},{8,9},{9,8},{10,11... | collective-permute-start | bytes 208904 | tf_op jit(solution)/shard_map/ppermute | solution.py:530
  22.7 18.4 %all-to-all-start = ((f32[128,1,128]{2,1,0:T(1,128)}), f32[128,1,128]{2,1,0:T(1,128)S(1)}, u32[]{:S(2)}, u32[]{:S(2)}) async-start(f32[128,1,128]{2,1,0:T(1,128)} %bitcast.1), calls=%async_computation | async-start | bytes 131072 | tf_op jit(solution)/shard_map/all_to_all | solution.py:543
  31.4 9.6 %copy-start.7 = (f32[128,512]{1,0:T(8,128)S(1)}, f32[128,512]{1,0:T(8,128)}, u32[]{:S(2)}) copy-start(f32[128,512]{1,0:T(8,128)} %get-tuple-element.34.r) | copy-start | bytes 786436

commit v6 on v5

--- a/solution.py
+++ b/solution.py
@@ -88,14 +88,23 @@
     cols = surf.shape[1]
     lane, sub = iota((8, cols), 1), iota((8, cols), 0)
     upper = sub < DEEP
-
-    def tiles(g, c, land, bottom, surf, diag, v, of_last):
-        code = code_of(land[...], bottom[...])
+    codes = [code_of(l0[...], b0[...]), code_of(l1[...], b1[...])]
+    both = [jnp.where(upper, g0[k], g1[k]) for k in range(LEV)], [jnp.where(upper, c0[k], c1[k]) for k in range(LEV)]
+    code = jnp.where(upper, *codes)
+    cu = jnp.where(lane < cols - 1, jnp.minimum(code, next_col(code)), 0.0)
+    ub = faces(*both, cu, next_col)
+    ub = ub - prev_col(ub)
+    corners = []
+    for high, lanes in ((False, slice(0, 128)), (True, slice(cols - 128, cols))):
+        cut = lambda xs: [x[:, lanes] for x in xs]
+        rest = [jnp.where(upper, s0[...], s1[...]), jnp.where(upper, d0[...], d1[...])]
+        corners.append(lane_pack(cut(both[0]), cut(both[1]), code[:, lanes], cut(rest), high))
+
+    def tiles(g, c, code, surf, diag, v, of_last):
         g, c = [g[k] for k in range(LEV)], [c[k] for k in range(LEV)]
-        cu = jnp.where(lane < cols - 1, jnp.minimum(code, next_col(code)), 0.0)
         cv = jnp.where(sub < 7, jnp.minimum(code, next_row(code)), 0.0)
-        ub, vb = faces(g, c, cu, cv)
-        rhs = surf[...] + 0.0625 * ((ub - prev_col(ub)) + (vb - prev_row(vb)))
+        vb = faces(g, c, cv, next_row)
+        rhs = surf[...] + 0.0625 * (ub + (vb - prev_row(vb)))
         edge = 7 if of_last else 0
 
         def outermost(x):
@@ -107,28 +116,26 @@
         half = DEEP if of_last else 0
         one = jnp.where(upper, turn(rhs, half, 0), turn(code, DEEP - half, 0))
         two = jnp.where(upper, turn(diag[...], half, 0), turn(v[...], DEEP - edge, 0))
-        ends = []
-        for high, lanes in ((False, slice(0, 128)), (True, slice(cols - 128, cols))):
-            cut = lambda xs: [x[:, lanes] for x in xs]
-            corner = lane_pack(cut(g), cut(c), code[:, lanes], cut([surf, diag]), high)
-            ends.append(jnp.where(sub[:, :128] < 5, two[:, lanes], corner if of_last else turn(corner, 5, 0)))
+        ends = [
+            jnp.where(sub[:, :128] < 5, two[:, lanes], corner if of_last else turn(corner, 5, 0))
+            for corner, lanes in zip(corners, (slice(0, 128), slice(cols - 128, cols)))
+        ]
         two = jnp.concatenate([ends[0], two[:, 128 : cols - 128], ends[1]], axis=1)
         return outermost(g), outermost(c), one, two
 
-    first = tiles(g0, c0, l0, b0, s0, d0, v0, False)
-    last = tiles(g1, c1, l1, b1, s1, d1, v1, True)
+    first = tiles(g0, c0, codes[0], s0, d0, v0, False)
+    last = tiles(g1, c1, codes[1], s1, d1, v1, True)
     even = is_even("row")
     for t in range(4):
         a_ref[8 * t : 8 * t + 8, :], b_ref[8 * t : 8 * t + 8, :] = pick(even, last[t], first[t])
 
 
-def faces(g, c, cu, cv):
-    ub, vb = jnp.zeros_like(cu), jnp.zeros_like(cv)
+def faces(g, c, coupling, step):
+    total = jnp.zeros_like(coupling)
     for k in range(LEV):
         gk, ck = g[k], c[k]
-        ub = ub + jnp.where(cu > k + 0.5, next_col(gk) - gk, 0.0) * (next_col(ck) + ck)
-        vb = vb + jnp.where(cv > k + 0.5, next_row(gk) - gk, 0.0) * (next_row(ck) + ck)
-    return ub, vb
+        total = total + jnp.where(coupling > k + 0.5, step(gk) - gk, 0.0) * (step(ck) + ck)
+    return total
 
 
 def operator(cu, cv, dg):
@@ -163,10 +170,12 @@
     group = iota(code.shape, 1) // DEEP
     base, one, two = (DEEP, 0, 1) if of_last else (0, 1, 0)
     places = [(g[k], 2 * k + one) for k in range(LEV)] + [(c[k], 16 + 2 * k + one) for k in range(LEV)]
-    places += [(code, 2 * k + two) for k in range(LEV)] + [(x, 16 + 2 * n + two) for n, x in enumerate(rest)]
+    places += [(x, 16 + 2 * n + two) for n, x in enumerate(rest)]
     if of_last:
         places.append((code, 31))
-    out = jnp.zeros_like(code)
+    out = jnp.where(group == two, turn(code, DEEP * two + base, 1), 0.0)
+    for by in (8, 16, 32):
+        out = out + turn(out, by, 1)
     for x, at in places:
         out = jnp.where(group == at, turn(x, DEEP * at + base, 1), out)
     return out
@@ -215,12 +224,20 @@
     out[rows:, :] = pick(is_even("col"), *packs)[0 if of_near else 1]
 
 
-def rhs_rows(g, c, land, bottom, surf, diag, sent_a, sent_b, near, far, r_ref, code_ref, diag_ref, rs_ref, codes_ref, diags_ref):
+def local_rhs(g, c, land, bottom, surf, r_ref, code_ref):
     rows, cols = surf.shape
+    code = code_of(land[...], bottom[...])
+    code_ref[...] = code
+    cu = jnp.where(iota(code.shape, 1) < cols - 1, jnp.minimum(code, next_col(code)), 0.0)
+    cv = jnp.where(iota(code.shape, 0) < rows - 1, jnp.minimum(code, next_row(code)), 0.0)
+    ub, vb = faces(g, c, cu, next_col), faces(g, c, cv, next_row)
+    r_ref[...] = surf[...] + 0.0625 * ((ub - prev_col(ub)) + (vb - prev_row(vb)))
+
+
+def inner(r_in, code_in, diag, sent_a, sent_b, near, far, r_ref, p1_ref, p2_ref, mom_ref, rs_ref, codes_ref, diags_ref, r_own, sem):
+    rows, cols = diag.shape
     even = is_even("row")
     lane, sub = iota((8, cols), 1), iota((8, cols), 0)
-    upper = sub < DEEP
-
     high, low = pick(even, sent_a[...], sent_b[...])
     north, south = pick(even, near[...], far[...])
 
@@ -236,32 +253,21 @@
     down = across(south, low, 7, 4)
     halo = row_halo(near, far, slice(0, cols))
     r_halo = halo(RHS) + jnp.where(sub == 0, -up, jnp.where(sub == 7, down, 0.0))
-    code = code_of(land[...], bottom[...])
-    cu = jnp.where(iota(code.shape, 1) < cols - 1, jnp.minimum(code, next_col(code)), 0.0)
-    cv = jnp.where(iota(code.shape, 0) < rows - 1, jnp.minimum(code, next_row(code)), 0.0)
-    ub, vb = faces(g, c, cu, cv)
-    r = surf[...] + 0.0625 * ((ub - prev_col(ub)) + (vb - prev_row(vb)))
-    low = r[:8] - jnp.where(sub == 0, down, 0.0)
-    high = r[rows - 8 :] + jnp.where(sub == 7, up, 0.0)
-    r = jnp.concatenate([low, r[8 : rows - 8], high, r_halo], axis=0)
-    code = jnp.concatenate([code, halo(CODE)], axis=0)
+    low = r_in[:8] - jnp.where(sub == 0, down, 0.0)
+    high = r_in[rows - 8 :] + jnp.where(sub == 7, up, 0.0)
+    r = jnp.concatenate([low, r_in[8 : rows - 8], high, r_halo], axis=0)
+    r_own[...] = r[:rows]
+    copy = pltpu.make_async_copy(r_own, r_ref, sem)
+    copy.start()
+    code = jnp.concatenate([code_in[...], halo(CODE)], axis=0)
     dg = jnp.concatenate([diag[...], halo(DIAG)], axis=0)
     left = iota((rows + 8, 128), 1) < 64
     for x, ref in ((r, rs_ref), (code, codes_ref), (dg, diags_ref)):
         ref[...] = jnp.where(left, turn(x[:, cols - 128 :], -68, 1), turn(x[:, :128], 68, 1))
-    r_ref[...] = r
-    code_ref[...] = code
-    diag_ref[...] = dg
-
-
-def inner(r_in, code_in, diag_in, r_ref, p1_ref, p2_ref, mom_ref, sem):
-    rows, cols = p1_ref.shape
-    copy = pltpu.make_async_copy(r_in.at[:rows, :], r_ref, sem)
-    copy.start()
-    code = 0.125 * code_in[...]
+    code = 0.125 * code
     cu = jnp.where(iota(code.shape, 1) < cols - 1, jnp.minimum(code, next_col(code)), 0.0)
     cv = jnp.minimum(code, next_row(code))
-    p1, p2, prods = products(r_in[...], cu, cv, diag_in[...], rows)
+    p1, p2, prods = products(r, cu, cv, dg, rows)
     p1_ref[...] = p1[:rows]
     p2_ref[...] = p2[:rows]
     lane = iota((8, 128), 1)
@@ -291,41 +297,33 @@
     lane = iota(high.shape, 1)
     place = lane % 8
     own, left = place < DEEP, lane < 64
-    level = (lane // 8).astype(F32) + 0.5
-
-    def rhs_terms(first, second, u_from, v_from):
-        gc = jnp.where(own, first, second)
-        mixed = jnp.where(own, second, first)
-        code = turn(mixed, 4, 1)
-        one, two = turn(gc, -1, 1) - gc, turn(gc, 63, 1) + turn(gc, 64, 1)
-        keep = (place >= u_from) & (place < u_from + 4)
-        open_u = (jnp.minimum(code, turn(mixed, 3, 1)) > level) & keep
-        ub = jnp.where(open_u, one, 0.0) * two
-        one, two = gc - turn(gc, 1, 1), turn(gc, 64, 1) + turn(gc, 65, 1)
-        keep = (place > u_from) & (place <= u_from + 4)
-        open_u = (jnp.minimum(code, turn(mixed, 5, 1)) > level) & keep
-        ub = ub - jnp.where(open_u, one, 0.0) * two
-        keep = (place >= v_from) & (place < v_from + 4)
-        open_v = (jnp.minimum(code, next_row(code)) > level) & keep
-        c = turn(gc, 64, 1)
-        vb = jnp.where(open_v, next_row(gc) - gc, 0.0) * (next_row(c) + c)
-        return ub + (vb - prev_row(vb))
-
-    at_east = rhs_terms(high, east, 3, 4)
+    at_east, at_west = jnp.where(own, high, east), jnp.where(own, west, low)
+
+    def shared(op):
+        minus, plus = [op(x) - x for x in (at_east, at_west)], [op(x) + x for x in (at_east, at_west)]
+        return jnp.where(left, minus[0], turn(minus[1], 64, 1)), jnp.where(left, turn(plus[0], 64, 1), plus[1])
+
+    code = jnp.where(left, turn(jnp.where(own, east, high), 4, 1), turn(jnp.where(own, low, west), 68, 1))
+    level = ((lane % 64) // 8).astype(F32) + 0.5
+    side = jnp.where(left, 0, 4)
+    keep_u = (place + side >= 3 + side // 4) & (place + side < 7 + side // 4)
+    keep_v = (place + side >= 4) & (place + side < 8)
+    one, two = shared(next_col)
+    ub = jnp.where((jnp.minimum(code, next_col(code)) > level) & keep_u, one, 0.0) * two
+    one, two = shared(next_row)
+    vb = jnp.where((jnp.minimum(code, next_row(code)) > level) & keep_v, one, 0.0) * two
+    total = 0.0625 * ((ub - prev_col(ub)) + (vb - prev_row(vb)))
     for by in (8, 16, 32):
-        at_east = at_east + turn(at_east, by, 1)
-    at_west = rhs_terms(west, low, 0, 0)
-    at_west = turn(at_west, 64, 1) + turn(at_west, 56, 1)
-    for by in (16, 32):
-        at_west = at_west + turn(at_west, -by, 1)
-
-    def filled(x, e, w):
-        return jnp.where((lane < 60) | (lane >= 68), x, jnp.where(left, e, w))
-
-    added = jnp.where((lane >= 59) & (lane < 69), jnp.where(left, at_east, at_west), 0.0)
-    r = filled(rs[...], turn(east, -4, 1), turn(west, -4, 1)) + 0.0625 * added
-    code = 0.125 * filled(codes[...], turn(east, 4, 1), turn(west, 4, 1))
-    dg = filled(diags[...], turn(east, -12, 1), turn(west, -12, 1))
+        total = total + turn(total, -by, 1)
+
+    def filled(x, at):
+        return jnp.where((lane < 60) | (lane >= 68), x, turn(came, 60 - at, 1))
+
+    came = jnp.where(own, east, west)
+    added = jnp.where((lane >= 59) & (lane < 69), jnp.where(left, turn(total, 56, 1), total), 0.0)
+    r = filled(rs[...], 64) + added
+    code = 0.125 * filled(codes[...], 56)
+    dg = filled(diags[...], 72)
     cu, cv = jnp.minimum(code, next_col(code)), jnp.minimum(code, next_row(code))
     p1, p2, prods = products(r, cu, cv, dg, rows)
     r_ref[...] = r
@@ -517,26 +515,26 @@
     )(g, c, land, bottom, surf_adj_next, diag, u_east, row_a)
     row_near = lax.ppermute(row_a, "row", swap_pairs("row", 0))
     row_sent, row_got = (row_a, row_b), (row_near, row_far)
+    rhs, code = call(
+        local_rhs,
+        [VMEM] * 5,
+        [(VMEM, two)] * 2,
+        name="local_rhs",
+        cost=pl.CostEstimate(flops=24 * g.size, bytes_accessed=8 * g.size, transcendentals=0),
+    )(g, c, land, bottom, surf_adj_next)
     (b,) = call(functools.partial(join_cols, False), [VMEM] * 3, [(VMEM, side)], name="join_far")(b, *row_got)
     far = lax.ppermute(b, "col", swap_pairs("col", 1))
-    *fields, rs, codes, diags = call(
-        rhs_rows,
-        [VMEM] * 10,
-        [(VMEM, (rows + 8, cols))] * 3 + [(VMEM, side)] * 3,
-        name="rhs_rows",
+    r, p1, p2, mom, rs, codes, diags = call(
+        inner,
+        [VMEM] * 7,
+        [(HBM, two)] + [(VMEM, two)] * 2 + [(VMEM, (48, 128))] + [(VMEM, side)] * 3,
+        [whole(), dma],
+        name="inner",
         cost=pl.CostEstimate(flops=24 * g.size, bytes_accessed=8 * g.size, transcendentals=0),
-    )(g, c, land, bottom, surf_adj_next, diag, *row_sent, *row_got)
+    )(rhs, code, diag, *row_sent, *row_got)
     (a,) = call(functools.partial(join_cols, True), [VMEM] * 4, [(VMEM, side)], name="join_near")(a, *row_got, rs)
     near = lax.ppermute(a, "col", swap_pairs("col", 0))
     col_sent, col_got = (a, b), (near, far)
-    r, p1, p2, mom = call(
-        inner,
-        [VMEM] * 3,
-        [(HBM, two)] + [(VMEM, two)] * 2 + [(VMEM, (48, 128))],
-        [dma],
-        name="inner",
-        cost=pl.CostEstimate(flops=12 * g.size, bytes_accessed=4 * g.size, transcendentals=0),
-    )(*fields)
     *sides, mom = call(outer, [VMEM] * 8, [(VMEM, side)] * 3 + [(VMEM, (size, 128))], name="outer")(
         rs, codes, diags, mom, *col_sent, *col_got
     )

time: 42.4 us -> 42 us (level)
  waiting for transfers between devices: 6.14 us -> 5.46 us
    ppermute x1, waiting for transfers between devices: 1.65 us -> 0.03 us  [shards(): row_near = lax.ppermute(row_a, 'row', swap_pairs('row', 0))]
    ppermute x1, waiting for transfers between devices: 0.31 us -> 1 us  [shards(): near = lax.ppermute(a, 'col', swap_pairs('col', 0))]
    all_to_all x1, starting transfers between devices: 8.74 us -> 9.27 us  [shards(): mom = lax.all_to_all(mom, ('row', 'col'), 0, 0, tiled=True)]
  transfers between devices with their start and end apart: 5 -> 5, of which waited for: 3 -> 3; matrix products, arithmetic and copies ran while one was open for 0% -> 0% of each run, Pallas kernels for 22% -> 23%
where the time goes in v6:
time: 42 us; the launch traced here: 41.8 us
  starting transfers between devices  21 us (50%)
  Pallas kernels  14.2 us (34%)
  waiting for transfers between devices  5.46 us (13%)
  between operations  0.83 us (2%)
    pallas_call x9, Pallas kernels, call(): run(*[pltpu.with_memory_space_constraint(x, spec.memory_space) for x, spe...  14.2 us
    all_to_all x1, starting transfers between devices, shards(): mom = lax.all_to_all(mom, ('row', 'col'), 0, 0, tiled=True)  9.27 us
    ppermute x1, starting transfers between devices, shards(): far = lax.ppermute(b, 'col', swap_pairs('col', 1))  6.37 us
    ppermute x1, starting transfers between devices, shards(): row_near = lax.ppermute(row_a, 'row', swap_pairs('row', 0))  4.52 us
    all_to_all x1, waiting for transfers between devices, shards(): mom = lax.all_to_all(mom, ('row', 'col'), 0, 0, tiled=True)  4.17 us
    ppermute x1, waiting for transfers between devices, shards(): near = lax.ppermute(a, 'col', swap_pairs('col', 0))  1 us
  transfers between devices with their start and end apart: 5, of which 3 were waited for; matrix products, arithmetic and copies ran while one was open for 0% of the time, Pallas kernels for 23%

profile of v6, /device:TPU:1, one launch (start us, length us, event | category | flops | bytes accessed | tf_op | source)
XLA Modules:
  0.0 41.8 jit_solution(13100613836256315522)
XLA Ops:
  0.6 0.0 copy-start.3
  0.6 0.0 copy-start.2
  0.7 0.0 copy-start
  0.7 0.0 copy-start.5
  0.7 0.0 copy-start.6
  0.7 1.7 %pack_rows.1 = (f32[32,512]{1,0:T(8,128)S(1)}, f32[32,512]{1,0:T(8,128)S(1)}) custom-call(f32[8,128,512]{2,1,0:T(8,128)} %g_in.1, f32[8,128,512]{2,1,0:T(8,128)} %c.5, s32[128,512]{1,0:T(8,128)} %land_in.1, s32[128,512]{1,0:T(8,128)} %bottom_in.1, f32[128,512]{1,0:T(8,128)} %surf.5, f32[128,512]{1,0:T(8,128)} %diag.5, f32[128,512]{1,0:T(8,128)} %v_in.1), custom_call_target="tpu_custom_call" | custom-call | tf_op jit(solution)/shard_map/pack_rows/pallas_call | solution.py:493
  2.4 0.8 %collective-permute-start.1 = (f32[32,512]{1,0:T(8,128)S(1)}, f32[32,512]{1,0:T(8,128)S(1)}, u32[]{:S(2)}, u32[]{:S(2)}) collective-permute-start(f32[32,512]{1,0:T(8,128)S(1)} %get-tuple-element.22.sent_b), channel_id=1, source_target_pairs={{16,32},{32,16},{48,64},{64,48},{80,96},{96,80},{17,33},{33,17},{4... | collective-permute-start | bytes 196616 | tf_op jit(solution)/shard_map/ppermute | solution.py:507
  3.3 0.2 copy-done.1
  3.5 1.0 %pack_cols.1 = (f32[128,128]{1,0:T(8,128)S(1)}, f32[128,128]{1,0:T(8,128)S(1)}, f32[32,512]{1,0:T(8,128)S(1)}) custom-call(f32[8,128,512]{2,1,0:T(8,128)S(1)} %copy-done, f32[8,128,512]{2,1,0:T(8,128)S(1)} %copy-done.1, s32[128,512]{1,0:T(8,128)S(1)} %copy-done.2, s32[128,512]{1,0:T(8,128)S(1)} %copy-done.3, f32[128,512]{1,0:T(8,128)S(1)} %copy-done.4, ...), custom_call_target="tpu_custom_call" | custom-call | flops 524288 | bytes 524288 | tf_op jit(solution)/shard_map/pack_cols/pallas_call | solution.py:493
  4.5 4.5 %collective-permute-start = (f32[32,512]{1,0:T(8,128)S(1)}, f32[32,512]{1,0:T(8,128)S(1)}, u32[]{:S(2)}, u32[]{:S(2)}) collective-permute-start(f32[32,512]{1,0:T(8,128)S(1)} %get-tuple-element.21.sent_a), channel_id=1, source_target_pairs={{0,16},{16,0},{32,48},{48,32},{64,80},{80,64},{96,112},{112,96},{1... | collective-permute-start | bytes 196616 | tf_op jit(solution)/shard_map/ppermute | solution.py:516
  9.0 1.6 %local_rhs.1 = (f32[128,512]{1,0:T(8,128)S(1)}, f32[128,512]{1,0:T(8,128)S(1)}) custom-call(f32[8,128,512]{2,1,0:T(8,128)S(1)} %copy-done, f32[8,128,512]{2,1,0:T(8,128)S(1)} %copy-done.1, s32[128,512]{1,0:T(8,128)S(1)} %copy-done.2, s32[128,512]{1,0:T(8,128)S(1)} %copy-done.3, f32[128,512]{1,0:T(8,128)S(1)} %copy-done.4), custom_call_target="tpu_custom_call" | custom-call | flops 12582912 | bytes 4194304 | tf_op jit(solution)/shard_map/local_rhs/pallas_call | solution.py:493
  10.6 0.0 collective-permute-done.1.far.rf
  10.6 0.0 collective-permute-done.near.rn
  10.7 6.4 %collective-permute-start.3 = (f32[136,128]{1,0:T(8,128)S(1)}, f32[136,128]{1,0:T(8,128)S(1)}, u32[]{:S(2)}, u32[]{:S(2)}) collective-permute-start(f32[136,128]{1,0:T(8,128)S(1)} %join_far.1.sent_b), channel_id=1, source_target_pairs={{1,2},{2,1},{3,4},{4,3},{5,6},{6,5},{7,8},{8,7},{9,10},{10,9},{11,... | collective-permute-start | bytes 208904 | tf_op jit(solution)/shard_map/ppermute | solution.py:526
  17.0 1.6 %inner.1 = (f32[128,512]{1,0:T(8,128)}, f32[128,512]{1,0:T(8,128)S(1)}, f32[128,512]{1,0:T(8,128)S(1)}, f32[48,128]{1,0:T(8,128)S(1)}, f32[136,128]{1,0:T(8,128)...) custom-call(f32[128,512]{1,0:T(8,128)S(1)} %get-tuple-element.24.r_in, f32[128,512]{1,0:T(8,128)S(1)} %get-tuple-element.25.code_in, ...), custom_call_target="tpu_custom_call" | custom-call | flops 12582912 | bytes 4194304 | tf_op jit(solution)/shard_map/inner/pallas_call | solution.py:493
  18.7 0.1 collective-permute-start.2
  18.8 0.2 collective-permute-done.3.cf.far
  19.0 1.0 %collective-permute-done.2.cn.near = f32[136,128]{1,0:T(8,128)S(1)} collective-permute-done((f32[136,128]{1,0:T(8,128)S(1)}, f32[136,128]{1,0:T(8,128)S(1)}, u32[]{:S(2)}, u32[]{:S(2)}) %collective-permute-start.2) | collective-permute-done | bytes 69664 | tf_op jit(solution)/shard_map/ppermute | solution.py:536
  20.0 1.7 %outer.1 = (f32[136,128]{1,0:T(8,128)S(1)}, f32[136,128]{1,0:T(8,128)S(1)}, f32[136,128]{1,0:T(8,128)S(1)}, f32[128,128]{1,0:T(8,128)}) custom-call(f32[136,128]{1,0:T(8,128)S(1)} %get-tuple-element.26.refs_0_.rs, f32[136,128]{1,0:T(8,128)S(1)} %get-tuple-element.28.codes, f32[136,128]{1,0:T(8,128)S(1)} %get-tuple-element.29.diags, ...), custom_call_target="tpu_custom_call" | custom-call | tf_op jit(solution)/shard_map/outer/pallas_call | solution.py:493
  21.7 9.3 %all-to-all-start = ((f32[128,1,128]{2,1,0:T(1,128)}), f32[128,1,128]{2,1,0:T(1,128)S(1)}, u32[]{:S(2)}, u32[]{:S(2)}) async-start(f32[128,1,128]{2,1,0:T(1,128)} %bitcast.1), calls=%async_computation | async-start | bytes 131072 | tf_op jit(solution)/shard_map/all_to_all | solution.py:541
  31.0 0.0 copy-start.7
  31.0 5.4 %tracer.1 = f32[8,128,512]{2,1,0:T(8,128)} custom-call(f32[8,128,512]{2,1,0:T(8,128)} %g_in.1, s32[128,512]{1,0:T(8,128)} %land_in.1, s32[128,512]{1,0:T(8,128)} %bottom_in.1, f32[128,512]{1,0:T(8,128)} %u_in.1, f32[128,512]{1,0:T(8,128)} %v_in.1, f32[32,512]{1,0:T(8,128)S(1)} %collective-permute-done.near.rn, f32[32,512]{1,0:T(8,128)S(1)} %collective-permute-done.1.far.rf, ...), custom_call_target="tpu_custom_call" | custom-call | flops 10485760 | bytes 6291456 | tf_op jit(solution)/shard_map/tracer/pallas_call | solution.py:493
  36.4 4.2 %all-to-all-done = f32[128,1,128]{2,1,0:T(1,128)S(1)} async-done(((f32[128,1,128]{2,1,0:T(1,128)}), f32[128,1,128]{2,1,0:T(1,128)S(1)}, u32[]{:S(2)}, u32[]{:S(2)}) %all-to-all-start) | async-done | bytes 65568 | tf_op jit(solution)/shard_map/all_to_all | solution.py:541
  40.6 1.2 %combine.1 = f32[128,512]{1,0:T(8,128)} custom-call(f32[128,128]{1,0:T(8,128)S(1)} %bitcast.4, f32[128,512]{1,0:T(8,128)S(1)} %copy-done.7, f32[128,512]{1,0:T(8,128)S(1)} %get-tuple-element.33.p1, f32[128,512]{1,0:T(8,128)S(1)} %get-tuple-element.34.p2, f32[136,128]{1,0:T(8,128)S(1)} %get-tuple-element.35.rs, f32[136,128]{1,0:T(8,128)S(1)} %get-tuple-element.36.p1s, ...), custom_call_target="tpu_custom_call" | custom-call | tf_op jit(solution)/shard_map/combine/pallas_call | solution.py:493
  (11 shorter events, 0.1 us)
Async XLA Ops:
  0.6 2.6 %copy-start.3 = (s32[128,512]{1,0:T(8,128)S(1)}, s32[128,512]{1,0:T(8,128)}, u32[]{:S(2)}) copy-start(s32[128,512]{1,0:T(8,128)} %bottom_in.1) | copy-start | bytes 786436
  0.6 2.6 %copy-start.2 = (s32[128,512]{1,0:T(8,128)S(1)}, s32[128,512]{1,0:T(8,128)}, u32[]{:S(2)}) copy-start(s32[128,512]{1,0:T(8,128)} %land_in.1) | copy-start | bytes 786436
  0.7 2.6 %copy-start = (f32[8,128,512]{2,1,0:T(8,128)S(1)}, f32[8,128,512]{2,1,0:T(8,128)}, u32[]{:S(2)}) copy-start(f32[8,128,512]{2,1,0:T(8,128)} %g_in.1) | copy-start | bytes 6291460
  0.7 2.6 %copy-start.5 = (f32[128,512]{1,0:T(8,128)S(1)}, f32[128,512]{1,0:T(8,128)}, u32[]{:S(2)}) copy-start(f32[128,512]{1,0:T(8,128)} %diag.5) | copy-start | bytes 786436
  0.7 2.6 %copy-start.4 = (f32[128,512]{1,0:T(8,128)S(1)}, f32[128,512]{1,0:T(8,128)}, u32[]{:S(2)}) copy-start(f32[128,512]{1,0:T(8,128)} %surf.5) | copy-start | bytes 786436
  0.7 2.8 %copy-start.1 = (f32[8,128,512]{2,1,0:T(8,128)S(1)}, f32[8,128,512]{2,1,0:T(8,128)}, u32[]{:S(2)}) copy-start(f32[8,128,512]{2,1,0:T(8,128)} %c.5) | copy-start | bytes 6291460
  0.7 2.8 %copy-start.6 = (f32[128,512]{1,0:T(8,128)S(1)}, f32[128,512]{1,0:T(8,128)}, u32[]{:S(2)}) copy-start(f32[128,512]{1,0:T(8,128)} %u_in.1) | copy-start | bytes 786436
  2.4 8.2 %collective-permute-start.1 = (f32[32,512]{1,0:T(8,128)S(1)}, f32[32,512]{1,0:T(8,128)S(1)}, u32[]{:S(2)}, u32[]{:S(2)}) collective-permute-start(f32[32,512]{1,0:T(8,128)S(1)} %get-tuple-element.22.sent_b), channel_id=1, source_target_pairs={{16,32},{32,16},{48,64},{64,48},{80,96},{96,80},{17,33},{33,17},{4... | collective-permute-start | bytes 196616 | tf_op jit(solution)/shard_map/ppermute | solution.py:507
  4.5 6.2 %collective-permute-start = (f32[32,512]{1,0:T(8,128)S(1)}, f32[32,512]{1,0:T(8,128)S(1)}, u32[]{:S(2)}, u32[]{:S(2)}) collective-permute-start(f32[32,512]{1,0:T(8,128)S(1)} %get-tuple-element.21.sent_a), channel_id=1, source_target_pairs={{0,16},{16,0},{32,48},{48,32},{64,80},{80,64},{96,112},{112,96},{1... | collective-permute-start | bytes 196616 | tf_op jit(solution)/shard_map/ppermute | solution.py:516
  10.7 8.4 %collective-permute-start.3 = (f32[136,128]{1,0:T(8,128)S(1)}, f32[136,128]{1,0:T(8,128)S(1)}, u32[]{:S(2)}, u32[]{:S(2)}) collective-permute-start(f32[136,128]{1,0:T(8,128)S(1)} %join_far.1.sent_b), channel_id=1, source_target_pairs={{1,2},{2,1},{3,4},{4,3},{5,6},{6,5},{7,8},{8,7},{9,10},{10,9},{11,... | collective-permute-start | bytes 208904 | tf_op jit(solution)/shard_map/ppermute | solution.py:526
  18.7 1.3 %collective-permute-start.2 = (f32[136,128]{1,0:T(8,128)S(1)}, f32[136,128]{1,0:T(8,128)S(1)}, u32[]{:S(2)}, u32[]{:S(2)}) collective-permute-start(f32[136,128]{1,0:T(8,128)S(1)} %join_near.1.sent_a), channel_id=1, source_target_pairs={{0,1},{1,0},{2,3},{3,2},{4,5},{5,4},{6,7},{7,6},{8,9},{9,8},{10,11... | collective-permute-start | bytes 208904 | tf_op jit(solution)/shard_map/ppermute | solution.py:536
  21.7 18.9 %all-to-all-start = ((f32[128,1,128]{2,1,0:T(1,128)}), f32[128,1,128]{2,1,0:T(1,128)S(1)}, u32[]{:S(2)}, u32[]{:S(2)}) async-start(f32[128,1,128]{2,1,0:T(1,128)} %bitcast.1), calls=%async_computation | async-start | bytes 131072 | tf_op jit(solution)/shard_map/all_to_all | solution.py:541
  31.0 9.6 %copy-start.7 = (f32[128,512]{1,0:T(8,128)S(1)}, f32[128,512]{1,0:T(8,128)}, u32[]{:S(2)}) copy-start(f32[128,512]{1,0:T(8,128)} %get-tuple-element.32.r) | copy-start | bytes 786436

commit v7 on v6

--- a/solution.py
+++ b/solution.py
@@ -94,11 +94,9 @@
     cu = jnp.where(lane < cols - 1, jnp.minimum(code, next_col(code)), 0.0)
     ub = faces(*both, cu, next_col)
     ub = ub - prev_col(ub)
-    corners = []
-    for high, lanes in ((False, slice(0, 128)), (True, slice(cols - 128, cols))):
-        cut = lambda xs: [x[:, lanes] for x in xs]
-        rest = [jnp.where(upper, s0[...], s1[...]), jnp.where(upper, d0[...], d1[...])]
-        corners.append(lane_pack(cut(both[0]), cut(both[1]), code[:, lanes], cut(rest), high))
+    cut = lambda x: [x[:, :128], x[:, cols - 128 :]]
+    rest = [jnp.where(upper, s0[...], s1[...]), jnp.where(upper, d0[...], d1[...])]
+    corners = lane_packs([cut(x) for x in both[0]], [cut(x) for x in both[1]], cut(code), [cut(x) for x in rest])
 
     def tiles(g, c, code, surf, diag, v, of_last):
         g, c = [g[k] for k in range(LEV)], [c[k] for k in range(LEV)]
@@ -166,35 +164,34 @@
     return tiles[0]
 
 
-def lane_pack(g, c, code, rest, of_last):
-    group = iota(code.shape, 1) // DEEP
-    base, one, two = (DEEP, 0, 1) if of_last else (0, 1, 0)
-    places = [(g[k], 2 * k + one) for k in range(LEV)] + [(c[k], 16 + 2 * k + one) for k in range(LEV)]
-    places += [(x, 16 + 2 * n + two) for n, x in enumerate(rest)]
-    if of_last:
-        places.append((code, 31))
-    out = jnp.where(group == two, turn(code, DEEP * two + base, 1), 0.0)
+def lane_packs(g, c, code, rest):
+    lane = iota(code[0].shape, 1)
+    group, left, own = lane // DEEP, lane < 64, lane % 8 < DEEP
+    one = jnp.zeros_like(code[0])
+    for k in range(LEV):
+        for (first, last), at in ((g[k], 8 * k), (c[k], 64 + 8 * k)):
+            one = jnp.where(lane // 8 == at // 8, turn(jnp.where(left, first, last), at + DEEP, 1), one)
+    two = jnp.where(group == 0, code[0], jnp.where(group == 1, turn(code[1], 8, 1), 0.0))
     for by in (8, 16, 32):
-        out = out + turn(out, by, 1)
-    for x, at in places:
-        out = jnp.where(group == at, turn(x, DEEP * at + base, 1), out)
-    return out
+        two = two + turn(two, by, 1)
+    two = jnp.where(group == 31, code[1], two)
+    for n, (first, last) in enumerate(rest):
+        two = jnp.where(group == 16 + 2 * n, turn(first, 64 + 8 * n, 1), two)
+        two = jnp.where(group == 17 + 2 * n, turn(last, 72 + 8 * n, 1), two)
+    return jnp.where(own, two, one), jnp.where(own, one, two)
 
 
 def pack_cols(g, c, land, bottom, surf, diag, u, row_in, a_ref, b_ref, row_ref):
     row_ref[...] = row_in[...]
     cols = surf.shape[1]
-    packs = [
-        lane_pack(
-            [g[k, :, lanes] for k in range(LEV)],
-            [c[k, :, lanes] for k in range(LEV)],
-            code_of(land[:, lanes], bottom[:, lanes]),
-            [x[:, lanes] for x in (surf, diag, u)],
-            of_last,
-        )
-        for of_last, lanes in ((True, slice(cols - 128, cols)), (False, slice(0, 128)))
-    ]
-    a_ref[...], b_ref[...] = pick(is_even("col"), *packs)
+    ends = slice(0, 128), slice(cols - 128, cols)
+    low, high = lane_packs(
+        [[g[k, :, lanes] for lanes in ends] for k in range(LEV)],
+        [[c[k, :, lanes] for lanes in ends] for k in range(LEV)],
+        [code_of(land[:, lanes], bottom[:, lanes]) for lanes in ends],
+        [[x[:, lanes] for lanes in ends] for x in (surf, diag, u)],
+    )
+    a_ref[...], b_ref[...] = pick(is_even("col"), high, low)
 
 
 def row_halo(near, far, lanes):
@@ -331,16 +328,20 @@
     p2_ref[...] = p2
     lane = iota((8, 128), 1)
     mine = ((lane >= 60 - NEAR) & (lane < 60)) | ((lane >= 68) & (lane < 68 + NEAR))
-    packed = jnp.zeros((8, 128), F32)
+    sub = iota((8, 128), 0)
+    sums = jnp.zeros((8, 128), F32)
     for m, prod in enumerate(prods):
         part = mom_in[8 * m : 8 * m + 8, :] + jnp.where(mine, fold(prod, slice(0, 128)), 0.0)
         for by in (4, 2, 1):
             part = part + turn(part, by, 0)
-        part = ((part + turn(part, 16, 1)) + (turn(part, 32, 1) + turn(part, 48, 1))) + (
-            (turn(part, 64, 1) + turn(part, 80, 1)) + (turn(part, 96, 1) + turn(part, 112, 1))
-        )
-        part = (part + turn(part, 4, 1)) + (turn(part, 8, 1) + turn(part, 12, 1))
-        packed = jnp.where(lane // 4 == m, part, packed)
+        sums = jnp.where(sub == m, part, sums)
+    sums = ((sums + turn(sums, 16, 1)) + (turn(sums, 32, 1) + turn(sums, 48, 1))) + (
+        (turn(sums, 64, 1) + turn(sums, 80, 1)) + (turn(sums, 96, 1) + turn(sums, 112, 1))
+    )
+    sums = (sums + turn(sums, 4, 1)) + (turn(sums, 8, 1) + turn(sums, 12, 1))
+    packed = jnp.zeros((8, 128), F32)
+    for m in range(len(prods)):
+        packed = jnp.where(lane // 4 == m, jnp.broadcast_to(sums[m : m + 1, :], (8, 128)), packed)
     for i in range(mom_ref.shape[0] // 8):
         mom_ref[8 * i : 8 * i + 8, :] = packed
 

time: 42 us -> 42 us (level)
  transfers between devices with their start and end apart: 5 -> 5, of which waited for: 3 -> 3; matrix products, arithmetic and copies ran while one was open for 0% -> 0% of each run, Pallas kernels for 23% -> 22%
where the time goes in v7:
time: 42 us; the launch traced here: 41.8 us
  starting transfers between devices  21.3 us (51%)
  Pallas kernels  13.9 us (33%)
  waiting for transfers between devices  5.46 us (13%)
  between operations  0.83 us (2%)
    pallas_call x9, Pallas kernels, call(): run(*[pltpu.with_memory_space_constraint(x, spec.memory_space) for x, spe...  13.9 us
    all_to_all x1, starting transfers between devices, shards(): mom = lax.all_to_all(mom, ('row', 'col'), 0, 0, tiled=True)  9.56 us
    ppermute x1, starting transfers between devices, shards(): far = lax.ppermute(b, 'col', swap_pairs('col', 1))  6.36 us
    ppermute x1, starting transfers between devices, shards(): row_near = lax.ppermute(row_a, 'row', swap_pairs('row', 0))  4.5 us
    all_to_all x1, waiting for transfers between devices, shards(): mom = lax.all_to_all(mom, ('row', 'col'), 0, 0, tiled=True)  4.17 us
    ppermute x1, waiting for transfers between devices, shards(): near = lax.ppermute(a, 'col', swap_pairs('col', 0))  1 us
  transfers between devices with their start and end apart: 5, of which 3 were waited for; matrix products, arithmetic and copies ran while one was open for 0% of the time, Pallas kernels for 22%

profile of v7, /device:TPU:1, one launch (start us, length us, event | category | flops | bytes accessed | tf_op | source)
XLA Modules:
  0.0 41.8 jit_solution(10731326982738488139)
XLA Ops:
  0.6 0.0 copy-start.3
  0.6 0.0 copy-start.2
  0.7 0.0 copy-start
  0.7 0.0 copy-start.5
  0.7 0.0 copy-start.6
  0.7 1.7 %pack_rows.1 = (f32[32,512]{1,0:T(8,128)S(1)}, f32[32,512]{1,0:T(8,128)S(1)}) custom-call(f32[8,128,512]{2,1,0:T(8,128)} %g_in.1, f32[8,128,512]{2,1,0:T(8,128)} %c.5, s32[128,512]{1,0:T(8,128)} %land_in.1, s32[128,512]{1,0:T(8,128)} %bottom_in.1, f32[128,512]{1,0:T(8,128)} %surf.5, f32[128,512]{1,0:T(8,128)} %diag.5, f32[128,512]{1,0:T(8,128)} %v_in.1), custom_call_target="tpu_custom_call" | custom-call | tf_op jit(solution)/shard_map/pack_rows/pallas_call | solution.py:494
  2.4 0.8 %collective-permute-start.1 = (f32[32,512]{1,0:T(8,128)S(1)}, f32[32,512]{1,0:T(8,128)S(1)}, u32[]{:S(2)}, u32[]{:S(2)}) collective-permute-start(f32[32,512]{1,0:T(8,128)S(1)} %get-tuple-element.22.sent_b), channel_id=1, source_target_pairs={{16,32},{32,16},{48,64},{64,48},{80,96},{96,80},{17,33},{33,17},{4... | collective-permute-start | bytes 196616 | tf_op jit(solution)/shard_map/ppermute | solution.py:508
  3.2 0.3 copy-done.1
  3.5 0.7 %pack_cols.1 = (f32[128,128]{1,0:T(8,128)S(1)}, f32[128,128]{1,0:T(8,128)S(1)}, f32[32,512]{1,0:T(8,128)S(1)}) custom-call(f32[8,128,512]{2,1,0:T(8,128)S(1)} %copy-done, f32[8,128,512]{2,1,0:T(8,128)S(1)} %copy-done.1, s32[128,512]{1,0:T(8,128)S(1)} %copy-done.2, s32[128,512]{1,0:T(8,128)S(1)} %copy-done.3, f32[128,512]{1,0:T(8,128)S(1)} %copy-done.4, ...), custom_call_target="tpu_custom_call" | custom-call | flops 524288 | bytes 524288 | tf_op jit(solution)/shard_map/pack_cols/pallas_call | solution.py:494
  4.2 4.5 %collective-permute-start = (f32[32,512]{1,0:T(8,128)S(1)}, f32[32,512]{1,0:T(8,128)S(1)}, u32[]{:S(2)}, u32[]{:S(2)}) collective-permute-start(f32[32,512]{1,0:T(8,128)S(1)} %get-tuple-element.21.sent_a), channel_id=1, source_target_pairs={{0,16},{16,0},{32,48},{48,32},{64,80},{80,64},{96,112},{112,96},{1... | collective-permute-start | bytes 196616 | tf_op jit(solution)/shard_map/ppermute | solution.py:517
  8.7 1.6 %local_rhs.1 = (f32[128,512]{1,0:T(8,128)S(1)}, f32[128,512]{1,0:T(8,128)S(1)}) custom-call(f32[8,128,512]{2,1,0:T(8,128)S(1)} %copy-done, f32[8,128,512]{2,1,0:T(8,128)S(1)} %copy-done.1, s32[128,512]{1,0:T(8,128)S(1)} %copy-done.2, s32[128,512]{1,0:T(8,128)S(1)} %copy-done.3, f32[128,512]{1,0:T(8,128)S(1)} %copy-done.4), custom_call_target="tpu_custom_call" | custom-call | flops 12582912 | bytes 4194304 | tf_op jit(solution)/shard_map/local_rhs/pallas_call | solution.py:494
  10.3 0.0 collective-permute-done.1.far.rf
  10.3 0.0 collective-permute-done.near.rn
  10.4 6.4 %collective-permute-start.3 = (f32[136,128]{1,0:T(8,128)S(1)}, f32[136,128]{1,0:T(8,128)S(1)}, u32[]{:S(2)}, u32[]{:S(2)}) collective-permute-start(f32[136,128]{1,0:T(8,128)S(1)} %join_far.1.sent_b), channel_id=1, source_target_pairs={{1,2},{2,1},{3,4},{4,3},{5,6},{6,5},{7,8},{8,7},{9,10},{10,9},{11,... | collective-permute-start | bytes 208904 | tf_op jit(solution)/shard_map/ppermute | solution.py:527
  16.7 1.6 %inner.1 = (f32[128,512]{1,0:T(8,128)}, f32[128,512]{1,0:T(8,128)S(1)}, f32[128,512]{1,0:T(8,128)S(1)}, f32[48,128]{1,0:T(8,128)S(1)}, f32[136,128]{1,0:T(8,128)...) custom-call(f32[128,512]{1,0:T(8,128)S(1)} %get-tuple-element.24.r_in, f32[128,512]{1,0:T(8,128)S(1)} %get-tuple-element.25.code_in, ...), custom_call_target="tpu_custom_call" | custom-call | flops 12582912 | bytes 4194304 | tf_op jit(solution)/shard_map/inner/pallas_call | solution.py:494
  18.4 0.1 collective-permute-start.2
  18.5 0.2 collective-permute-done.3.cf.far
  18.7 1.0 %collective-permute-done.2.cn.near = f32[136,128]{1,0:T(8,128)S(1)} collective-permute-done((f32[136,128]{1,0:T(8,128)S(1)}, f32[136,128]{1,0:T(8,128)S(1)}, u32[]{:S(2)}, u32[]{:S(2)}) %collective-permute-start.2) | collective-permute-done | bytes 69664 | tf_op jit(solution)/shard_map/ppermute | solution.py:537
  19.7 1.7 %outer.1 = (f32[136,128]{1,0:T(8,128)S(1)}, f32[136,128]{1,0:T(8,128)S(1)}, f32[136,128]{1,0:T(8,128)S(1)}, f32[128,128]{1,0:T(8,128)}) custom-call(f32[136,128]{1,0:T(8,128)S(1)} %get-tuple-element.26.refs_0_.rs, f32[136,128]{1,0:T(8,128)S(1)} %get-tuple-element.28.codes, f32[136,128]{1,0:T(8,128)S(1)} %get-tuple-element.29.diags, ...), custom_call_target="tpu_custom_call" | custom-call | tf_op jit(solution)/shard_map/outer/pallas_call | solution.py:494
  21.4 9.6 %all-to-all-start = ((f32[128,1,128]{2,1,0:T(1,128)}), f32[128,1,128]{2,1,0:T(1,128)S(1)}, u32[]{:S(2)}, u32[]{:S(2)}) async-start(f32[128,1,128]{2,1,0:T(1,128)} %bitcast.1), calls=%async_computation | async-start | bytes 131072 | tf_op jit(solution)/shard_map/all_to_all | solution.py:542
  30.9 0.0 copy-start.7
  31.0 5.4 %tracer.1 = f32[8,128,512]{2,1,0:T(8,128)} custom-call(f32[8,128,512]{2,1,0:T(8,128)} %g_in.1, s32[128,512]{1,0:T(8,128)} %land_in.1, s32[128,512]{1,0:T(8,128)} %bottom_in.1, f32[128,512]{1,0:T(8,128)} %u_in.1, f32[128,512]{1,0:T(8,128)} %v_in.1, f32[32,512]{1,0:T(8,128)S(1)} %collective-permute-done.near.rn, f32[32,512]{1,0:T(8,128)S(1)} %collective-permute-done.1.far.rf, ...), custom_call_target="tpu_custom_call" | custom-call | flops 10485760 | bytes 6291456 | tf_op jit(solution)/shard_map/tracer/pallas_call | solution.py:494
  36.4 4.2 %all-to-all-done = f32[128,1,128]{2,1,0:T(1,128)S(1)} async-done(((f32[128,1,128]{2,1,0:T(1,128)}), f32[128,1,128]{2,1,0:T(1,128)S(1)}, u32[]{:S(2)}, u32[]{:S(2)}) %all-to-all-start) | async-done | bytes 65568 | tf_op jit(solution)/shard_map/all_to_all | solution.py:542
  40.6 1.2 %combine.1 = f32[128,512]{1,0:T(8,128)} custom-call(f32[128,128]{1,0:T(8,128)S(1)} %bitcast.4, f32[128,512]{1,0:T(8,128)S(1)} %copy-done.7, f32[128,512]{1,0:T(8,128)S(1)} %get-tuple-element.33.p1, f32[128,512]{1,0:T(8,128)S(1)} %get-tuple-element.34.p2, f32[136,128]{1,0:T(8,128)S(1)} %get-tuple-element.35.rs, f32[136,128]{1,0:T(8,128)S(1)} %get-tuple-element.36.p1s, ...), custom_call_target="tpu_custom_call" | custom-call | tf_op jit(solution)/shard_map/combine/pallas_call | solution.py:494
  (11 shorter events, 0.1 us)
Async XLA Ops:
  0.6 2.6 %copy-start.3 = (s32[128,512]{1,0:T(8,128)S(1)}, s32[128,512]{1,0:T(8,128)}, u32[]{:S(2)}) copy-start(s32[128,512]{1,0:T(8,128)} %bottom_in.1) | copy-start | bytes 786436
  0.6 2.6 %copy-start.2 = (s32[128,512]{1,0:T(8,128)S(1)}, s32[128,512]{1,0:T(8,128)}, u32[]{:S(2)}) copy-start(s32[128,512]{1,0:T(8,128)} %land_in.1) | copy-start | bytes 786436
  0.7 2.6 %copy-start = (f32[8,128,512]{2,1,0:T(8,128)S(1)}, f32[8,128,512]{2,1,0:T(8,128)}, u32[]{:S(2)}) copy-start(f32[8,128,512]{2,1,0:T(8,128)} %g_in.1) | copy-start | bytes 6291460
  0.7 2.6 %copy-start.5 = (f32[128,512]{1,0:T(8,128)S(1)}, f32[128,512]{1,0:T(8,128)}, u32[]{:S(2)}) copy-start(f32[128,512]{1,0:T(8,128)} %diag.5) | copy-start | bytes 786436
  0.7 2.6 %copy-start.4 = (f32[128,512]{1,0:T(8,128)S(1)}, f32[128,512]{1,0:T(8,128)}, u32[]{:S(2)}) copy-start(f32[128,512]{1,0:T(8,128)} %surf.5) | copy-start | bytes 786436
  0.7 2.8 %copy-start.1 = (f32[8,128,512]{2,1,0:T(8,128)S(1)}, f32[8,128,512]{2,1,0:T(8,128)}, u32[]{:S(2)}) copy-start(f32[8,128,512]{2,1,0:T(8,128)} %c.5) | copy-start | bytes 6291460
  0.7 2.8 %copy-start.6 = (f32[128,512]{1,0:T(8,128)S(1)}, f32[128,512]{1,0:T(8,128)}, u32[]{:S(2)}) copy-start(f32[128,512]{1,0:T(8,128)} %u_in.1) | copy-start | bytes 786436
  2.4 7.9 %collective-permute-start.1 = (f32[32,512]{1,0:T(8,128)S(1)}, f32[32,512]{1,0:T(8,128)S(1)}, u32[]{:S(2)}, u32[]{:S(2)}) collective-permute-start(f32[32,512]{1,0:T(8,128)S(1)} %get-tuple-element.22.sent_b), channel_id=1, source_target_pairs={{16,32},{32,16},{48,64},{64,48},{80,96},{96,80},{17,33},{33,17},{4... | collective-permute-start | bytes 196616 | tf_op jit(solution)/shard_map/ppermute | solution.py:508
  4.2 6.2 %collective-permute-start = (f32[32,512]{1,0:T(8,128)S(1)}, f32[32,512]{1,0:T(8,128)S(1)}, u32[]{:S(2)}, u32[]{:S(2)}) collective-permute-start(f32[32,512]{1,0:T(8,128)S(1)} %get-tuple-element.21.sent_a), channel_id=1, source_target_pairs={{0,16},{16,0},{32,48},{48,32},{64,80},{80,64},{96,112},{112,96},{1... | collective-permute-start | bytes 196616 | tf_op jit(solution)/shard_map/ppermute | solution.py:517
  10.4 8.3 %collective-permute-start.3 = (f32[136,128]{1,0:T(8,128)S(1)}, f32[136,128]{1,0:T(8,128)S(1)}, u32[]{:S(2)}, u32[]{:S(2)}) collective-permute-start(f32[136,128]{1,0:T(8,128)S(1)} %join_far.1.sent_b), channel_id=1, source_target_pairs={{1,2},{2,1},{3,4},{4,3},{5,6},{6,5},{7,8},{8,7},{9,10},{10,9},{11,... | collective-permute-start | bytes 208904 | tf_op jit(solution)/shard_map/ppermute | solution.py:527
  18.4 1.3 %collective-permute-start.2 = (f32[136,128]{1,0:T(8,128)S(1)}, f32[136,128]{1,0:T(8,128)S(1)}, u32[]{:S(2)}, u32[]{:S(2)}) collective-permute-start(f32[136,128]{1,0:T(8,128)S(1)} %join_near.1.sent_a), channel_id=1, source_target_pairs={{0,1},{1,0},{2,3},{3,2},{4,5},{5,4},{6,7},{7,6},{8,9},{9,8},{10,11... | collective-permute-start | bytes 208904 | tf_op jit(solution)/shard_map/ppermute | solution.py:537
  21.4 19.2 %all-to-all-start = ((f32[128,1,128]{2,1,0:T(1,128)}), f32[128,1,128]{2,1,0:T(1,128)S(1)}, u32[]{:S(2)}, u32[]{:S(2)}) async-start(f32[128,1,128]{2,1,0:T(1,128)} %bitcast.1), calls=%async_computation | async-start | bytes 131072 | tf_op jit(solution)/shard_map/all_to_all | solution.py:542
  30.9 9.6 %copy-start.7 = (f32[128,512]{1,0:T(8,128)S(1)}, f32[128,512]{1,0:T(8,128)}, u32[]{:S(2)}) copy-start(f32[128,512]{1,0:T(8,128)} %get-tuple-element.32.r) | copy-start | bytes 786436

commit v8 on v7

--- a/solution.py
+++ b/solution.py
@@ -95,8 +95,8 @@
     ub = faces(*both, cu, next_col)
     ub = ub - prev_col(ub)
     cut = lambda x: [x[:, :128], x[:, cols - 128 :]]
-    rest = [jnp.where(upper, s0[...], s1[...]), jnp.where(upper, d0[...], d1[...])]
-    corners = lane_packs([cut(x) for x in both[0]], [cut(x) for x in both[1]], cut(code), [cut(x) for x in rest])
+    diags = jnp.where(upper, d0[...], d1[...])
+    corners = lane_packs([cut(x) for x in both[0]], [cut(x) for x in both[1]], cut(code), cut(diags))
 
     def tiles(g, c, code, surf, diag, v, of_last):
         g, c = [g[k] for k in range(LEV)], [c[k] for k in range(LEV)]
@@ -164,21 +164,21 @@
     return tiles[0]
 
 
-def lane_packs(g, c, code, rest):
+def lane_packs(g, c, code, diag, u=None):
     lane = iota(code[0].shape, 1)
-    group, left, own = lane // DEEP, lane < 64, lane % 8 < DEEP
-    one = jnp.zeros_like(code[0])
-    for k in range(LEV):
-        for (first, last), at in ((g[k], 8 * k), (c[k], 64 + 8 * k)):
-            one = jnp.where(lane // 8 == at // 8, turn(jnp.where(left, first, last), at + DEEP, 1), one)
-    two = jnp.where(group == 0, code[0], jnp.where(group == 1, turn(code[1], 8, 1), 0.0))
-    for by in (8, 16, 32):
-        two = two + turn(two, by, 1)
-    two = jnp.where(group == 31, code[1], two)
-    for n, (first, last) in enumerate(rest):
-        two = jnp.where(group == 16 + 2 * n, turn(first, 64 + 8 * n, 1), two)
-        two = jnp.where(group == 17 + 2 * n, turn(last, 72 + 8 * n, 1), two)
-    return jnp.where(own, two, one), jnp.where(own, one, two)
+    packs = []
+    for end, edge in ((0, 0), (1, 127)):
+        out = jnp.where(lane == 16, turn(code[end], 16 - edge, 1), 0.0)
+        for by in (1, 2, 4):
+            out = out + turn(out, by, 1)
+        places = [(g[k], edge, k, 1) for k in range(LEV)] + [(c[k], edge, 8 + k, 1) for k in range(LEV)]
+        places += [(code, 125, 24, 2), (diag, 126, 29, 2)] if end else [(code, 1, 24, 2), (diag, 0, 26, 2)]
+        if end and u is not None:
+            places.append((u, 127, 31, 1))
+        for x, at, to, width in places:
+            out = jnp.where((lane >= to) & (lane < to + width), turn(x[end], to - at, 1), out)
+        packs.append(out)
+    return packs
 
 
 def pack_cols(g, c, land, bottom, surf, diag, u, row_in, a_ref, b_ref, row_ref):
@@ -189,7 +189,7 @@
         [[g[k, :, lanes] for lanes in ends] for k in range(LEV)],
         [[c[k, :, lanes] for lanes in ends] for k in range(LEV)],
         [code_of(land[:, lanes], bottom[:, lanes]) for lanes in ends],
-        [[x[:, lanes] for lanes in ends] for x in (surf, diag, u)],
+        *[[x[:, lanes] for lanes in ends] for x in (diag, u)],
     )
     a_ref[...], b_ref[...] = pick(is_even("col"), high, low)
 
@@ -208,17 +208,57 @@
     return plane
 
 
-def join_cols(of_near, own, near, far, *refs):
-    rows, width = own.shape[0], near.shape[1]
+def with_rows(r, sent_a, sent_b, near, far, lanes):
+    rows = r.shape[0]
+    even = is_even("row")
+    high, low = pick(even, sent_a[:, lanes], sent_b[:, lanes])
+    north, south = pick(even, near[:, lanes], far[:, lanes])
+    sub = iota((8, r.shape[1]), 0)
+
+    def across(below, above):
+        open_v = jnp.minimum(below[23:24], above[20:21]) > sub.astype(F32) + 0.5
+        total = jnp.where(open_v, above[:8] - below[:8], 0.0) * (above[8:16] + below[8:16])
+        for by in (4, 2, 1):
+            total = total + turn(total, by, 0)
+        return 0.0625 * total
+
+    up, down = across(high, north), across(south, low)
+    halo = row_halo(near, far, lanes)(RHS) + jnp.where(sub == 0, -up, jnp.where(sub == 7, down, 0.0))
+    first = r[:8] - jnp.where(sub == 0, down, 0.0)
+    last = r[rows - 8 :] + jnp.where(sub == 7, up, 0.0)
+    return jnp.concatenate([first, r[8 : rows - 8], last, halo], axis=0)
+
+
+def join_cols(of_near, own, r, sent_a, sent_b, near, far, *refs):
+    rows, width = r.shape
     out = refs[-1]
-    even = is_even("row")
-    packs = []
+    north, south = pick(is_even("row"), near[24:, :], far[24:, :])
+    sub = iota((8, 128), 0)
+    halos, sides = [], []
     for lanes in (slice(width - 128, width), slice(0, 128)):
-        north, south = pick(even, near[24:, lanes], far[24:, lanes])
-        sub = iota(north.shape, 0)
-        packs.append(jnp.where(sub < 3, turn(north, -5, 0), jnp.where(sub < 5, 0.0, south)))
-    out[:rows, :] = own[...]
-    out[rows:, :] = pick(is_even("col"), *packs)[0 if of_near else 1]
+        halos.append(jnp.where(sub < 3, turn(north[:, lanes], -5, 0), jnp.where(sub < 5, 0.0, south[:, lanes])))
+        sides.append(with_rows(r[:, lanes], sent_a, sent_b, near, far, lanes))
+    which = 0 if of_near else 1
+    even = is_even("col")
+    last = even if of_near else jnp.logical_not(even)
+    full = jnp.concatenate([own[...], pick(even, *halos)[which]], axis=0)
+    rhs = turn(pick(even, *sides)[which], 29, 1)
+    lane = iota(full.shape, 1)
+    start = jnp.where(last, 26, 29)
+    full = jnp.where((lane >= start) & (lane < start + 3), rhs, full)
+    tall = rows // 4
+    block = iota((tall, 128), 1) // 32
+    folded = full[:tall]
+    for b in range(1, 4):
+        folded = jnp.where(block == b, turn(full[b * tall : (b + 1) * tall], 32 * b, 1), folded)
+    out[:tall, :] = folded
+    out[tall:, :] = full[rows:]
+
+
+def unfold(x, by):
+    tall = x.shape[0] - 8
+    blocks = [turn(x[:tall], by - 32 * b, 1) for b in range(4)]
+    return jnp.concatenate(blocks + [turn(x[tall:], by, 1)], axis=0)
 
 
 def local_rhs(g, c, land, bottom, surf, r_ref, code_ref):
@@ -233,26 +273,8 @@
 
 def inner(r_in, code_in, diag, sent_a, sent_b, near, far, r_ref, p1_ref, p2_ref, mom_ref, rs_ref, codes_ref, diags_ref, r_own, sem):
     rows, cols = diag.shape
-    even = is_even("row")
-    lane, sub = iota((8, cols), 1), iota((8, cols), 0)
-    high, low = pick(even, sent_a[...], sent_b[...])
-    north, south = pick(even, near[...], far[...])
-
-    def across(below, above, here, there):
-        pair = [x[16 + at : 17 + at, :] for x, at in ((below, here), (above, there))]
-        open_v = jnp.minimum(*pair) > sub.astype(F32) + 0.5
-        total = jnp.where(open_v, above[:8] - below[:8], 0.0) * (above[8:16] + below[8:16])
-        for by in (4, 2, 1):
-            total = total + turn(total, by, 0)
-        return 0.0625 * total
-
-    up = across(high, north, 7, 4)
-    down = across(south, low, 7, 4)
     halo = row_halo(near, far, slice(0, cols))
-    r_halo = halo(RHS) + jnp.where(sub == 0, -up, jnp.where(sub == 7, down, 0.0))
-    low = r_in[:8] - jnp.where(sub == 0, down, 0.0)
-    high = r_in[rows - 8 :] + jnp.where(sub == 7, up, 0.0)
-    r = jnp.concatenate([low, r_in[8 : rows - 8], high, r_halo], axis=0)
+    r = with_rows(r_in[...], sent_a, sent_b, near, far, slice(0, cols))
     r_own[...] = r[:rows]
     copy = pltpu.make_async_copy(r_own, r_ref, sem)
     copy.start()
@@ -278,10 +300,10 @@
 
 def col_halo(near, far):
     east, west = pick(is_even("col"), near[...], far[...])
-    left = iota(east.shape, 1) < 64
-
-    def plane(of_east, of_west):
-        return jnp.where(left, turn(east, -of_east, 1), turn(west, 124 - of_west, 1))
+
+    def plane(at):
+        tile = unfold(east, -at)
+        return jnp.where(iota(tile.shape, 1) < 64, tile, unfold(west, 127 - at))
 
     return plane
 
@@ -291,36 +313,35 @@
     even = is_even("col")
     high, low = pick(even, sent_a[...], sent_b[...])
     east, west = pick(even, near[...], far[...])
-    lane = iota(high.shape, 1)
-    place = lane % 8
-    own, left = place < DEEP, lane < 64
-    at_east, at_west = jnp.where(own, high, east), jnp.where(own, west, low)
-
-    def shared(op):
-        minus, plus = [op(x) - x for x in (at_east, at_west)], [op(x) + x for x in (at_east, at_west)]
-        return jnp.where(left, minus[0], turn(minus[1], 64, 1)), jnp.where(left, turn(plus[0], 64, 1), plus[1])
-
-    code = jnp.where(left, turn(jnp.where(own, east, high), 4, 1), turn(jnp.where(own, low, west), 68, 1))
-    level = ((lane % 64) // 8).astype(F32) + 0.5
-    side = jnp.where(left, 0, 4)
-    keep_u = (place + side >= 3 + side // 4) & (place + side < 7 + side // 4)
-    keep_v = (place + side >= 4) & (place + side < 8)
-    one, two = shared(next_col)
-    ub = jnp.where((jnp.minimum(code, next_col(code)) > level) & keep_u, one, 0.0) * two
-    one, two = shared(next_row)
-    vb = jnp.where((jnp.minimum(code, next_row(code)) > level) & keep_v, one, 0.0) * two
-    total = 0.0625 * ((ub - prev_col(ub)) + (vb - prev_row(vb)))
-    for by in (8, 16, 32):
-        total = total + turn(total, -by, 1)
-
-    def filled(x, at):
-        return jnp.where((lane < 60) | (lane >= 68), x, turn(came, 60 - at, 1))
-
-    came = jnp.where(own, east, west)
-    added = jnp.where((lane >= 59) & (lane < 69), jnp.where(left, turn(total, 56, 1), total), 0.0)
-    r = filled(rs[...], 64) + added
-    code = 0.125 * filled(codes[...], 56)
-    dg = filled(diags[...], 72)
+    at = iota(high.shape, 1) % 32
+
+    def between(first, end, x):
+        return jnp.where((at >= first) & (at < end), x, 0.0)
+
+    def across(below, above, to):
+        open_u = turn(jnp.minimum(below, above), -16, 1) > at.astype(F32) + 0.5
+        total = between(0, 8, jnp.where(open_u, above - below, 0.0) * turn(above + below, -8, 1))
+        moved = [turn(total, to + 1 - k, 1) for k in range(LEV + 1)]
+        pairs = [moved[k] + moved[k + 1] for k in range(1, LEV - 1, 2)]
+        shared = (pairs[0] + pairs[1]) + (pairs[2] + moved[LEV - 1])
+        one, two = shared + moved[LEV], shared + moved[0]
+        first = to % 32
+        return 0.0625 * (between(first, first + 1, one) - between(first + 1, first + 2, two))
+
+    def placed(x, e, w, by):
+        came = unfold(e + w, by)
+        lane = iota(came.shape, 1)
+        return jnp.where((lane < 60) | (lane >= 68), x, came), came
+
+    _, added = placed(
+        0.0, across(high, east, 28) + between(29, 32, east), across(west, low, 36) + turn(between(26, 29, west), 8, 1), 31
+    )
+    lane = iota(added.shape, 1)
+    r = jnp.where((lane < 60) | (lane >= 68), rs[...], 0.0) + jnp.where((lane >= 59) & (lane < 69), added, 0.0)
+    nearest = jnp.where(at == 26, turn(west, 3, 1), west)
+    code, _ = placed(codes[...], between(23, 26, east), turn(between(24, 27, nearest), 4, 1), 37)
+    code = 0.125 * code
+    dg, _ = placed(diags[...], between(26, 28, east), turn(between(29, 31, west), 3, 1), 34)
     cu, cv = jnp.minimum(code, next_col(code)), jnp.minimum(code, next_row(code))
     p1, p2, prods = products(r, cu, cv, dg, rows)
     r_ref[...] = r
@@ -360,22 +381,22 @@
     sub = iota((8, cols), 0)
     north, south = pick(is_even("row"), rn[...], rf[...])
 
-    def wide(own, lanes, above, below):
+    def wide(own, lane, above, below):
         at = [8 * (x // 8) for x in (above, below)]
         halo = jnp.where(
             sub == 0,
             turn(north[at[0] : at[0] + 8], -(above % 8), 0),
             turn(south[at[1] : at[1] + 8], 7 - below % 8, 0),
         )
-        return jnp.concatenate([jnp.concatenate([own, halo], axis=0), ch(*lanes)], axis=1)
-
-    code = wide(code_of(land[...], bottom[...]), (0, 4), 20, 23)
+        return jnp.concatenate([jnp.concatenate([own, halo], axis=0), ch(lane)], axis=1)
+
+    code = wide(code_of(land[...], bottom[...]), 23, 20, 23)
     cu, cv = jnp.minimum(code, next_col(code)), jnp.minimum(code, next_row(code))
-    uw = 0.125 * wide(u[...], (80, 84), 28, 28)
-    vw = 0.125 * wide(v[...], (80, 84), 28, 28)
+    uw = 0.125 * wide(u[...], 31, 28, 28)
+    vw = 0.125 * wide(v[...], 31, 28, 28)
     for k in range(LEV):
         deep[k].wait()
-        gk = wide(g[k], (8 * k + 4, 8 * k), k, k)
+        gk = wide(g[k], k, k, k)
         pu = jnp.where(cu > k + 0.5, next_col(gk) - gk, 0.0) * uw
         pv = jnp.where(cv > k + 0.5, next_row(gk) - gk, 0.0) * vw
         total = gk + pu + prev_col(pu) + pv + prev_row(pv)
@@ -523,7 +544,10 @@
         name="local_rhs",
         cost=pl.CostEstimate(flops=24 * g.size, bytes_accessed=8 * g.size, transcendentals=0),
     )(g, c, land, bottom, surf_adj_next)
-    (b,) = call(functools.partial(join_cols, False), [VMEM] * 3, [(VMEM, side)], name="join_far")(b, *row_got)
+    sent = (rows // 4 + 8, 128)
+    (b,) = call(functools.partial(join_cols, False), [VMEM] * 6, [(VMEM, sent)], name="join_far")(
+        b, rhs, *row_sent, *row_got
+    )
     far = lax.ppermute(b, "col", swap_pairs("col", 1))
     r, p1, p2, mom, rs, codes, diags = call(
         inner,
@@ -533,7 +557,9 @@
         name="inner",
         cost=pl.CostEstimate(flops=24 * g.size, bytes_accessed=8 * g.size, transcendentals=0),
     )(rhs, code, diag, *row_sent, *row_got)
-    (a,) = call(functools.partial(join_cols, True), [VMEM] * 4, [(VMEM, side)], name="join_near")(a, *row_got, rs)
+    (a,) = call(functools.partial(join_cols, True), [VMEM] * 7, [(VMEM, sent)], name="join_near")(
+        a, rhs, *row_sent, *row_got, rs
+    )
     near = lax.ppermute(a, "col", swap_pairs("col", 0))
     col_sent, col_got = (a, b), (near, far)
     *sides, mom = call(outer, [VMEM] * 8, [(VMEM, side)] * 3 + [(VMEM, (size, 128))], name="outer")(

time: 42 us -> 41.4 us (0.986)
  starting transfers between devices: 21.3 us -> 20.4 us
    all_to_all x1, starting transfers between devices: 9.56 us -> 8.64 us  [shards(): mom = lax.all_to_all(mom, ('row', 'col'), 0, 0, tiled=True)]
    pallas_call x9, Pallas kernels: 13.9 us -> 14.3 us  [call(): run(*[pltpu.with_memory_space_constraint(x, spec.memory_space) for x, spe...]
  transfers between devices with their start and end apart: 5 -> 5, of which waited for: 3 -> 2; matrix products, arithmetic and copies ran while one was open for 0% -> 0% of each run, Pallas kernels for 22% -> 24%
where the time goes in v8:
time: 41.4 us; the launch traced here: 41.2 us
  starting transfers between devices  20.4 us (49%)
  Pallas kernels  14.3 us (35%)
  waiting for transfers between devices  5.39 us (13%)
  between operations  0.82 us (2%)
    pallas_call x9, Pallas kernels, call(): run(*[pltpu.with_memory_space_constraint(x, spec.memory_space) for x, spe...  14.3 us
    all_to_all x1, starting transfers between devices, shards(): mom = lax.all_to_all(mom, ('row', 'col'), 0, 0, tiled=True)  8.64 us
    ppermute x1, starting transfers between devices, shards(): far = lax.ppermute(b, 'col', swap_pairs('col', 1))  6.36 us
    ppermute x1, starting transfers between devices, shards(): row_near = lax.ppermute(row_a, 'row', swap_pairs('row', 0))  4.53 us
    all_to_all x1, waiting for transfers between devices, shards(): mom = lax.all_to_all(mom, ('row', 'col'), 0, 0, tiled=True)  4.19 us
    ppermute x1, waiting for transfers between devices, shards(): near = lax.ppermute(a, 'col', swap_pairs('col', 0))  1.17 us
  transfers between devices with their start and end apart: 5, of which 2 were waited for; matrix products, arithmetic and copies ran while one was open for 0% of the time, Pallas kernels for 24%

profile of v8, /device:TPU:1, one launch (start us, length us, event | category | flops | bytes accessed | tf_op | source)
XLA Modules:
  0.0 41.2 jit_solution(14708100151936891071)
XLA Ops:
  0.6 0.0 copy-start.3
  0.6 0.0 copy-start.2
  0.7 0.0 copy-start
  0.7 0.0 copy-start.6
  0.7 1.7 %pack_rows.1 = (f32[32,512]{1,0:T(8,128)S(1)}, f32[32,512]{1,0:T(8,128)S(1)}) custom-call(f32[8,128,512]{2,1,0:T(8,128)} %g_in.1, f32[8,128,512]{2,1,0:T(8,128)} %c.5, s32[128,512]{1,0:T(8,128)} %land_in.1, s32[128,512]{1,0:T(8,128)} %bottom_in.1, f32[128,512]{1,0:T(8,128)} %surf.5, f32[128,512]{1,0:T(8,128)} %diag.5, f32[128,512]{1,0:T(8,128)} %v_in.1), custom_call_target="tpu_custom_call" | custom-call | tf_op jit(solution)/shard_map/pack_rows/pallas_call | solution.py:515
  2.4 0.8 %collective-permute-start.1 = (f32[32,512]{1,0:T(8,128)S(1)}, f32[32,512]{1,0:T(8,128)S(1)}, u32[]{:S(2)}, u32[]{:S(2)}) collective-permute-start(f32[32,512]{1,0:T(8,128)S(1)} %get-tuple-element.22.sent_b), channel_id=1, source_target_pairs={{16,32},{32,16},{48,64},{64,48},{80,96},{96,80},{17,33},{33,17},{4... | collective-permute-start | bytes 196616 | tf_op jit(solution)/shard_map/ppermute | solution.py:529
  3.3 0.2 copy-done.1
  3.5 1.0 %pack_cols.1 = (f32[128,128]{1,0:T(8,128)S(1)}, f32[128,128]{1,0:T(8,128)S(1)}, f32[32,512]{1,0:T(8,128)S(1)}) custom-call(f32[8,128,512]{2,1,0:T(8,128)S(1)} %copy-done, f32[8,128,512]{2,1,0:T(8,128)S(1)} %copy-done.1, s32[128,512]{1,0:T(8,128)S(1)} %copy-done.2, s32[128,512]{1,0:T(8,128)S(1)} %copy-done.3, f32[128,512]{1,0:T(8,128)S(1)} %copy-done.4, ...), custom_call_target="tpu_custom_call" | custom-call | flops 524288 | bytes 524288 | tf_op jit(solution)/shard_map/pack_cols/pallas_call | solution.py:515
  4.5 4.5 %collective-permute-start = (f32[32,512]{1,0:T(8,128)S(1)}, f32[32,512]{1,0:T(8,128)S(1)}, u32[]{:S(2)}, u32[]{:S(2)}) collective-permute-start(f32[32,512]{1,0:T(8,128)S(1)} %get-tuple-element.21.sent_a), channel_id=1, source_target_pairs={{0,16},{16,0},{32,48},{48,32},{64,80},{80,64},{96,112},{112,96},{1... | collective-permute-start | bytes 196616 | tf_op jit(solution)/shard_map/ppermute | solution.py:538
  9.0 1.6 %local_rhs.1 = (f32[128,512]{1,0:T(8,128)S(1)}, f32[128,512]{1,0:T(8,128)S(1)}) custom-call(f32[8,128,512]{2,1,0:T(8,128)S(1)} %copy-done, f32[8,128,512]{2,1,0:T(8,128)S(1)} %copy-done.1, s32[128,512]{1,0:T(8,128)S(1)} %copy-done.2, s32[128,512]{1,0:T(8,128)S(1)} %copy-done.3, f32[128,512]{1,0:T(8,128)S(1)} %copy-done.4), custom_call_target="tpu_custom_call" | custom-call | flops 12582912 | bytes 4194304 | tf_op jit(solution)/shard_map/local_rhs/pallas_call | solution.py:515
  10.7 0.0 collective-permute-done.1.far.rf
  10.7 0.0 collective-permute-done.near.rn
  10.7 0.2 join_far.1.sent_b
  10.9 6.4 %collective-permute-start.3 = (f32[40,128]{1,0:T(8,128)S(1)}, f32[40,128]{1,0:T(8,128)S(1)}, u32[]{:S(2)}, u32[]{:S(2)}) collective-permute-start(f32[40,128]{1,0:T(8,128)S(1)} %join_far.1.sent_b), channel_id=1, source_target_pairs={{1,2},{2,1},{3,4},{4,3},{5,6},{6,5},{7,8},{8,7},{9,10},{10,9},{11,... | collective-permute-start | bytes 61448 | tf_op jit(solution)/shard_map/ppermute | solution.py:551
  17.2 1.6 %inner.1 = (f32[128,512]{1,0:T(8,128)}, f32[128,512]{1,0:T(8,128)S(1)}, f32[128,512]{1,0:T(8,128)S(1)}, f32[48,128]{1,0:T(8,128)S(1)}, f32[136,128]{1,0:T(8,128)...) custom-call(f32[128,512]{1,0:T(8,128)S(1)} %get-tuple-element.24.r_in.r, f32[128,512]{1,0:T(8,128)S(1)} %get-tuple-element.25.code_in, ...), custom_call_target="tpu_custom_call" | custom-call | flops 12582912 | bytes 4194304 | tf_op jit(solution)/shard_map/inner/pallas_call | solution.py:515
  18.8 0.2 join_near.1.sent_a
  19.0 0.1 collective-permute-start.2
  19.1 1.2 %collective-permute-done.2.cn.near = f32[40,128]{1,0:T(8,128)S(1)} collective-permute-done((f32[40,128]{1,0:T(8,128)S(1)}, f32[40,128]{1,0:T(8,128)S(1)}, u32[]{:S(2)}, u32[]{:S(2)}) %collective-permute-start.2) | collective-permute-done | bytes 20512 | tf_op jit(solution)/shard_map/ppermute | solution.py:563
  20.3 1.5 %outer.1 = (f32[136,128]{1,0:T(8,128)S(1)}, f32[136,128]{1,0:T(8,128)S(1)}, f32[136,128]{1,0:T(8,128)S(1)}, f32[128,128]{1,0:T(8,128)}) custom-call(f32[136,128]{1,0:T(8,128)S(1)} %get-tuple-element.26.refs_0_.rs, f32[136,128]{1,0:T(8,128)S(1)} %get-tuple-element.28.codes, f32[136,128]{1,0:T(8,128)S(1)} %get-tuple-element.29.diags, ...), custom_call_target="tpu_custom_call" | custom-call | tf_op jit(solution)/shard_map/outer/pallas_call | solution.py:515
  21.7 8.6 %all-to-all-start = ((f32[128,1,128]{2,1,0:T(1,128)}), f32[128,1,128]{2,1,0:T(1,128)S(1)}, u32[]{:S(2)}, u32[]{:S(2)}) async-start(f32[128,1,128]{2,1,0:T(1,128)} %bitcast.1), calls=%async_computation | async-start | bytes 131072 | tf_op jit(solution)/shard_map/all_to_all | solution.py:568
  30.4 0.0 copy-start.7
  30.4 5.4 %tracer.1 = f32[8,128,512]{2,1,0:T(8,128)} custom-call(f32[8,128,512]{2,1,0:T(8,128)} %g_in.1, s32[128,512]{1,0:T(8,128)} %land_in.1, s32[128,512]{1,0:T(8,128)} %bottom_in.1, f32[128,512]{1,0:T(8,128)} %u_in.1, f32[128,512]{1,0:T(8,128)} %v_in.1, f32[32,512]{1,0:T(8,128)S(1)} %collective-permute-done.near.rn, f32[32,512]{1,0:T(8,128)S(1)} %collective-permute-done.1.far.rf, ...), custom_call_target="tpu_custom_call" | custom-call | flops 10485760 | bytes 6291456 | tf_op jit(solution)/shard_map/tracer/pallas_call | solution.py:515
  35.8 4.2 %all-to-all-done = f32[128,1,128]{2,1,0:T(1,128)S(1)} async-done(((f32[128,1,128]{2,1,0:T(1,128)}), f32[128,1,128]{2,1,0:T(1,128)S(1)}, u32[]{:S(2)}, u32[]{:S(2)}) %all-to-all-start) | async-done | bytes 65568 | tf_op jit(solution)/shard_map/all_to_all | solution.py:568
  40.0 1.2 %combine.1 = f32[128,512]{1,0:T(8,128)} custom-call(f32[128,128]{1,0:T(8,128)S(1)} %bitcast.4, f32[128,512]{1,0:T(8,128)S(1)} %copy-done.7, f32[128,512]{1,0:T(8,128)S(1)} %get-tuple-element.33.p1, f32[128,512]{1,0:T(8,128)S(1)} %get-tuple-element.34.p2, f32[136,128]{1,0:T(8,128)S(1)} %get-tuple-element.35.rs, f32[136,128]{1,0:T(8,128)S(1)} %get-tuple-element.36.p1s, ...), custom_call_target="tpu_custom_call" | custom-call | tf_op jit(solution)/shard_map/combine/pallas_call | solution.py:515
  (11 shorter events, 0.0 us)
Async XLA Ops:
  0.6 2.6 %copy-start.3 = (s32[128,512]{1,0:T(8,128)S(1)}, s32[128,512]{1,0:T(8,128)}, u32[]{:S(2)}) copy-start(s32[128,512]{1,0:T(8,128)} %bottom_in.1) | copy-start | bytes 786436
  0.6 2.6 %copy-start.2 = (s32[128,512]{1,0:T(8,128)S(1)}, s32[128,512]{1,0:T(8,128)}, u32[]{:S(2)}) copy-start(s32[128,512]{1,0:T(8,128)} %land_in.1) | copy-start | bytes 786436
  0.7 2.6 %copy-start = (f32[8,128,512]{2,1,0:T(8,128)S(1)}, f32[8,128,512]{2,1,0:T(8,128)}, u32[]{:S(2)}) copy-start(f32[8,128,512]{2,1,0:T(8,128)} %g_in.1) | copy-start | bytes 6291460
  0.7 2.6 %copy-start.5 = (f32[128,512]{1,0:T(8,128)S(1)}, f32[128,512]{1,0:T(8,128)}, u32[]{:S(2)}) copy-start(f32[128,512]{1,0:T(8,128)} %diag.5) | copy-start | bytes 786436
  0.7 2.6 %copy-start.4 = (f32[128,512]{1,0:T(8,128)S(1)}, f32[128,512]{1,0:T(8,128)}, u32[]{:S(2)}) copy-start(f32[128,512]{1,0:T(8,128)} %surf.5) | copy-start | bytes 786436
  0.7 2.8 %copy-start.1 = (f32[8,128,512]{2,1,0:T(8,128)S(1)}, f32[8,128,512]{2,1,0:T(8,128)}, u32[]{:S(2)}) copy-start(f32[8,128,512]{2,1,0:T(8,128)} %c.5) | copy-start | bytes 6291460
  0.7 2.8 %copy-start.6 = (f32[128,512]{1,0:T(8,128)S(1)}, f32[128,512]{1,0:T(8,128)}, u32[]{:S(2)}) copy-start(f32[128,512]{1,0:T(8,128)} %u_in.1) | copy-start | bytes 786436
  2.4 8.2 %collective-permute-start.1 = (f32[32,512]{1,0:T(8,128)S(1)}, f32[32,512]{1,0:T(8,128)S(1)}, u32[]{:S(2)}, u32[]{:S(2)}) collective-permute-start(f32[32,512]{1,0:T(8,128)S(1)} %get-tuple-element.22.sent_b), channel_id=1, source_target_pairs={{16,32},{32,16},{48,64},{64,48},{80,96},{96,80},{17,33},{33,17},{4... | collective-permute-start | bytes 196616 | tf_op jit(solution)/shard_map/ppermute | solution.py:529
  4.5 6.2 %collective-permute-start = (f32[32,512]{1,0:T(8,128)S(1)}, f32[32,512]{1,0:T(8,128)S(1)}, u32[]{:S(2)}, u32[]{:S(2)}) collective-permute-start(f32[32,512]{1,0:T(8,128)S(1)} %get-tuple-element.21.sent_a), channel_id=1, source_target_pairs={{0,16},{16,0},{32,48},{48,32},{64,80},{80,64},{96,112},{112,96},{1... | collective-permute-start | bytes 196616 | tf_op jit(solution)/shard_map/ppermute | solution.py:538
  10.9 8.2 %collective-permute-start.3 = (f32[40,128]{1,0:T(8,128)S(1)}, f32[40,128]{1,0:T(8,128)S(1)}, u32[]{:S(2)}, u32[]{:S(2)}) collective-permute-start(f32[40,128]{1,0:T(8,128)S(1)} %join_far.1.sent_b), channel_id=1, source_target_pairs={{1,2},{2,1},{3,4},{4,3},{5,6},{6,5},{7,8},{8,7},{9,10},{10,9},{11,... | collective-permute-start | bytes 61448 | tf_op jit(solution)/shard_map/ppermute | solution.py:551
  19.0 1.3 %collective-permute-start.2 = (f32[40,128]{1,0:T(8,128)S(1)}, f32[40,128]{1,0:T(8,128)S(1)}, u32[]{:S(2)}, u32[]{:S(2)}) collective-permute-start(f32[40,128]{1,0:T(8,128)S(1)} %join_near.1.sent_a), channel_id=1, source_target_pairs={{0,1},{1,0},{2,3},{3,2},{4,5},{5,4},{6,7},{7,6},{8,9},{9,8},{10,11... | collective-permute-start | bytes 61448 | tf_op jit(solution)/shard_map/ppermute | solution.py:563
  21.7 18.3 %all-to-all-start = ((f32[128,1,128]{2,1,0:T(1,128)}), f32[128,1,128]{2,1,0:T(1,128)S(1)}, u32[]{:S(2)}, u32[]{:S(2)}) async-start(f32[128,1,128]{2,1,0:T(1,128)} %bitcast.1), calls=%async_computation | async-start | bytes 131072 | tf_op jit(solution)/shard_map/all_to_all | solution.py:568
  30.4 9.6 %copy-start.7 = (f32[128,512]{1,0:T(8,128)S(1)}, f32[128,512]{1,0:T(8,128)}, u32[]{:S(2)}) copy-start(f32[128,512]{1,0:T(8,128)} %get-tuple-element.32.r) | copy-start | bytes 786436

commit v9 on v8

--- a/solution.py
+++ b/solution.py
@@ -96,7 +96,10 @@
     ub = ub - prev_col(ub)
     cut = lambda x: [x[:, :128], x[:, cols - 128 :]]
     diags = jnp.where(upper, d0[...], d1[...])
-    corners = lane_packs([cut(x) for x in both[0]], [cut(x) for x in both[1]], cut(code), cut(diags))
+    corners = [
+        lane_pack(end, [cut(x)[end] for x in both[0]], [cut(x)[end] for x in both[1]], cut(code)[end], cut(diags)[end])
+        for end in range(2)
+    ]
 
     def tiles(g, c, code, surf, diag, v, of_last):
         g, c = [g[k] for k in range(LEV)], [c[k] for k in range(LEV)]
@@ -164,34 +167,24 @@
     return tiles[0]
 
 
-def lane_packs(g, c, code, diag, u=None):
-    lane = iota(code[0].shape, 1)
-    packs = []
-    for end, edge in ((0, 0), (1, 127)):
-        out = jnp.where(lane == 16, turn(code[end], 16 - edge, 1), 0.0)
-        for by in (1, 2, 4):
-            out = out + turn(out, by, 1)
-        places = [(g[k], edge, k, 1) for k in range(LEV)] + [(c[k], edge, 8 + k, 1) for k in range(LEV)]
-        places += [(code, 125, 24, 2), (diag, 126, 29, 2)] if end else [(code, 1, 24, 2), (diag, 0, 26, 2)]
-        if end and u is not None:
-            places.append((u, 127, 31, 1))
-        for x, at, to, width in places:
-            out = jnp.where((lane >= to) & (lane < to + width), turn(x[end], to - at, 1), out)
-        packs.append(out)
-    return packs
-
-
-def pack_cols(g, c, land, bottom, surf, diag, u, row_in, a_ref, b_ref, row_ref):
+def lane_pack(end, g, c, code, diag, u=None):
+    lane = iota(code.shape, 1)
+    edge = 127 if end else 0
+    out = jnp.where(lane == 16, turn(code, 16 - edge, 1), 0.0)
+    for by in (1, 2, 4):
+        out = out + turn(out, by, 1)
+    places = [(g[k], edge, k, 1) for k in range(LEV)] + [(c[k], edge, 8 + k, 1) for k in range(LEV)]
+    places += [(code, 125, 24, 2), (diag, 126, 29, 2)] if end else [(code, 1, 24, 2), (diag, 0, 26, 2)]
+    if u is not None:
+        places.append((u, 127, 31, 1))
+    for x, at, to, width in places:
+        out = jnp.where((lane >= to) & (lane < to + width), turn(x, to - at, 1), out)
+    return out
+
+
+def codes_of(land, bottom, row_in, code_ref, row_ref):
     row_ref[...] = row_in[...]
-    cols = surf.shape[1]
-    ends = slice(0, 128), slice(cols - 128, cols)
-    low, high = lane_packs(
-        [[g[k, :, lanes] for lanes in ends] for k in range(LEV)],
-        [[c[k, :, lanes] for lanes in ends] for k in range(LEV)],
-        [code_of(land[:, lanes], bottom[:, lanes]) for lanes in ends],
-        *[[x[:, lanes] for lanes in ends] for x in (diag, u)],
-    )
-    a_ref[...], b_ref[...] = pick(is_even("col"), high, low)
+    code_ref[...] = code_of(land[...], bottom[...])
 
 
 def row_halo(near, far, lanes):
@@ -229,7 +222,7 @@
     return jnp.concatenate([first, r[8 : rows - 8], last, halo], axis=0)
 
 
-def join_cols(of_near, own, r, sent_a, sent_b, near, far, *refs):
+def join_cols(of_near, high, low, r, sent_a, sent_b, near, far, *refs):
     rows, width = r.shape
     out = refs[-1]
     north, south = pick(is_even("row"), near[24:, :], far[24:, :])
@@ -241,7 +234,8 @@
     which = 0 if of_near else 1
     even = is_even("col")
     last = even if of_near else jnp.logical_not(even)
-    full = jnp.concatenate([own[...], pick(even, *halos)[which]], axis=0)
+    own = pick(even, high[...], low[...])[which]
+    full = jnp.concatenate([own, pick(even, *halos)[which]], axis=0)
     rhs = turn(pick(even, *sides)[which], 29, 1)
     lane = iota(full.shape, 1)
     start = jnp.where(last, 26, 29)
@@ -261,14 +255,16 @@
     return jnp.concatenate(blocks + [turn(x[tall:], by, 1)], axis=0)
 
 
-def local_rhs(g, c, land, bottom, surf, r_ref, code_ref):
+def local_rhs(g, c, code_in, surf, diag, u, r_ref, first_ref, last_ref):
     rows, cols = surf.shape
-    code = code_of(land[...], bottom[...])
-    code_ref[...] = code
+    code = code_in[...]
     cu = jnp.where(iota(code.shape, 1) < cols - 1, jnp.minimum(code, next_col(code)), 0.0)
     cv = jnp.where(iota(code.shape, 0) < rows - 1, jnp.minimum(code, next_row(code)), 0.0)
     ub, vb = faces(g, c, cu, next_col), faces(g, c, cv, next_row)
     r_ref[...] = surf[...] + 0.0625 * ((ub - prev_col(ub)) + (vb - prev_row(vb)))
+    for end, (tile, ref) in enumerate(((slice(0, 128), first_ref), (slice(cols - 128, cols), last_ref))):
+        gs, cs = [g[k, :, tile] for k in range(LEV)], [c[k, :, tile] for k in range(LEV)]
+        ref[...] = lane_pack(end, gs, cs, code[:, tile], diag[:, tile], u[:, tile] if end else None)
 
 
 def inner(r_in, code_in, diag, sent_a, sent_b, near, far, r_ref, p1_ref, p2_ref, mom_ref, rs_ref, codes_ref, diags_ref, r_own, sem):
@@ -528,25 +524,25 @@
     )(g, c, land, bottom, surf_adj_next, diag, v_north)
     row_far = lax.ppermute(row_b, "row", swap_pairs("row", 1))
     deep = pltpu.VMEM(g.shape, F32)
-    a, b, row_a = call(
-        pack_cols,
-        [VMEM] * 8,
-        [(VMEM, (rows, 128))] * 2 + [(VMEM, (32, cols))],
-        name="pack_cols",
+    code, row_a = call(
+        codes_of,
+        [VMEM] * 3,
+        [(VMEM, two), (VMEM, (32, cols))],
+        name="codes_of",
         cost=pl.CostEstimate(flops=g.size, bytes_accessed=g.size, transcendentals=0),
-    )(g, c, land, bottom, surf_adj_next, diag, u_east, row_a)
+    )(land, bottom, row_a)
     row_near = lax.ppermute(row_a, "row", swap_pairs("row", 0))
     row_sent, row_got = (row_a, row_b), (row_near, row_far)
-    rhs, code = call(
+    rhs, low, high = call(
         local_rhs,
-        [VMEM] * 5,
-        [(VMEM, two)] * 2,
+        [VMEM] * 6,
+        [(VMEM, two)] + [(VMEM, (rows, 128))] * 2,
         name="local_rhs",
         cost=pl.CostEstimate(flops=24 * g.size, bytes_accessed=8 * g.size, transcendentals=0),
-    )(g, c, land, bottom, surf_adj_next)
+    )(g, c, code, surf_adj_next, diag, u_east)
     sent = (rows // 4 + 8, 128)
-    (b,) = call(functools.partial(join_cols, False), [VMEM] * 6, [(VMEM, sent)], name="join_far")(
-        b, rhs, *row_sent, *row_got
+    (b,) = call(functools.partial(join_cols, False), [VMEM] * 7, [(VMEM, sent)], name="join_far")(
+        high, low, rhs, *row_sent, *row_got
     )
     far = lax.ppermute(b, "col", swap_pairs("col", 1))
     r, p1, p2, mom, rs, codes, diags = call(
@@ -557,8 +553,8 @@
         name="inner",
         cost=pl.CostEstimate(flops=24 * g.size, bytes_accessed=8 * g.size, transcendentals=0),
     )(rhs, code, diag, *row_sent, *row_got)
-    (a,) = call(functools.partial(join_cols, True), [VMEM] * 7, [(VMEM, sent)], name="join_near")(
-        a, rhs, *row_sent, *row_got, rs
+    (a,) = call(functools.partial(join_cols, True), [VMEM] * 8, [(VMEM, sent)], name="join_near")(
+        high, low, rhs, *row_sent, *row_got, rs
     )
     near = lax.ppermute(a, "col", swap_pairs("col", 0))
     col_sent, col_got = (a, b), (near, far)

time: 41.4 us -> 41.4 us (level)
    ppermute x1, starting transfers between devices: 6.36 us -> 5.76 us  [shards(): far = lax.ppermute(b, 'col', swap_pairs('col', 1))]
    all_to_all x1, starting transfers between devices: 8.64 us -> 9.17 us  [shards(): mom = lax.all_to_all(mom, ('row', 'col'), 0, 0, tiled=True)]
where the time goes in v9:
time: 41.4 us; the launch traced here: 41.2 us
  starting transfers between devices  20.6 us (50%)
  Pallas kernels  14.4 us (35%)
  waiting for transfers between devices  5.36 us (13%)
  between operations  0.82 us (2%)
    pallas_call x9, Pallas kernels, call(): run(*[pltpu.with_memory_space_constraint(x, spec.memory_space) for x, spe...  14.4 us
    all_to_all x1, starting transfers between devices, shards(): mom = lax.all_to_all(mom, ('row', 'col'), 0, 0, tiled=True)  9.17 us
    ppermute x1, starting transfers between devices, shards(): far = lax.ppermute(b, 'col', swap_pairs('col', 1))  5.76 us
    ppermute x1, starting transfers between devices, shards(): row_near = lax.ppermute(row_a, 'row', swap_pairs('row', 0))  4.75 us
    all_to_all x1, waiting for transfers between devices, shards(): mom = lax.all_to_all(mom, ('row', 'col'), 0, 0, tiled=True)  4.19 us
    ppermute x1, waiting for transfers between devices, shards(): near = lax.ppermute(a, 'col', swap_pairs('col', 0))  1.17 us
  transfers between devices with their start and end apart: 5, of which 2 were waited for; matrix products, arithmetic and copies ran while one was open for 0% of the time, Pallas kernels for 24%

profile of v9, /device:TPU:1, one launch (start us, length us, event | category | flops | bytes accessed | tf_op | source)
XLA Modules:
  0.0 41.2 jit_solution(15458227819355784728)
XLA Ops:
  0.6 0.0 copy-start.4
  0.6 0.0 copy-start.3
  0.7 0.0 copy-start
  0.7 0.0 copy-start.5
  0.7 0.0 copy-start.6
  0.7 1.7 %pack_rows.1 = (f32[32,512]{1,0:T(8,128)S(1)}, f32[32,512]{1,0:T(8,128)S(1)}) custom-call(f32[8,128,512]{2,1,0:T(8,128)} %g_in.1, f32[8,128,512]{2,1,0:T(8,128)} %c.3, s32[128,512]{1,0:T(8,128)} %land_in.1, s32[128,512]{1,0:T(8,128)} %bottom_in.1, f32[128,512]{1,0:T(8,128)} %surf.3, f32[128,512]{1,0:T(8,128)} %diag.5, f32[128,512]{1,0:T(8,128)} %v_in.1), custom_call_target="tpu_custom_call" | custom-call | tf_op jit(solution)/shard_map/pack_rows/pallas_call | solution.py:511
  2.4 0.8 %collective-permute-start.1 = (f32[32,512]{1,0:T(8,128)S(1)}, f32[32,512]{1,0:T(8,128)S(1)}, u32[]{:S(2)}, u32[]{:S(2)}) collective-permute-start(f32[32,512]{1,0:T(8,128)S(1)} %get-tuple-element.22.sent_b), channel_id=1, source_target_pairs={{16,32},{32,16},{48,64},{64,48},{80,96},{96,80},{17,33},{33,17},{4... | collective-permute-start | bytes 196616 | tf_op jit(solution)/shard_map/ppermute | solution.py:525
  3.3 4.7 %collective-permute-start = (f32[32,512]{1,0:T(8,128)S(1)}, f32[32,512]{1,0:T(8,128)S(1)}, u32[]{:S(2)}, u32[]{:S(2)}) collective-permute-start(f32[32,512]{1,0:T(8,128)S(1)} %get-tuple-element.21.sent_a), channel_id=1, source_target_pairs={{0,16},{16,0},{32,48},{48,32},{64,80},{80,64},{96,112},{112,96},{1... | collective-permute-start | bytes 196616 | tf_op jit(solution)/shard_map/ppermute | solution.py:534
  8.0 2.7 %local_rhs.1 = (f32[128,512]{1,0:T(8,128)S(1)}, f32[128,128]{1,0:T(8,128)S(1)}, f32[128,128]{1,0:T(8,128)S(1)}) custom-call(f32[8,128,512]{2,1,0:T(8,128)S(1)} %copy-done, f32[8,128,512]{2,1,0:T(8,128)S(1)} %copy-done.1, f32[128,512]{1,0:T(8,128)S(1)} %get-tuple-element.23.code_in, f32[128,512]{1,0:T(8,128)S(1)} %copy-done.5, f32[128,512]{1,0:T(8,128)S(1)} %copy-done.2, ...), custom_call_target="tpu_custom_call" | custom-call | flops 12582912 | bytes 4194304 | tf_op jit(solution)/shard_map/local_rhs/pallas_call | solution.py:511
  10.8 0.0 collective-permute-done.1.far.rf
  10.8 0.0 collective-permute-done.near.rn
  10.8 0.2 join_far.1.sent_b
  10.9 5.8 %collective-permute-start.3 = (f32[40,128]{1,0:T(8,128)S(1)}, f32[40,128]{1,0:T(8,128)S(1)}, u32[]{:S(2)}, u32[]{:S(2)}) collective-permute-start(f32[40,128]{1,0:T(8,128)S(1)} %join_far.1.sent_b), channel_id=1, source_target_pairs={{1,2},{2,1},{3,4},{4,3},{5,6},{6,5},{7,8},{8,7},{9,10},{10,9},{11,... | collective-permute-start | bytes 61448 | tf_op jit(solution)/shard_map/ppermute | solution.py:547
  16.7 1.6 %inner.1 = (f32[128,512]{1,0:T(8,128)}, f32[128,512]{1,0:T(8,128)S(1)}, f32[128,512]{1,0:T(8,128)S(1)}, f32[48,128]{1,0:T(8,128)S(1)}, f32[136,128]{1,0:T(8,128)...) custom-call(f32[128,512]{1,0:T(8,128)S(1)} %get-tuple-element.26.r_in.r, f32[128,512]{1,0:T(8,128)S(1)} %get-tuple-element.23.code_in, ...), custom_call_target="tpu_custom_call" | custom-call | flops 12582912 | bytes 4194304 | tf_op jit(solution)/shard_map/inner/pallas_call | solution.py:511
  18.3 0.2 join_near.1.sent_a
  18.5 0.1 collective-permute-start.2
  18.6 0.0 collective-permute-done.3.cf.far
  18.6 1.2 %collective-permute-done.2.cn.near = f32[40,128]{1,0:T(8,128)S(1)} collective-permute-done((f32[40,128]{1,0:T(8,128)S(1)}, f32[40,128]{1,0:T(8,128)S(1)}, u32[]{:S(2)}, u32[]{:S(2)}) %collective-permute-start.2) | collective-permute-done | bytes 20512 | tf_op jit(solution)/shard_map/ppermute | solution.py:559
  19.7 1.5 %outer.1 = (f32[136,128]{1,0:T(8,128)S(1)}, f32[136,128]{1,0:T(8,128)S(1)}, f32[136,128]{1,0:T(8,128)S(1)}, f32[128,128]{1,0:T(8,128)}) custom-call(f32[136,128]{1,0:T(8,128)S(1)} %get-tuple-element.27.refs_0_.rs, f32[136,128]{1,0:T(8,128)S(1)} %get-tuple-element.28.codes, f32[136,128]{1,0:T(8,128)S(1)} %get-tuple-element.29.diags, ...), custom_call_target="tpu_custom_call" | custom-call | tf_op jit(solution)/shard_map/outer/pallas_call | solution.py:511
  21.2 9.2 %all-to-all-start = ((f32[128,1,128]{2,1,0:T(1,128)}), f32[128,1,128]{2,1,0:T(1,128)S(1)}, u32[]{:S(2)}, u32[]{:S(2)}) async-start(f32[128,1,128]{2,1,0:T(1,128)} %bitcast.1), calls=%async_computation | async-start | bytes 131072 | tf_op jit(solution)/shard_map/all_to_all | solution.py:564
  30.4 0.0 copy-start.7
  30.4 5.4 %tracer.1 = f32[8,128,512]{2,1,0:T(8,128)} custom-call(f32[8,128,512]{2,1,0:T(8,128)} %g_in.1, s32[128,512]{1,0:T(8,128)} %land_in.1, s32[128,512]{1,0:T(8,128)} %bottom_in.1, f32[128,512]{1,0:T(8,128)} %u_in.1, f32[128,512]{1,0:T(8,128)} %v_in.1, f32[32,512]{1,0:T(8,128)S(1)} %collective-permute-done.near.rn, f32[32,512]{1,0:T(8,128)S(1)} %collective-permute-done.1.far.rf, ...), custom_call_target="tpu_custom_call" | custom-call | flops 10485760 | bytes 6291456 | tf_op jit(solution)/shard_map/tracer/pallas_call | solution.py:511
  35.8 4.2 %all-to-all-done = f32[128,1,128]{2,1,0:T(1,128)S(1)} async-done(((f32[128,1,128]{2,1,0:T(1,128)}), f32[128,1,128]{2,1,0:T(1,128)S(1)}, u32[]{:S(2)}, u32[]{:S(2)}) %all-to-all-start) | async-done | bytes 65568 | tf_op jit(solution)/shard_map/all_to_all | solution.py:564
  40.0 1.2 %combine.1 = f32[128,512]{1,0:T(8,128)} custom-call(f32[128,128]{1,0:T(8,128)S(1)} %bitcast.4, f32[128,512]{1,0:T(8,128)S(1)} %copy-done.7, f32[128,512]{1,0:T(8,128)S(1)} %get-tuple-element.33.p1, f32[128,512]{1,0:T(8,128)S(1)} %get-tuple-element.34.p2, f32[136,128]{1,0:T(8,128)S(1)} %get-tuple-element.35.rs, f32[136,128]{1,0:T(8,128)S(1)} %get-tuple-element.36.p1s, ...), custom_call_target="tpu_custom_call" | custom-call | tf_op jit(solution)/shard_map/combine/pallas_call | solution.py:511
  (11 shorter events, 0.1 us)
Async XLA Ops:
  0.6 2.6 %copy-start.4 = (s32[128,512]{1,0:T(8,128)S(1)}, s32[128,512]{1,0:T(8,128)}, u32[]{:S(2)}) copy-start(s32[128,512]{1,0:T(8,128)} %bottom_in.1) | copy-start | bytes 786436
  0.6 2.6 %copy-start.3 = (s32[128,512]{1,0:T(8,128)S(1)}, s32[128,512]{1,0:T(8,128)}, u32[]{:S(2)}) copy-start(s32[128,512]{1,0:T(8,128)} %land_in.1) | copy-start | bytes 786436
  0.7 7.4 %copy-start.2 = (f32[128,512]{1,0:T(8,128)S(1)}, f32[128,512]{1,0:T(8,128)}, u32[]{:S(2)}) copy-start(f32[128,512]{1,0:T(8,128)} %diag.5) | copy-start | bytes 786436
  0.7 7.4 %copy-start = (f32[8,128,512]{2,1,0:T(8,128)S(1)}, f32[8,128,512]{2,1,0:T(8,128)}, u32[]{:S(2)}) copy-start(f32[8,128,512]{2,1,0:T(8,128)} %g_in.1) | copy-start | bytes 6291460
  0.7 7.4 %copy-start.5 = (f32[128,512]{1,0:T(8,128)S(1)}, f32[128,512]{1,0:T(8,128)}, u32[]{:S(2)}) copy-start(f32[128,512]{1,0:T(8,128)} %surf.3) | copy-start | bytes 786436
  0.7 7.3 %copy-start.1 = (f32[8,128,512]{2,1,0:T(8,128)S(1)}, f32[8,128,512]{2,1,0:T(8,128)}, u32[]{:S(2)}) copy-start(f32[8,128,512]{2,1,0:T(8,128)} %c.3) | copy-start | bytes 6291460
  0.7 7.3 %copy-start.6 = (f32[128,512]{1,0:T(8,128)S(1)}, f32[128,512]{1,0:T(8,128)}, u32[]{:S(2)}) copy-start(f32[128,512]{1,0:T(8,128)} %u_in.1) | copy-start | bytes 786436
  2.4 8.3 %collective-permute-start.1 = (f32[32,512]{1,0:T(8,128)S(1)}, f32[32,512]{1,0:T(8,128)S(1)}, u32[]{:S(2)}, u32[]{:S(2)}) collective-permute-start(f32[32,512]{1,0:T(8,128)S(1)} %get-tuple-element.22.sent_b), channel_id=1, source_target_pairs={{16,32},{32,16},{48,64},{64,48},{80,96},{96,80},{17,33},{33,17},{4... | collective-permute-start | bytes 196616 | tf_op jit(solution)/shard_map/ppermute | solution.py:525
  3.3 7.5 %collective-permute-start = (f32[32,512]{1,0:T(8,128)S(1)}, f32[32,512]{1,0:T(8,128)S(1)}, u32[]{:S(2)}, u32[]{:S(2)}) collective-permute-start(f32[32,512]{1,0:T(8,128)S(1)} %get-tuple-element.21.sent_a), channel_id=1, source_target_pairs={{0,16},{16,0},{32,48},{48,32},{64,80},{80,64},{96,112},{112,96},{1... | collective-permute-start | bytes 196616 | tf_op jit(solution)/shard_map/ppermute | solution.py:534
  10.9 7.6 %collective-permute-start.3 = (f32[40,128]{1,0:T(8,128)S(1)}, f32[40,128]{1,0:T(8,128)S(1)}, u32[]{:S(2)}, u32[]{:S(2)}) collective-permute-start(f32[40,128]{1,0:T(8,128)S(1)} %join_far.1.sent_b), channel_id=1, source_target_pairs={{1,2},{2,1},{3,4},{4,3},{5,6},{6,5},{7,8},{8,7},{9,10},{10,9},{11,... | collective-permute-start | bytes 61448 | tf_op jit(solution)/shard_map/ppermute | solution.py:547
  18.5 1.3 %collective-permute-start.2 = (f32[40,128]{1,0:T(8,128)S(1)}, f32[40,128]{1,0:T(8,128)S(1)}, u32[]{:S(2)}, u32[]{:S(2)}) collective-permute-start(f32[40,128]{1,0:T(8,128)S(1)} %join_near.1.sent_a), channel_id=1, source_target_pairs={{0,1},{1,0},{2,3},{3,2},{4,5},{5,4},{6,7},{7,6},{8,9},{9,8},{10,11... | collective-permute-start | bytes 61448 | tf_op jit(solution)/shard_map/ppermute | solution.py:559
  21.2 18.8 %all-to-all-start = ((f32[128,1,128]{2,1,0:T(1,128)}), f32[128,1,128]{2,1,0:T(1,128)S(1)}, u32[]{:S(2)}, u32[]{:S(2)}) async-start(f32[128,1,128]{2,1,0:T(1,128)} %bitcast.1), calls=%async_computation | async-start | bytes 131072 | tf_op jit(solution)/shard_map/all_to_all | solution.py:564
  30.4 9.6 %copy-start.7 = (f32[128,512]{1,0:T(8,128)S(1)}, f32[128,512]{1,0:T(8,128)}, u32[]{:S(2)}) copy-start(f32[128,512]{1,0:T(8,128)} %get-tuple-element.32.r) | copy-start | bytes 786436

commit v10 on v9

--- a/solution.py
+++ b/solution.py
@@ -267,7 +267,18 @@
         ref[...] = lane_pack(end, gs, cs, code[:, tile], diag[:, tile], u[:, tile] if end else None)
 
 
-def inner(r_in, code_in, diag, sent_a, sent_b, near, far, r_ref, p1_ref, p2_ref, mom_ref, rs_ref, codes_ref, diags_ref, r_own, sem):
+def ends_of(r_in, code_in, diag, sent_a, sent_b, near, far, rs_ref, codes_ref, diags_ref):
+    rows, cols = diag.shape
+    halo = row_halo(near, far, slice(0, cols))
+    r = with_rows(r_in[...], sent_a, sent_b, near, far, slice(0, cols))
+    code = jnp.concatenate([code_in[...], halo(CODE)], axis=0)
+    dg = jnp.concatenate([diag[...], halo(DIAG)], axis=0)
+    left = iota((rows + 8, 128), 1) < 64
+    for x, ref in ((r, rs_ref), (code, codes_ref), (dg, diags_ref)):
+        ref[...] = jnp.where(left, turn(x[:, cols - 128 :], -68, 1), turn(x[:, :128], 68, 1))
+
+
+def inner(r_in, code_in, diag, sent_a, sent_b, near, far, r_ref, p1_ref, p2_ref, mom_ref, r_own, sem):
     rows, cols = diag.shape
     halo = row_halo(near, far, slice(0, cols))
     r = with_rows(r_in[...], sent_a, sent_b, near, far, slice(0, cols))
@@ -276,9 +287,6 @@
     copy.start()
     code = jnp.concatenate([code_in[...], halo(CODE)], axis=0)
     dg = jnp.concatenate([diag[...], halo(DIAG)], axis=0)
-    left = iota((rows + 8, 128), 1) < 64
-    for x, ref in ((r, rs_ref), (code, codes_ref), (dg, diags_ref)):
-        ref[...] = jnp.where(left, turn(x[:, cols - 128 :], -68, 1), turn(x[:, :128], 68, 1))
     code = 0.125 * code
     cu = jnp.where(iota(code.shape, 1) < cols - 1, jnp.minimum(code, next_col(code)), 0.0)
     cv = jnp.minimum(code, next_row(code))
@@ -545,19 +553,21 @@
         high, low, rhs, *row_sent, *row_got
     )
     far = lax.ppermute(b, "col", swap_pairs("col", 1))
-    r, p1, p2, mom, rs, codes, diags = call(
-        inner,
-        [VMEM] * 7,
-        [(HBM, two)] + [(VMEM, two)] * 2 + [(VMEM, (48, 128))] + [(VMEM, side)] * 3,
-        [whole(), dma],
-        name="inner",
-        cost=pl.CostEstimate(flops=24 * g.size, bytes_accessed=8 * g.size, transcendentals=0),
-    )(rhs, code, diag, *row_sent, *row_got)
+    fields = (rhs, code, diag, *row_sent, *row_got)
+    rs, codes, diags = call(ends_of, [VMEM] * 7, [(VMEM, side)] * 3, name="ends_of")(*fields)
     (a,) = call(functools.partial(join_cols, True), [VMEM] * 8, [(VMEM, sent)], name="join_near")(
         high, low, rhs, *row_sent, *row_got, rs
     )
     near = lax.ppermute(a, "col", swap_pairs("col", 0))
     col_sent, col_got = (a, b), (near, far)
+    r, p1, p2, mom = call(
+        inner,
+        [VMEM] * 7,
+        [(HBM, two)] + [(VMEM, two)] * 2 + [(VMEM, (48, 128))],
+        [whole(), dma],
+        name="inner",
+        cost=pl.CostEstimate(flops=24 * g.size, bytes_accessed=8 * g.size, transcendentals=0),
+    )(*fields)
     *sides, mom = call(outer, [VMEM] * 8, [(VMEM, side)] * 3 + [(VMEM, (size, 128))], name="outer")(
         rs, codes, diags, mom, *col_sent, *col_got
     )

time: 41.4 us -> 41.4 us (level)
  starting transfers between devices: 20.6 us -> 22 us
  waiting for transfers between devices: 5.36 us -> 4.39 us
    all_to_all x1, starting transfers between devices: 9.17 us -> 10.6 us  [shards(): mom = lax.all_to_all(mom, ('row', 'col'), 0, 0, tiled=True)]
    ppermute x1, waiting for transfers between devices: 1.17 us -> 0.17 us  [shards(): near = lax.ppermute(a, 'col', swap_pairs('col', 0))]
    pallas_call x9 -> x10, Pallas kernels: 14.4 us -> 14 us  [call(): run(*[pltpu.with_memory_space_constraint(x, spec.memory_space) for x, spe...]
  transfers between devices with their start and end apart: 5 -> 5, of which waited for: 2 -> 2; matrix products, arithmetic and copies ran while one was open for 0% -> 0% of each run, Pallas kernels for 24% -> 23%
where the time goes in v10:
time: 41.4 us; the launch traced here: 41.2 us
  starting transfers between devices  22 us (53%)
  Pallas kernels  14 us (34%)
  waiting for transfers between devices  4.39 us (11%)
  between operations  0.82 us (2%)
    pallas_call x10, Pallas kernels, call(): run(*[pltpu.with_memory_space_constraint(x, spec.memory_space) for x, spe...  14 us
    all_to_all x1, starting transfers between devices, shards(): mom = lax.all_to_all(mom, ('row', 'col'), 0, 0, tiled=True)  10.6 us
    ppermute x1, starting transfers between devices, shards(): far = lax.ppermute(b, 'col', swap_pairs('col', 1))  5.76 us
    ppermute x1, starting transfers between devices, shards(): row_near = lax.ppermute(row_a, 'row', swap_pairs('row', 0))  4.75 us
    all_to_all x1, waiting for transfers between devices, shards(): mom = lax.all_to_all(mom, ('row', 'col'), 0, 0, tiled=True)  4.19 us
  transfers between devices with their start and end apart: 5, of which 2 were waited for; matrix products, arithmetic and copies ran while one was open for 0% of the time, Pallas kernels for 23%

profile of v10, /device:TPU:1, one launch (start us, length us, event | category | flops | bytes accessed | tf_op | source)
XLA Modules:
  0.0 41.2 jit_solution(7165840685290511400)
XLA Ops:
  0.6 0.0 copy-start.4
  0.7 0.0 copy-start.3
  0.7 0.0 copy-start
  0.7 0.0 copy-start.6
  0.7 1.7 %pack_rows.1 = (f32[32,512]{1,0:T(8,128)S(1)}, f32[32,512]{1,0:T(8,128)S(1)}) custom-call(f32[8,128,512]{2,1,0:T(8,128)} %g_in.1, f32[8,128,512]{2,1,0:T(8,128)} %c.3, s32[128,512]{1,0:T(8,128)} %land_in.1, s32[128,512]{1,0:T(8,128)} %bottom_in.1, f32[128,512]{1,0:T(8,128)} %surf.3, f32[128,512]{1,0:T(8,128)} %diag.7, f32[128,512]{1,0:T(8,128)} %v_in.1), custom_call_target="tpu_custom_call" | custom-call | tf_op jit(solution)/shard_map/pack_rows/pallas_call | solution.py:519
  2.4 0.8 %collective-permute-start.1 = (f32[32,512]{1,0:T(8,128)S(1)}, f32[32,512]{1,0:T(8,128)S(1)}, u32[]{:S(2)}, u32[]{:S(2)}) collective-permute-start(f32[32,512]{1,0:T(8,128)S(1)} %get-tuple-element.22.sent_b), channel_id=1, source_target_pairs={{16,32},{32,16},{48,64},{64,48},{80,96},{96,80},{17,33},{33,17},{4... | collective-permute-start | bytes 196616 | tf_op jit(solution)/shard_map/ppermute | solution.py:533
  3.3 4.7 %collective-permute-start = (f32[32,512]{1,0:T(8,128)S(1)}, f32[32,512]{1,0:T(8,128)S(1)}, u32[]{:S(2)}, u32[]{:S(2)}) collective-permute-start(f32[32,512]{1,0:T(8,128)S(1)} %get-tuple-element.21.sent_a), channel_id=1, source_target_pairs={{0,16},{16,0},{32,48},{48,32},{64,80},{80,64},{96,112},{112,96},{1... | collective-permute-start | bytes 196616 | tf_op jit(solution)/shard_map/ppermute | solution.py:542
  8.0 2.7 %local_rhs.1 = (f32[128,512]{1,0:T(8,128)S(1)}, f32[128,128]{1,0:T(8,128)S(1)}, f32[128,128]{1,0:T(8,128)S(1)}) custom-call(f32[8,128,512]{2,1,0:T(8,128)S(1)} %copy-done, f32[8,128,512]{2,1,0:T(8,128)S(1)} %copy-done.1, f32[128,512]{1,0:T(8,128)S(1)} %get-tuple-element.23.code_in, f32[128,512]{1,0:T(8,128)S(1)} %copy-done.5, f32[128,512]{1,0:T(8,128)S(1)} %copy-done.2, ...), custom_call_target="tpu_custom_call" | custom-call | flops 12582912 | bytes 4194304 | tf_op jit(solution)/shard_map/local_rhs/pallas_call | solution.py:519
  10.8 0.0 collective-permute-done.1.far.rf
  10.8 0.0 collective-permute-done.near.rn
  10.8 0.2 join_far.1.sent_b
  10.9 5.8 %collective-permute-start.3 = (f32[40,128]{1,0:T(8,128)S(1)}, f32[40,128]{1,0:T(8,128)S(1)}, u32[]{:S(2)}, u32[]{:S(2)}) collective-permute-start(f32[40,128]{1,0:T(8,128)S(1)} %join_far.1.sent_b), channel_id=1, source_target_pairs={{1,2},{2,1},{3,4},{4,3},{5,6},{6,5},{7,8},{8,7},{9,10},{10,9},{11,... | collective-permute-start | bytes 61448 | tf_op jit(solution)/shard_map/ppermute | solution.py:555
  16.7 0.2 ends_of.1
  16.9 0.2 join_near.1.sent_a
  17.1 0.1 collective-permute-start.2
  17.2 1.0 %inner.1 = (f32[128,512]{1,0:T(8,128)}, f32[128,512]{1,0:T(8,128)S(1)}, f32[128,512]{1,0:T(8,128)S(1)}, f32[48,128]{1,0:T(8,128)S(1)}) custom-call(f32[128,512]{1,0:T(8,128)S(1)} %get-tuple-element.26.r_in.r, f32[128,512]{1,0:T(8,128)S(1)} %get-tuple-element.23.code_in, f32[128,512]{1,0:T(8,128)S(1)} %copy-done.2, f32[32,512]{1,0:T(8,128)S(1)} %get-tuple-element.21.sent_a, ...), custom_call_target="tpu_custom_call" | custom-call | flops 12582912 | bytes 4194304 | tf_op jit(solution)/shard_map/inner/pallas_call | solution.py:519
  18.1 0.0 collective-permute-done.3.cf.far
  18.2 0.2 collective-permute-done.2.cn.near
  18.3 1.5 %outer.1 = (f32[136,128]{1,0:T(8,128)S(1)}, f32[136,128]{1,0:T(8,128)S(1)}, f32[136,128]{1,0:T(8,128)S(1)}, f32[128,128]{1,0:T(8,128)}) custom-call(f32[136,128]{1,0:T(8,128)S(1)} %get-tuple-element.27.refs_0_.rs, f32[136,128]{1,0:T(8,128)S(1)} %get-tuple-element.28.codes, f32[136,128]{1,0:T(8,128)S(1)} %get-tuple-element.29.diags, ...), custom_call_target="tpu_custom_call" | custom-call | tf_op jit(solution)/shard_map/outer/pallas_call | solution.py:519
  19.8 10.6 %all-to-all-start = ((f32[128,1,128]{2,1,0:T(1,128)}), f32[128,1,128]{2,1,0:T(1,128)S(1)}, u32[]{:S(2)}, u32[]{:S(2)}) async-start(f32[128,1,128]{2,1,0:T(1,128)} %bitcast.1), calls=%async_computation | async-start | bytes 131072 | tf_op jit(solution)/shard_map/all_to_all | solution.py:574
  30.4 0.0 copy-start.7
  30.4 5.4 %tracer.1 = f32[8,128,512]{2,1,0:T(8,128)} custom-call(f32[8,128,512]{2,1,0:T(8,128)} %g_in.1, s32[128,512]{1,0:T(8,128)} %land_in.1, s32[128,512]{1,0:T(8,128)} %bottom_in.1, f32[128,512]{1,0:T(8,128)} %u_in.1, f32[128,512]{1,0:T(8,128)} %v_in.1, f32[32,512]{1,0:T(8,128)S(1)} %collective-permute-done.near.rn, f32[32,512]{1,0:T(8,128)S(1)} %collective-permute-done.1.far.rf, ...), custom_call_target="tpu_custom_call" | custom-call | flops 10485760 | bytes 6291456 | tf_op jit(solution)/shard_map/tracer/pallas_call | solution.py:519
  35.8 4.2 %all-to-all-done = f32[128,1,128]{2,1,0:T(1,128)S(1)} async-done(((f32[128,1,128]{2,1,0:T(1,128)}), f32[128,1,128]{2,1,0:T(1,128)S(1)}, u32[]{:S(2)}, u32[]{:S(2)}) %all-to-all-start) | async-done | bytes 65568 | tf_op jit(solution)/shard_map/all_to_all | solution.py:574
  40.0 1.2 %combine.1 = f32[128,512]{1,0:T(8,128)} custom-call(f32[128,128]{1,0:T(8,128)S(1)} %bitcast.4, f32[128,512]{1,0:T(8,128)S(1)} %copy-done.7, f32[128,512]{1,0:T(8,128)S(1)} %get-tuple-element.33.p1, f32[128,512]{1,0:T(8,128)S(1)} %get-tuple-element.34.p2, f32[136,128]{1,0:T(8,128)S(1)} %get-tuple-element.35.rs, f32[136,128]{1,0:T(8,128)S(1)} %get-tuple-element.36.p1s, ...), custom_call_target="tpu_custom_call" | custom-call | tf_op jit(solution)/shard_map/combine/pallas_call | solution.py:519
  (12 shorter events, 0.1 us)
Async XLA Ops:
  0.6 7.4 %copy-start.2 = (f32[128,512]{1,0:T(8,128)S(1)}, f32[128,512]{1,0:T(8,128)}, u32[]{:S(2)}) copy-start(f32[128,512]{1,0:T(8,128)} %diag.7) | copy-start | bytes 786436
  0.6 2.6 %copy-start.4 = (s32[128,512]{1,0:T(8,128)S(1)}, s32[128,512]{1,0:T(8,128)}, u32[]{:S(2)}) copy-start(s32[128,512]{1,0:T(8,128)} %bottom_in.1) | copy-start | bytes 786436
  0.7 2.6 %copy-start.3 = (s32[128,512]{1,0:T(8,128)S(1)}, s32[128,512]{1,0:T(8,128)}, u32[]{:S(2)}) copy-start(s32[128,512]{1,0:T(8,128)} %land_in.1) | copy-start | bytes 786436
  0.7 7.4 %copy-start = (f32[8,128,512]{2,1,0:T(8,128)S(1)}, f32[8,128,512]{2,1,0:T(8,128)}, u32[]{:S(2)}) copy-start(f32[8,128,512]{2,1,0:T(8,128)} %g_in.1) | copy-start | bytes 6291460
  0.7 7.4 %copy-start.5 = (f32[128,512]{1,0:T(8,128)S(1)}, f32[128,512]{1,0:T(8,128)}, u32[]{:S(2)}) copy-start(f32[128,512]{1,0:T(8,128)} %surf.3) | copy-start | bytes 786436
  0.7 7.3 %copy-start.1 = (f32[8,128,512]{2,1,0:T(8,128)S(1)}, f32[8,128,512]{2,1,0:T(8,128)}, u32[]{:S(2)}) copy-start(f32[8,128,512]{2,1,0:T(8,128)} %c.3) | copy-start | bytes 6291460
  0.7 7.3 %copy-start.6 = (f32[128,512]{1,0:T(8,128)S(1)}, f32[128,512]{1,0:T(8,128)}, u32[]{:S(2)}) copy-start(f32[128,512]{1,0:T(8,128)} %u_in.1) | copy-start | bytes 786436
  2.4 8.3 %collective-permute-start.1 = (f32[32,512]{1,0:T(8,128)S(1)}, f32[32,512]{1,0:T(8,128)S(1)}, u32[]{:S(2)}, u32[]{:S(2)}) collective-permute-start(f32[32,512]{1,0:T(8,128)S(1)} %get-tuple-element.22.sent_b), channel_id=1, source_target_pairs={{16,32},{32,16},{48,64},{64,48},{80,96},{96,80},{17,33},{33,17},{4... | collective-permute-start | bytes 196616 | tf_op jit(solution)/shard_map/ppermute | solution.py:533
  3.3 7.5 %collective-permute-start = (f32[32,512]{1,0:T(8,128)S(1)}, f32[32,512]{1,0:T(8,128)S(1)}, u32[]{:S(2)}, u32[]{:S(2)}) collective-permute-start(f32[32,512]{1,0:T(8,128)S(1)} %get-tuple-element.21.sent_a), channel_id=1, source_target_pairs={{0,16},{16,0},{32,48},{48,32},{64,80},{80,64},{96,112},{112,96},{1... | collective-permute-start | bytes 196616 | tf_op jit(solution)/shard_map/ppermute | solution.py:542
  10.9 7.2 %collective-permute-start.3 = (f32[40,128]{1,0:T(8,128)S(1)}, f32[40,128]{1,0:T(8,128)S(1)}, u32[]{:S(2)}, u32[]{:S(2)}) collective-permute-start(f32[40,128]{1,0:T(8,128)S(1)} %join_far.1.sent_b), channel_id=1, source_target_pairs={{1,2},{2,1},{3,4},{4,3},{5,6},{6,5},{7,8},{8,7},{9,10},{10,9},{11,... | collective-permute-start | bytes 61448 | tf_op jit(solution)/shard_map/ppermute | solution.py:555
  17.1 1.3 %collective-permute-start.2 = (f32[40,128]{1,0:T(8,128)S(1)}, f32[40,128]{1,0:T(8,128)S(1)}, u32[]{:S(2)}, u32[]{:S(2)}) collective-permute-start(f32[40,128]{1,0:T(8,128)S(1)} %join_near.1.sent_a), channel_id=1, source_target_pairs={{0,1},{1,0},{2,3},{3,2},{4,5},{5,4},{6,7},{7,6},{8,9},{9,8},{10,11... | collective-permute-start | bytes 61448 | tf_op jit(solution)/shard_map/ppermute | solution.py:561
  19.8 20.2 %all-to-all-start = ((f32[128,1,128]{2,1,0:T(1,128)}), f32[128,1,128]{2,1,0:T(1,128)S(1)}, u32[]{:S(2)}, u32[]{:S(2)}) async-start(f32[128,1,128]{2,1,0:T(1,128)} %bitcast.1), calls=%async_computation | async-start | bytes 131072 | tf_op jit(solution)/shard_map/all_to_all | solution.py:574
  30.4 9.6 %copy-start.7 = (f32[128,512]{1,0:T(8,128)S(1)}, f32[128,512]{1,0:T(8,128)}, u32[]{:S(2)}) copy-start(f32[128,512]{1,0:T(8,128)} %get-tuple-element.32.r) | copy-start | bytes 786436

commit v11 on v9

--- a/solution.py
+++ b/solution.py
@@ -360,7 +360,7 @@
     for m in range(len(prods)):
         packed = jnp.where(lane // 4 == m, jnp.broadcast_to(sums[m : m + 1, :], (8, 128)), packed)
     for i in range(mom_ref.shape[0] // 8):
-        mom_ref[8 * i : 8 * i + 8, :] = packed
+        mom_ref[8 * i : 8 * i + 8, :] = packed[:, : mom_ref.shape[1]]
 
 
 def tracer_kernel(g_in, land_in, bottom_in, u_in, v_in, rn, rf, cn, cf, out_ref, g, land, bottom, u, v, out, sems, g_sems, out_sems):
@@ -441,7 +441,7 @@
 
 
 def combine(mom, r, p1, p2, rs, p1s, p2s, x_ref, x, sems):
-    zero = jnp.zeros((8, 128), F32)
+    zero = jnp.zeros((8, mom.shape[1]), F32)
     tiles = [(mom[8 * i : 8 * i + 8, :], zero) for i in range(mom.shape[0] // 8)]
     while len(tiles) > 1:
         tiles = [add(tiles[i], tiles[i + 1]) for i in range(0, len(tiles), 2)]
@@ -558,7 +558,7 @@
     )
     near = lax.ppermute(a, "col", swap_pairs("col", 0))
     col_sent, col_got = (a, b), (near, far)
-    *sides, mom = call(outer, [VMEM] * 8, [(VMEM, side)] * 3 + [(VMEM, (size, 128))], name="outer")(
+    *sides, mom = call(outer, [VMEM] * 8, [(VMEM, side)] * 3 + [(VMEM, (size, 32))], name="outer")(
         rs, codes, diags, mom, *col_sent, *col_got
     )
     mom = lax.all_to_all(mom, ("row", "col"), 0, 0, tiled=True)

time: 41.4 us -> 41.4 us (level)
  no operation moved by 1% of the time
where the time goes in v11:
time: 41.4 us; the launch traced here: 41.2 us
  starting transfers between devices  20.6 us (50%)
  Pallas kernels  14.4 us (35%)
  waiting for transfers between devices  5.36 us (13%)
  between operations  0.82 us (2%)
    pallas_call x9, Pallas kernels, call(): run(*[pltpu.with_memory_space_constraint(x, spec.memory_space) for x, spe...  14.4 us
    all_to_all x1, starting transfers between devices, shards(): mom = lax.all_to_all(mom, ('row', 'col'), 0, 0, tiled=True)  9.17 us
    ppermute x1, starting transfers between devices, shards(): far = lax.ppermute(b, 'col', swap_pairs('col', 1))  5.76 us
    ppermute x1, starting transfers between devices, shards(): row_near = lax.ppermute(row_a, 'row', swap_pairs('row', 0))  4.75 us
    all_to_all x1, waiting for transfers between devices, shards(): mom = lax.all_to_all(mom, ('row', 'col'), 0, 0, tiled=True)  4.19 us
    ppermute x1, waiting for transfers between devices, shards(): near = lax.ppermute(a, 'col', swap_pairs('col', 0))  1.17 us
  transfers between devices with their start and end apart: 5, of which 2 were waited for; matrix products, arithmetic and copies ran while one was open for 0% of the time, Pallas kernels for 24%

profile of v11, /device:TPU:1, one launch (start us, length us, event | category | flops | bytes accessed | tf_op | source)
XLA Modules:
  0.0 41.2 jit_solution(7895666820032061684)
XLA Ops:
  0.6 0.0 copy-start.4
  0.6 0.0 copy-start.3
  0.7 0.0 copy-start
  0.7 0.0 copy-start.5
  0.7 0.0 copy-start.6
  0.7 1.7 %pack_rows.1 = (f32[32,512]{1,0:T(8,128)S(1)}, f32[32,512]{1,0:T(8,128)S(1)}) custom-call(f32[8,128,512]{2,1,0:T(8,128)} %g_in.1, f32[8,128,512]{2,1,0:T(8,128)} %c.3, s32[128,512]{1,0:T(8,128)} %land_in.1, s32[128,512]{1,0:T(8,128)} %bottom_in.1, f32[128,512]{1,0:T(8,128)} %surf.3, f32[128,512]{1,0:T(8,128)} %diag.5, f32[128,512]{1,0:T(8,128)} %v_in.1), custom_call_target="tpu_custom_call" | custom-call | tf_op jit(solution)/shard_map/pack_rows/pallas_call | solution.py:511
  2.4 0.8 %collective-permute-start.1 = (f32[32,512]{1,0:T(8,128)S(1)}, f32[32,512]{1,0:T(8,128)S(1)}, u32[]{:S(2)}, u32[]{:S(2)}) collective-permute-start(f32[32,512]{1,0:T(8,128)S(1)} %get-tuple-element.22.sent_b), channel_id=1, source_target_pairs={{16,32},{32,16},{48,64},{64,48},{80,96},{96,80},{17,33},{33,17},{4... | collective-permute-start | bytes 196616 | tf_op jit(solution)/shard_map/ppermute | solution.py:525
  3.3 4.7 %collective-permute-start = (f32[32,512]{1,0:T(8,128)S(1)}, f32[32,512]{1,0:T(8,128)S(1)}, u32[]{:S(2)}, u32[]{:S(2)}) collective-permute-start(f32[32,512]{1,0:T(8,128)S(1)} %get-tuple-element.21.sent_a), channel_id=1, source_target_pairs={{0,16},{16,0},{32,48},{48,32},{64,80},{80,64},{96,112},{112,96},{1... | collective-permute-start | bytes 196616 | tf_op jit(solution)/shard_map/ppermute | solution.py:534
  8.0 2.7 %local_rhs.1 = (f32[128,512]{1,0:T(8,128)S(1)}, f32[128,128]{1,0:T(8,128)S(1)}, f32[128,128]{1,0:T(8,128)S(1)}) custom-call(f32[8,128,512]{2,1,0:T(8,128)S(1)} %copy-done, f32[8,128,512]{2,1,0:T(8,128)S(1)} %copy-done.1, f32[128,512]{1,0:T(8,128)S(1)} %get-tuple-element.23.code_in, f32[128,512]{1,0:T(8,128)S(1)} %copy-done.5, f32[128,512]{1,0:T(8,128)S(1)} %copy-done.2, ...), custom_call_target="tpu_custom_call" | custom-call | flops 12582912 | bytes 4194304 | tf_op jit(solution)/shard_map/local_rhs/pallas_call | solution.py:511
  10.8 0.0 collective-permute-done.1.far.rf
  10.8 0.0 collective-permute-done.near.rn
  10.8 0.2 join_far.1.sent_b
  10.9 5.8 %collective-permute-start.3 = (f32[40,128]{1,0:T(8,128)S(1)}, f32[40,128]{1,0:T(8,128)S(1)}, u32[]{:S(2)}, u32[]{:S(2)}) collective-permute-start(f32[40,128]{1,0:T(8,128)S(1)} %join_far.1.sent_b), channel_id=1, source_target_pairs={{1,2},{2,1},{3,4},{4,3},{5,6},{6,5},{7,8},{8,7},{9,10},{10,9},{11,... | collective-permute-start | bytes 61448 | tf_op jit(solution)/shard_map/ppermute | solution.py:547
  16.7 1.6 %inner.1 = (f32[128,512]{1,0:T(8,128)}, f32[128,512]{1,0:T(8,128)S(1)}, f32[128,512]{1,0:T(8,128)S(1)}, f32[48,128]{1,0:T(8,128)S(1)}, f32[136,128]{1,0:T(8,128)...) custom-call(f32[128,512]{1,0:T(8,128)S(1)} %get-tuple-element.26.r_in.r, f32[128,512]{1,0:T(8,128)S(1)} %get-tuple-element.23.code_in, ...), custom_call_target="tpu_custom_call" | custom-call | flops 12582912 | bytes 4194304 | tf_op jit(solution)/shard_map/inner/pallas_call | solution.py:511
  18.3 0.2 join_near.1.sent_a
  18.5 0.1 collective-permute-start.2
  18.6 0.0 collective-permute-done.3.cf.far
  18.6 1.2 %collective-permute-done.2.cn.near = f32[40,128]{1,0:T(8,128)S(1)} collective-permute-done((f32[40,128]{1,0:T(8,128)S(1)}, f32[40,128]{1,0:T(8,128)S(1)}, u32[]{:S(2)}, u32[]{:S(2)}) %collective-permute-start.2) | collective-permute-done | bytes 20512 | tf_op jit(solution)/shard_map/ppermute | solution.py:559
  19.7 1.5 %outer.1 = (f32[136,128]{1,0:T(8,128)S(1)}, f32[136,128]{1,0:T(8,128)S(1)}, f32[136,128]{1,0:T(8,128)S(1)}, f32[128,32]{1,0:T(8,128)}) custom-call(f32[136,128]{1,0:T(8,128)S(1)} %get-tuple-element.27.refs_0_.rs, f32[136,128]{1,0:T(8,128)S(1)} %get-tuple-element.28.codes, f32[136,128]{1,0:T(8,128)S(1)} %get-tuple-element.29.diags, ...), custom_call_target="tpu_custom_call" | custom-call | tf_op jit(solution)/shard_map/outer/pallas_call | solution.py:511
  21.2 9.2 %all-to-all-start = ((f32[128,1,32]{2,1,0:T(1,128)}), f32[128,1,32]{2,1,0:T(1,128)S(1)}, u32[]{:S(2)}, u32[]{:S(2)}) async-start(f32[128,1,32]{2,1,0:T(1,128)} %bitcast.1), calls=%async_computation | async-start | bytes 131072 | tf_op jit(solution)/shard_map/all_to_all | solution.py:564
  30.4 0.0 copy-start.7
  30.4 5.4 %tracer.1 = f32[8,128,512]{2,1,0:T(8,128)} custom-call(f32[8,128,512]{2,1,0:T(8,128)} %g_in.1, s32[128,512]{1,0:T(8,128)} %land_in.1, s32[128,512]{1,0:T(8,128)} %bottom_in.1, f32[128,512]{1,0:T(8,128)} %u_in.1, f32[128,512]{1,0:T(8,128)} %v_in.1, f32[32,512]{1,0:T(8,128)S(1)} %collective-permute-done.near.rn, f32[32,512]{1,0:T(8,128)S(1)} %collective-permute-done.1.far.rf, ...), custom_call_target="tpu_custom_call" | custom-call | flops 10485760 | bytes 6291456 | tf_op jit(solution)/shard_map/tracer/pallas_call | solution.py:511
  35.8 4.2 %all-to-all-done = f32[128,1,32]{2,1,0:T(1,128)S(1)} async-done(((f32[128,1,32]{2,1,0:T(1,128)}), f32[128,1,32]{2,1,0:T(1,128)S(1)}, u32[]{:S(2)}, u32[]{:S(2)}) %all-to-all-start) | async-done | bytes 16416 | tf_op jit(solution)/shard_map/all_to_all | solution.py:564
  40.0 1.2 %combine.1 = f32[128,512]{1,0:T(8,128)} custom-call(f32[128,32]{1,0:T(8,128)S(1)} %bitcast.4, f32[128,512]{1,0:T(8,128)S(1)} %copy-done.7, f32[128,512]{1,0:T(8,128)S(1)} %get-tuple-element.33.p1, f32[128,512]{1,0:T(8,128)S(1)} %get-tuple-element.34.p2, f32[136,128]{1,0:T(8,128)S(1)} %get-tuple-element.35.rs, f32[136,128]{1,0:T(8,128)S(1)} %get-tuple-element.36.p1s, ...), custom_call_target="tpu_custom_call" | custom-call | tf_op jit(solution)/shard_map/combine/pallas_call | solution.py:511
  (11 shorter events, 0.1 us)
Async XLA Ops:
  0.6 2.6 %copy-start.4 = (s32[128,512]{1,0:T(8,128)S(1)}, s32[128,512]{1,0:T(8,128)}, u32[]{:S(2)}) copy-start(s32[128,512]{1,0:T(8,128)} %bottom_in.1) | copy-start | bytes 786436
  0.6 2.6 %copy-start.3 = (s32[128,512]{1,0:T(8,128)S(1)}, s32[128,512]{1,0:T(8,128)}, u32[]{:S(2)}) copy-start(s32[128,512]{1,0:T(8,128)} %land_in.1) | copy-start | bytes 786436
  0.7 7.4 %copy-start.2 = (f32[128,512]{1,0:T(8,128)S(1)}, f32[128,512]{1,0:T(8,128)}, u32[]{:S(2)}) copy-start(f32[128,512]{1,0:T(8,128)} %diag.5) | copy-start | bytes 786436
  0.7 7.4 %copy-start = (f32[8,128,512]{2,1,0:T(8,128)S(1)}, f32[8,128,512]{2,1,0:T(8,128)}, u32[]{:S(2)}) copy-start(f32[8,128,512]{2,1,0:T(8,128)} %g_in.1) | copy-start | bytes 6291460
  0.7 7.4 %copy-start.5 = (f32[128,512]{1,0:T(8,128)S(1)}, f32[128,512]{1,0:T(8,128)}, u32[]{:S(2)}) copy-start(f32[128,512]{1,0:T(8,128)} %surf.3) | copy-start | bytes 786436
  0.7 7.3 %copy-start.1 = (f32[8,128,512]{2,1,0:T(8,128)S(1)}, f32[8,128,512]{2,1,0:T(8,128)}, u32[]{:S(2)}) copy-start(f32[8,128,512]{2,1,0:T(8,128)} %c.3) | copy-start | bytes 6291460
  0.7 7.3 %copy-start.6 = (f32[128,512]{1,0:T(8,128)S(1)}, f32[128,512]{1,0:T(8,128)}, u32[]{:S(2)}) copy-start(f32[128,512]{1,0:T(8,128)} %u_in.1) | copy-start | bytes 786436
  2.4 8.3 %collective-permute-start.1 = (f32[32,512]{1,0:T(8,128)S(1)}, f32[32,512]{1,0:T(8,128)S(1)}, u32[]{:S(2)}, u32[]{:S(2)}) collective-permute-start(f32[32,512]{1,0:T(8,128)S(1)} %get-tuple-element.22.sent_b), channel_id=1, source_target_pairs={{16,32},{32,16},{48,64},{64,48},{80,96},{96,80},{17,33},{33,17},{4... | collective-permute-start | bytes 196616 | tf_op jit(solution)/shard_map/ppermute | solution.py:525
  3.3 7.5 %collective-permute-start = (f32[32,512]{1,0:T(8,128)S(1)}, f32[32,512]{1,0:T(8,128)S(1)}, u32[]{:S(2)}, u32[]{:S(2)}) collective-permute-start(f32[32,512]{1,0:T(8,128)S(1)} %get-tuple-element.21.sent_a), channel_id=1, source_target_pairs={{0,16},{16,0},{32,48},{48,32},{64,80},{80,64},{96,112},{112,96},{1... | collective-permute-start | bytes 196616 | tf_op jit(solution)/shard_map/ppermute | solution.py:534
  10.9 7.6 %collective-permute-start.3 = (f32[40,128]{1,0:T(8,128)S(1)}, f32[40,128]{1,0:T(8,128)S(1)}, u32[]{:S(2)}, u32[]{:S(2)}) collective-permute-start(f32[40,128]{1,0:T(8,128)S(1)} %join_far.1.sent_b), channel_id=1, source_target_pairs={{1,2},{2,1},{3,4},{4,3},{5,6},{6,5},{7,8},{8,7},{9,10},{10,9},{11,... | collective-permute-start | bytes 61448 | tf_op jit(solution)/shard_map/ppermute | solution.py:547
  18.5 1.3 %collective-permute-start.2 = (f32[40,128]{1,0:T(8,128)S(1)}, f32[40,128]{1,0:T(8,128)S(1)}, u32[]{:S(2)}, u32[]{:S(2)}) collective-permute-start(f32[40,128]{1,0:T(8,128)S(1)} %join_near.1.sent_a), channel_id=1, source_target_pairs={{0,1},{1,0},{2,3},{3,2},{4,5},{5,4},{6,7},{7,6},{8,9},{9,8},{10,11... | collective-permute-start | bytes 61448 | tf_op jit(solution)/shard_map/ppermute | solution.py:559
  21.2 18.8 %all-to-all-start = ((f32[128,1,32]{2,1,0:T(1,128)}), f32[128,1,32]{2,1,0:T(1,128)S(1)}, u32[]{:S(2)}, u32[]{:S(2)}) async-start(f32[128,1,32]{2,1,0:T(1,128)} %bitcast.1), calls=%async_computation | async-start | bytes 131072 | tf_op jit(solution)/shard_map/all_to_all | solution.py:564
  30.4 9.6 %copy-start.7 = (f32[128,512]{1,0:T(8,128)S(1)}, f32[128,512]{1,0:T(8,128)}, u32[]{:S(2)}) copy-start(f32[128,512]{1,0:T(8,128)} %get-tuple-element.32.r) | copy-start | bytes 786436
